TPU v7x, 256 devices: a whole 4x4x8 slice. The times are simulated.
256 devices in a mesh: dp: 16 (over x_lo, z), row: 4 (over y), col: 4 (over x_hi, core).
Axes of the slice: x: 4 (x_hi: 2, x_lo: 2; x = x_hi * 2 + x_lo), y: 4, z: 8, core: 2. Of those that a mesh axis runs over, the one named last changes fastest.
Arguments:
- tokens: bfloat16 [32768, 6144], P(('dp', 'row'), 'col'), parts along dimension 0, may hold values from -6 to 6
- w_up: bfloat16 [6144, 3072], P('row', 'col'), may hold values from -0.078125 to 0.078125
- cotangent: bfloat16 [32768, 3072], P(('dp', 'row'), 'col'), parts along dimension 0, may hold values from -6 to 6
Outputs:
- hidden: bfloat16 [32768, 3072], P(('dp', 'row'), 'col'), parts along dimension 0
- d_tokens: bfloat16 [32768, 6144], P(('dp', 'col'), 'row'), parts along dimension 0
There are 16 independent parts, one for each index of `dp`. A program takes and returns all parts, laid end to end along the dimension named above; an argument that names none is the same for every part. Nothing has to cross between parts.
All inputs are finite; a program needn't handle non-finite values.
Results may differ from a plain program's by a relative error of at most 0.0049.
Values may be sent and summed in bfloat16 or wider, within the bound.
No kernel may reach another device: no remote copies, remote signals or barrier semaphores. Data moves between devices by JAX's collectives and lax.ppermute only.
A program may use at most 128 MiB of HBM per device.

v0:
```python
import math

import jax
import jax.numpy as jnp
from jax import lax
from jax.sharding import PartitionSpec as P

coeff = math.sqrt(2.0 / math.pi)


def from_behind(block, axis, distance):
    devices = range(lax.axis_size(axis))
    route = [((i - distance) % len(devices), i) for i in devices]
    return lax.ppermute(block, axis, route)


def swapped(block, axis, apart):
    count = lax.axis_size(axis)
    route = []
    for low in range(count):
        high = low | 1 << apart
        if high != low and high < count:
            route += [(low, high), (high, low)]
    return lax.ppermute(block, axis, route)


def x_step(block, by):
    return from_behind(block, "col", by)


def w_step(block, by):
    return from_behind(block, "row", by)


def wt_step(block, by):
    return from_behind(block, "col", by)


def grad_step(block, by):
    return from_behind(block, "row", by)


def skewed(block, index, roller, levels):
    for level in range(levels):
        moved = roller(block, -(1 << level))
        block = jnp.where(index >> level & 1 == 1, moved, block)
    return block


def mirror(block, row_index, col_index, levels):
    for level in range(levels):
        moved = swapped(swapped(block, "row", level), "col", level)
        differ = row_index >> level & 1 != col_index >> level & 1
        block = jnp.where(differ, moved, block)
    return block


def body(tokens, w_up, cotangent):
    count = lax.axis_size("row")
    levels = count.bit_length() - 1
    row_index = lax.axis_index("row")
    col_index = lax.axis_index("col")
    x_cur = skewed(tokens, row_index, x_step, levels)
    w_cur = skewed(w_up, col_index, w_step, levels)
    pre = jnp.zeros((tokens.shape[0], w_up.shape[1]), jnp.float32)
    for turn in range(count):
        pre = pre + jnp.dot(x_cur, w_cur, preferred_element_type=jnp.float32)
        if turn + 1 < count:
            x_cur = x_step(x_cur, -1)
            w_cur = w_step(w_cur, -1)
    inner = coeff * (pre + 0.044715 * pre * pre * pre)
    tanh_val = jnp.tanh(inner)
    hidden = (0.5 * pre * (1.0 + tanh_val)).astype(jnp.bfloat16)
    slope = 0.5 * (1.0 + tanh_val) + 0.5 * pre * (1.0 - tanh_val * tanh_val) * coeff * (
        1.0 + 3.0 * 0.044715 * pre * pre
    )
    d_pre = (cotangent.astype(jnp.float32) * slope).astype(jnp.bfloat16)
    mirrored = mirror(d_pre, row_index, col_index, levels)
    w_cur = skewed(w_up, row_index, wt_step, levels)
    g_cur = skewed(mirrored, col_index, grad_step, levels)
    total = jnp.zeros((d_pre.shape[0], w_up.shape[0]), jnp.float32)
    for turn in range(count):
        total = total + lax.dot_general(
            g_cur, w_cur, (((1,), (1,)), ((), ())), preferred_element_type=jnp.float32
        )
        if turn + 1 < count:
            w_cur = wt_step(w_cur, -1)
            g_cur = grad_step(g_cur, -1)
    return (hidden, total.astype(jnp.bfloat16))


def solution(mesh):
    placed = (P(("dp", "row"), "col"), P("row", "col"), P(("dp", "row"), "col"))
    return jax.shard_map(
        body,
        mesh=mesh,
        in_specs=placed,
        out_specs=(P(("dp", "row"), "col"), P(("dp", "col"), "row")),
        check_vma=False,
    )
```

profile of v0, /device:TPU:4, one launch (start us, length us, event | category | flops | bytes accessed | tf_op | source)
XLA Modules:
  0.0 433.1 jit_solution(8585243309425442873)
XLA Ops:
  0.7 3.1 collective-permute-start.2
  3.8 23.6 %collective-permute-done.16 = bf16[1536,768]{1,0:T(8,128)(2,1)S(1)} collective-permute-done((bf16[1536,768]{1,0:T(8,128)(2,1)}, bf16[1536,768]{1,0:T(8,128)(2,1)S(1)}, u32[]{:S(2)}, u32[]{:S(2)}) %collective-permute-start.16) | collective-permute-done | bytes 2359328 | tf_op jit(solution)/shard_map/ppermute | solution.py:14
  27.4 1.4 copy-done
  28.8 26.4 %collective-permute-done.2 = bf16[1536,768]{1,0:T(8,128)(2,1)} collective-permute-done((bf16[1536,768]{1,0:T(8,128)(2,1)}, bf16[1536,768]{1,0:T(8,128)(2,1)}, u32[]{:S(2)}, u32[]{:S(2)}) %collective-permute-start.2) | collective-permute-done | bytes 2359328 | tf_op jit(solution)/shard_map/ppermute | solution.py:14
  55.2 3.5 broadcast_select_fusion
  58.7 2.7 collective-permute-start.3
  61.4 52.7 %collective-permute-done.3 = bf16[1536,768]{1,0:T(8,128)(2,1)} collective-permute-done((bf16[1536,768]{1,0:T(8,128)(2,1)}, bf16[1536,768]{1,0:T(8,128)(2,1)}, u32[]{:S(2)}, u32[]{:S(2)}) %collective-permute-start.3) | collective-permute-done | bytes 2359328 | tf_op jit(solution)/shard_map/ppermute | solution.py:14
  114.0 3.4 broadcast_select_fusion.3
  117.4 4.4 %collective-permute-start.5 = (bf16[1536,768]{1,0:T(8,128)(2,1)}, bf16[1536,768]{1,0:T(8,128)(2,1)}, u32[]{:S(2)}, u32[]{:S(2)}) collective-permute-start(bf16[1536,768]{1,0:T(8,128)(2,1)} %broadcast_select_fusion.3), channel_id=1, source_target_pairs={{4,0},{8,4},{12,8},{0,12},{5,1},{9,5},{13,9},{1,13},{6,2},{10,6},{... | collective-permute-start | bytes 7077896 | tf_op jit(solution)/shard_map/ppermute | solution.py:14
  121.8 2.7 broadcast_select_fusion.4
  124.5 37.4 %collective-permute-done.1 = bf16[512,1536]{1,0:T(8,128)(2,1)} collective-permute-done((bf16[512,1536]{1,0:T(8,128)(2,1)}, bf16[512,1536]{1,0:T(8,128)(2,1)}, u32[]{:S(2)}, u32[]{:S(2)}) %collective-permute-start.1) | collective-permute-done | bytes 1572896 | tf_op jit(solution)/shard_map/ppermute | solution.py:14
  161.9 1.6 broadcast_select_fusion.5
  163.6 8.8 %collective-permute-done.5 = bf16[1536,768]{1,0:T(8,128)(2,1)} collective-permute-done((bf16[1536,768]{1,0:T(8,128)(2,1)}, bf16[1536,768]{1,0:T(8,128)(2,1)}, u32[]{:S(2)}, u32[]{:S(2)}) %collective-permute-start.5) | collective-permute-done | bytes 2359328 | tf_op jit(solution)/shard_map/ppermute | solution.py:14
  172.3 3.7 collective-permute-start.7
  176.0 5.5 %collective-permute-done.4 = bf16[512,1536]{1,0:T(8,128)(2,1)S(1)} collective-permute-done((bf16[512,1536]{1,0:T(8,128)(2,1)S(1)}, bf16[512,1536]{1,0:T(8,128)(2,1)S(1)}, u32[]{:S(2)}, u32[]{:S(2)}) %collective-permute-start.4) | collective-permute-done | bytes 1572896 | tf_op jit(solution)/shard_map/ppermute | solution.py:14
  181.5 3.4 collective-permute-start.6
  184.9 40.7 %collective-permute-done.7 = bf16[1536,768]{1,0:T(8,128)(2,1)S(1)} collective-permute-done((bf16[1536,768]{1,0:T(8,128)(2,1)}, bf16[1536,768]{1,0:T(8,128)(2,1)S(1)}, u32[]{:S(2)}, u32[]{:S(2)}) %collective-permute-start.7) | collective-permute-done | bytes 2359328 | tf_op jit(solution)/shard_map/ppermute | solution.py:14
  225.7 3.6 collective-permute-start.9
  229.2 0.6 collective-permute-start.17
  229.8 3.0 fusion.8
  232.9 3.0 fusion.9
  235.9 1.4 fusion.10
  237.3 26.7 %collective-permute-done.8 = bf16[512,1536]{1,0:T(8,128)(2,1)S(1)} collective-permute-done((bf16[512,1536]{1,0:T(8,128)(2,1)S(1)}, bf16[512,1536]{1,0:T(8,128)(2,1)S(1)}, u32[]{:S(2)}, u32[]{:S(2)}) %collective-permute-start.8) | collective-permute-done | bytes 1572896 | tf_op jit(solution)/shard_map/ppermute | solution.py:14
  264.0 13.6 %collective-permute-done.9 = bf16[1536,768]{1,0:T(8,128)(2,1)S(1)} collective-permute-done((bf16[1536,768]{1,0:T(8,128)(2,1)S(1)}, bf16[1536,768]{1,0:T(8,128)(2,1)S(1)}, u32[]{:S(2)}, u32[]{:S(2)}) %collective-permute-start.9) | collective-permute-done | bytes 2359328 | tf_op jit(solution)/shard_map/ppermute | solution.py:14
  277.6 3.2 fusion.7
  280.9 16.3 %collective-permute-done.10 = bf16[512,768]{1,0:T(8,128)(2,1)} collective-permute-done((bf16[512,768]{1,0:T(8,128)(2,1)S(1)}, bf16[512,768]{1,0:T(8,128)(2,1)}, u32[]{:S(2)}, u32[]{:S(2)}) %collective-permute-start.10) | collective-permute-done | bytes 786464 | tf_op jit(solution)/shard_map/ppermute | solution.py:24
  297.2 1.5 collective-permute-done.17
  298.8 1.7 broadcast_select_fusion.1
  300.5 2.9 collective-permute-start.12
  303.4 18.5 %collective-permute-done.12 = bf16[512,768]{1,0:T(8,128)(2,1)S(1)} collective-permute-done((bf16[512,768]{1,0:T(8,128)(2,1)S(1)}, bf16[512,768]{1,0:T(8,128)(2,1)S(1)}, u32[]{:S(2)}, u32[]{:S(2)}) %collective-permute-start.12) | collective-permute-done | bytes 786464 | tf_op jit(solution)/shard_map/ppermute | solution.py:24
  321.9 2.8 collective-permute-start.13
  324.7 4.1 collective-permute-done.19
  328.8 3.4 collective-permute-start.21
  332.2 14.9 %collective-permute-done.13 = bf16[512,768]{1,0:T(8,128)(2,1)S(1)} collective-permute-done((bf16[512,768]{1,0:T(8,128)(2,1)S(1)}, bf16[512,768]{1,0:T(8,128)(2,1)S(1)}, u32[]{:S(2)}, u32[]{:S(2)}) %collective-permute-start.13) | collective-permute-done | bytes 786464 | tf_op jit(solution)/shard_map/ppermute | solution.py:24
  347.2 3.1 collective-permute-start.14
  350.3 14.7 %collective-permute-done.14 = bf16[512,768]{1,0:T(8,128)(2,1)S(1)} collective-permute-done((bf16[512,768]{1,0:T(8,128)(2,1)S(1)}, bf16[512,768]{1,0:T(8,128)(2,1)S(1)}, u32[]{:S(2)}, u32[]{:S(2)}) %collective-permute-start.14) | collective-permute-done | bytes 786464 | tf_op jit(solution)/shard_map/ppermute | solution.py:14
  365.1 2.0 collective-permute-start.15
  367.1 12.6 %collective-permute-done.15 = bf16[512,768]{1,0:T(8,128)(2,1)S(1)} collective-permute-done((bf16[512,768]{1,0:T(8,128)(2,1)S(1)}, bf16[512,768]{1,0:T(8,128)(2,1)S(1)}, u32[]{:S(2)}, u32[]{:S(2)}) %collective-permute-start.15) | collective-permute-done | bytes 786464 | tf_op jit(solution)/shard_map/ppermute | solution.py:14
  379.8 4.2 collective-permute-start.18
  384.0 15.1 %collective-permute-done.18 = bf16[512,768]{1,0:T(8,128)(2,1)S(1)} collective-permute-done((bf16[512,768]{1,0:T(8,128)(2,1)S(1)}, bf16[512,768]{1,0:T(8,128)(2,1)S(1)}, u32[]{:S(2)}, u32[]{:S(2)}) %collective-permute-start.18) | collective-permute-done | bytes 786464 | tf_op jit(solution)/shard_map/ppermute | solution.py:14
  399.1 2.5 collective-permute-start.20
  401.6 3.1 fusion.11
  404.7 12.1 %collective-permute-done.20 = bf16[512,768]{1,0:T(8,128)(2,1)S(1)} collective-permute-done((bf16[512,768]{1,0:T(8,128)(2,1)S(1)}, bf16[512,768]{1,0:T(8,128)(2,1)S(1)}, u32[]{:S(2)}, u32[]{:S(2)}) %collective-permute-start.20) | collective-permute-done | bytes 786464 | tf_op jit(solution)/shard_map/ppermute | solution.py:14
  416.8 2.5 collective-permute-start.22
  419.3 3.1 convolution_add_fusion.2
  422.4 1.4 convolution_add_fusion.1
  423.8 6.7 %collective-permute-done.22 = bf16[512,768]{1,0:T(8,128)(2,1)S(1)} collective-permute-done((bf16[512,768]{1,0:T(8,128)(2,1)S(1)}, bf16[512,768]{1,0:T(8,128)(2,1)S(1)}, u32[]{:S(2)}, u32[]{:S(2)}) %collective-permute-start.22) | collective-permute-done | bytes 786464 | tf_op jit(solution)/shard_map/ppermute | solution.py:14
  430.5 2.6 fusion
  (21 shorter events, 0.5 us)
Async XLA Ops:
  0.6 26.8 %collective-permute-start.16 = (bf16[1536,768]{1,0:T(8,128)(2,1)}, bf16[1536,768]{1,0:T(8,128)(2,1)S(1)}, u32[]{:S(2)}, u32[]{:S(2)}) collective-permute-start(bf16[1536,768]{1,0:T(8,128)(2,1)} %param.4), channel_id=1, source_target_pairs={{1,0},{2,1},{3,2},{0,3},{5,4},{6,5},{7,6},{4,7},{9,8},{10,9},{11,1... | collective-permute-start | bytes 7077896 | tf_op jit(solution)/shard_map/ppermute | solution.py:14
  0.7 54.5 %collective-permute-start.2 = (bf16[1536,768]{1,0:T(8,128)(2,1)}, bf16[1536,768]{1,0:T(8,128)(2,1)}, u32[]{:S(2)}, u32[]{:S(2)}) collective-permute-start(bf16[1536,768]{1,0:T(8,128)(2,1)} %param.4), channel_id=1, source_target_pairs={{4,0},{8,4},{12,8},{0,12},{5,1},{9,5},{13,9},{1,13},{6,2},{10,6},{... | collective-permute-start | bytes 7077896 | tf_op jit(solution)/shard_map/ppermute | solution.py:14
  27.4 1.4 copy-start
  58.7 55.3 %collective-permute-start.3 = (bf16[1536,768]{1,0:T(8,128)(2,1)}, bf16[1536,768]{1,0:T(8,128)(2,1)}, u32[]{:S(2)}, u32[]{:S(2)}) collective-permute-start(bf16[1536,768]{1,0:T(8,128)(2,1)} %get-tuple-element.3), channel_id=1, source_target_pairs={{8,0},{12,4},{0,8},{4,12},{9,1},{13,5},{1,9},{5,13},{10,2},{14,6},... | collective-permute-start | bytes 7077896 | tf_op jit(solution)/shard_map/ppermute | solution.py:14
  61.4 60.4 %collective-permute-start = (bf16[512,1536]{1,0:T(8,128)(2,1)}, bf16[512,1536]{1,0:T(8,128)(2,1)}, u32[]{:S(2)}, u32[]{:S(2)}) collective-permute-start(bf16[512,1536]{1,0:T(8,128)(2,1)} %param.3), channel_id=1, source_target_pairs={{1,0},{2,1},{3,2},{0,3},{5,4},{6,5},{7,6},{4,7},{9,8},{10,9},{11,1... | collective-permute-start | bytes 4718600 | tf_op jit(solution)/shard_map/ppermute | solution.py:14
  117.4 54.9 %collective-permute-start.5 = (bf16[1536,768]{1,0:T(8,128)(2,1)}, bf16[1536,768]{1,0:T(8,128)(2,1)}, u32[]{:S(2)}, u32[]{:S(2)}) collective-permute-start(bf16[1536,768]{1,0:T(8,128)(2,1)} %broadcast_select_fusion.3), channel_id=1, source_target_pairs={{4,0},{8,4},{12,8},{0,12},{5,1},{9,5},{13,9},{1,13},{6,2},{10,6},{... | collective-permute-start | bytes 7077896 | tf_op jit(solution)/shard_map/ppermute | solution.py:14
  124.5 37.4 %collective-permute-start.1 = (bf16[512,1536]{1,0:T(8,128)(2,1)}, bf16[512,1536]{1,0:T(8,128)(2,1)}, u32[]{:S(2)}, u32[]{:S(2)}) collective-permute-start(bf16[512,1536]{1,0:T(8,128)(2,1)} %broadcast_select_fusion.4), channel_id=1, source_target_pairs={{2,0},{3,1},{0,2},{1,3},{6,4},{7,5},{4,6},{5,7},{10,8},{11,9},{8,1... | collective-permute-start | bytes 4718600 | tf_op jit(solution)/shard_map/ppermute | solution.py:14
  163.5 18.0 %collective-permute-start.4 = (bf16[512,1536]{1,0:T(8,128)(2,1)S(1)}, bf16[512,1536]{1,0:T(8,128)(2,1)S(1)}, u32[]{:S(2)}, u32[]{:S(2)}) collective-permute-start(bf16[512,1536]{1,0:T(8,128)(2,1)S(1)} %broadcast_select_fusion.5), channel_id=1, source_target_pairs={{1,0},{2,1},{3,2},{0,3},{5,4},{6,5},{7,6},{4,7},{9,8},{10,9},{11,1... | collective-permute-start | bytes 4718600 | tf_op jit(solution)/shard_map/ppermute | solution.py:14
  172.3 53.3 %collective-permute-start.7 = (bf16[1536,768]{1,0:T(8,128)(2,1)}, bf16[1536,768]{1,0:T(8,128)(2,1)S(1)}, u32[]{:S(2)}, u32[]{:S(2)}) collective-permute-start(bf16[1536,768]{1,0:T(8,128)(2,1)} %collective-permute-done.5), channel_id=1, source_target_pairs={{4,0},{8,4},{12,8},{0,12},{5,1},{9,5},{13,9},{1,13},{6,2},{10,6},{... | collective-permute-start | bytes 7077896 | tf_op jit(solution)/shard_map/ppermute | solution.py:14
  181.5 47.7 %collective-permute-start.6 = (bf16[512,1536]{1,0:T(8,128)(2,1)S(1)}, bf16[512,1536]{1,0:T(8,128)(2,1)S(1)}, u32[]{:S(2)}, u32[]{:S(2)}) collective-permute-start(bf16[512,1536]{1,0:T(8,128)(2,1)S(1)} %collective-permute-done.4), channel_id=1, source_target_pairs={{1,0},{2,1},{3,2},{0,3},{5,4},{6,5},{7,6},{4,7},{9,8},{10,9},{11,1... | collective-permute-start | bytes 4718600 | tf_op jit(solution)/shard_map/ppermute | solution.py:14
  225.7 52.0 %collective-permute-start.9 = (bf16[1536,768]{1,0:T(8,128)(2,1)S(1)}, bf16[1536,768]{1,0:T(8,128)(2,1)S(1)}, u32[]{:S(2)}, u32[]{:S(2)}) collective-permute-start(bf16[1536,768]{1,0:T(8,128)(2,1)S(1)} %collective-permute-done.7), channel_id=1, source_target_pairs={{4,0},{8,4},{12,8},{0,12},{5,1},{9,5},{13,9},{1,13},{6,2},{10,6},{... | collective-permute-start | bytes 7077896 | tf_op jit(solution)/shard_map/ppermute | solution.py:14
  229.2 34.8 %collective-permute-start.8 = (bf16[512,1536]{1,0:T(8,128)(2,1)S(1)}, bf16[512,1536]{1,0:T(8,128)(2,1)S(1)}, u32[]{:S(2)}, u32[]{:S(2)}) collective-permute-start(bf16[512,1536]{1,0:T(8,128)(2,1)S(1)} %collective-permute-done.6), channel_id=1, source_target_pairs={{1,0},{2,1},{3,2},{0,3},{5,4},{6,5},{7,6},{4,7},{9,8},{10,9},{11,1... | collective-permute-start | bytes 4718600 | tf_op jit(solution)/shard_map/ppermute | solution.py:14
  229.2 69.5 %collective-permute-start.17 = (bf16[1536,768]{1,0:T(8,128)(2,1)S(1)}, bf16[1536,768]{1,0:T(8,128)(2,1)S(1)}, u32[]{:S(2)}, u32[]{:S(2)}) collective-permute-start(bf16[1536,768]{1,0:T(8,128)(2,1)S(1)} %get-tuple-element.2), channel_id=1, source_target_pairs={{2,0},{3,1},{0,2},{1,3},{6,4},{7,5},{4,6},{5,7},{10,8},{11,9},{8,1... | collective-permute-start | bytes 7077896 | tf_op jit(solution)/shard_map/ppermute | solution.py:14
  235.9 41.7 %copy-start.1 = (bf16[512,768]{1,0:T(8,128)(2,1)S(1)}, bf16[512,768]{1,0:T(8,128)(2,1)}, u32[]{:S(2)}) copy-start(bf16[512,768]{1,0:T(8,128)(2,1)} %param.5) | copy-start | bytes 2359300
  280.9 16.3 %collective-permute-start.10 = (bf16[512,768]{1,0:T(8,128)(2,1)S(1)}, bf16[512,768]{1,0:T(8,128)(2,1)}, u32[]{:S(2)}, u32[]{:S(2)}) collective-permute-start(bf16[512,768]{1,0:T(8,128)(2,1)S(1)} %get-tuple-element.4), channel_id=1, source_target_pairs={{0,4},{4,0},{8,12},{12,8},{1,5},{5,1},{9,13},{13,9},{2,6},{6,2},{1... | collective-permute-start | bytes 2359304 | tf_op jit(solution)/shard_map/ppermute | solution.py:24
  297.2 3.2 collective-permute-start.11
  300.4 28.4 %collective-permute-start.19 = (bf16[1536,768]{1,0:T(8,128)(2,1)}, bf16[1536,768]{1,0:T(8,128)(2,1)}, u32[]{:S(2)}, u32[]{:S(2)}) collective-permute-start(bf16[1536,768]{1,0:T(8,128)(2,1)} %broadcast_select_fusion.1), channel_id=1, source_target_pairs={{1,0},{2,1},{3,2},{0,3},{5,4},{6,5},{7,6},{4,7},{9,8},{10,9},{11,1... | collective-permute-start | bytes 7077896 | tf_op jit(solution)/shard_map/ppermute | solution.py:14
  300.5 21.4 %collective-permute-start.12 = (bf16[512,768]{1,0:T(8,128)(2,1)S(1)}, bf16[512,768]{1,0:T(8,128)(2,1)S(1)}, u32[]{:S(2)}, u32[]{:S(2)}) collective-permute-start(bf16[512,768]{1,0:T(8,128)(2,1)S(1)} %broadcast_select_fusion.6), channel_id=1, source_target_pairs={{0,8},{8,0},{4,12},{12,4},{1,9},{9,1},{5,13},{13,5},{2,10},{10,2},... | collective-permute-start | bytes 2359304 | tf_op jit(solution)/shard_map/ppermute | solution.py:24
  321.9 25.2 %collective-permute-start.13 = (bf16[512,768]{1,0:T(8,128)(2,1)S(1)}, bf16[512,768]{1,0:T(8,128)(2,1)S(1)}, u32[]{:S(2)}, u32[]{:S(2)}) collective-permute-start(bf16[512,768]{1,0:T(8,128)(2,1)S(1)} %collective-permute-done.12), channel_id=1, source_target_pairs={{0,2},{2,0},{1,3},{3,1},{4,6},{6,4},{5,7},{7,5},{8,10},{10,8},{9,1... | collective-permute-start | bytes 2359304 | tf_op jit(solution)/shard_map/ppermute | solution.py:24
  328.8 55.2 %collective-permute-start.21 = (bf16[1536,768]{1,0:T(8,128)(2,1)}, bf16[1536,768]{1,0:T(8,128)(2,1)S(1)}, u32[]{:S(2)}, u32[]{:S(2)}) collective-permute-start(bf16[1536,768]{1,0:T(8,128)(2,1)} %collective-permute-done.19), channel_id=1, source_target_pairs={{1,0},{2,1},{3,2},{0,3},{5,4},{6,5},{7,6},{4,7},{9,8},{10,9},{11,1... | collective-permute-start | bytes 7077896 | tf_op jit(solution)/shard_map/ppermute | solution.py:14
  347.2 17.8 %collective-permute-start.14 = (bf16[512,768]{1,0:T(8,128)(2,1)S(1)}, bf16[512,768]{1,0:T(8,128)(2,1)S(1)}, u32[]{:S(2)}, u32[]{:S(2)}) collective-permute-start(bf16[512,768]{1,0:T(8,128)(2,1)S(1)} %broadcast_select_fusion.7), channel_id=1, source_target_pairs={{4,0},{8,4},{12,8},{0,12},{5,1},{9,5},{13,9},{1,13},{6,2},{10,6},{... | collective-permute-start | bytes 2359304 | tf_op jit(solution)/shard_map/ppermute | solution.py:14
  365.1 14.6 %collective-permute-start.15 = (bf16[512,768]{1,0:T(8,128)(2,1)S(1)}, bf16[512,768]{1,0:T(8,128)(2,1)S(1)}, u32[]{:S(2)}, u32[]{:S(2)}) collective-permute-start(bf16[512,768]{1,0:T(8,128)(2,1)S(1)} %broadcast_select_fusion.8), channel_id=1, source_target_pairs={{8,0},{12,4},{0,8},{4,12},{9,1},{13,5},{1,9},{5,13},{10,2},{14,6},... | collective-permute-start | bytes 2359304 | tf_op jit(solution)/shard_map/ppermute | solution.py:14
  379.8 19.3 %collective-permute-start.18 = (bf16[512,768]{1,0:T(8,128)(2,1)S(1)}, bf16[512,768]{1,0:T(8,128)(2,1)S(1)}, u32[]{:S(2)}, u32[]{:S(2)}) collective-permute-start(bf16[512,768]{1,0:T(8,128)(2,1)S(1)} %broadcast_select_fusion.9), channel_id=1, source_target_pairs={{4,0},{8,4},{12,8},{0,12},{5,1},{9,5},{13,9},{1,13},{6,2},{10,6},{... | collective-permute-start | bytes 2359304 | tf_op jit(solution)/shard_map/ppermute | solution.py:14
  384.0 39.8 %collective-permute-start.23 = (bf16[1536,768]{1,0:T(8,128)(2,1)S(1)}, bf16[1536,768]{1,0:T(8,128)(2,1)S(1)}, u32[]{:S(2)}, u32[]{:S(2)}) collective-permute-start(bf16[1536,768]{1,0:T(8,128)(2,1)S(1)} %collective-permute-done.21), channel_id=1, source_target_pairs={{1,0},{2,1},{3,2},{0,3},{5,4},{6,5},{7,6},{4,7},{9,8},{10,9},{11,1... | collective-permute-start | bytes 7077896 | tf_op jit(solution)/shard_map/ppermute | solution.py:14
  399.1 17.7 %collective-permute-start.20 = (bf16[512,768]{1,0:T(8,128)(2,1)S(1)}, bf16[512,768]{1,0:T(8,128)(2,1)S(1)}, u32[]{:S(2)}, u32[]{:S(2)}) collective-permute-start(bf16[512,768]{1,0:T(8,128)(2,1)S(1)} %collective-permute-done.18), channel_id=1, source_target_pairs={{4,0},{8,4},{12,8},{0,12},{5,1},{9,5},{13,9},{1,13},{6,2},{10,6},{... | collective-permute-start | bytes 2359304 | tf_op jit(solution)/shard_map/ppermute | solution.py:14
  416.8 13.8 %collective-permute-start.22 = (bf16[512,768]{1,0:T(8,128)(2,1)S(1)}, bf16[512,768]{1,0:T(8,128)(2,1)S(1)}, u32[]{:S(2)}, u32[]{:S(2)}) collective-permute-start(bf16[512,768]{1,0:T(8,128)(2,1)S(1)} %collective-permute-done.20), channel_id=1, source_target_pairs={{4,0},{8,4},{12,8},{0,12},{5,1},{9,5},{13,9},{1,13},{6,2},{10,6},{... | collective-permute-start | bytes 2359304 | tf_op jit(solution)/shard_map/ppermute | solution.py:14
where the time goes:
time: 436 us; the launch traced here: 433 us
  waiting for transfers between devices  352 us (81%)
  starting transfers between devices  45 us (10%)
  matrix products  20.9 us (5%)
  other arithmetic  13.1 us (3%)
    ppermute x20, waiting for transfers between devices, from_behind(): return lax.ppermute(block, axis, route)  302 us
    ppermute x4, waiting for transfers between devices, swapped(): return lax.ppermute(block, axis, route)  49.7 us
    ppermute x20, starting transfers between devices, from_behind(): return lax.ppermute(block, axis, route)  39.3 us
    select_n x7, other arithmetic, skewed(): block = jnp.where(index >> level & 1 == 1, moved, block)  13 us
    dot_general x4, matrix products, body(): pre = pre + jnp.dot(x_cur, w_cur, preferred_element_type=jnp.float32)  10.7 us
    dot_general x4, matrix products, body(): lax.dot_general(g_cur, w_cur, (((1,), (1,)), ((), ())), preferred_element...  10.2 us
  transfers between devices with their start and end apart: 24, of which 19 were waited for; matrix products, arithmetic and copies ran while one was open for 6% of the time, Pallas kernels for 0%

commit v1 on v0

v1 whole, which is shorter than its diff:
```python
import functools
import math

import jax
import jax.numpy as jnp
from jax import lax
from jax.experimental import pallas as pl
from jax.experimental.pallas import tpu as pltpu
from jax.sharding import PartitionSpec as P

COEFF = math.sqrt(2.0 / math.pi)
MIB = 1 << 20


def route(sizes, target):
    pairs = []
    for i in range(sizes[0]):
        for j in range(sizes[1]):
            a, b = target(i, j)
            pairs.append((i * sizes[1] + j, a * sizes[1] + b))
    return pairs


def to_row(x, d):
    n = lax.axis_size("row")
    return lax.ppermute(x, "row", [(i, (i + d) % n) for i in range(n)])


def col_swap(x, m):
    n = lax.axis_size("col")
    return lax.ppermute(x, "col", [(i, i ^ m) for i in range(n)])


def turned(r, c):
    core = c & 1
    if (c >> 1) != (r >> 1):
        step = 2 if core else 0
    else:
        step = 1 if core else -1
    return (r + step) % 4, r


def mirror(x):
    return lax.ppermute(x, ("row", "col"), route((4, 4), turned))


def turned_from(row, col):
    step = (row - col + 4) & 3
    cross = 1 - (step & 1)
    core = jnp.where((step == 1) | (step == 2), 1, 0)
    return 2 * ((col >> 1) ^ cross) + core


def ring(x):
    h = x.shape[0] // 2
    prev, nxt = to_row(x, 1), to_row(x, -1)
    return prev, nxt, to_row(prev[:h], 1), to_row(nxt[h:], -1)


def z_gather(x):
    dp = lax.axis_size("dp")
    z = min(8, dp)
    groups = [list(range(i, i + z)) for i in range(0, dp, z)]
    return lax.all_gather(x, "dp", axis_index_groups=groups)


def gelu_parts(pre):
    sq = pre * pre
    t = jnp.tanh(COEFF * (pre + 0.044715 * sq * pre))
    hidden = 0.5 * pre * (1.0 + t)
    slope = 0.5 * (1.0 + t) + 0.5 * pre * (1.0 - t * t) * COEFF * (1.0 + 3.0 * 0.044715 * sq)
    return hidden, slope


def up_kernel(at, nw, t0, t1, t2, t3, *rest):
    w_refs = rest[:nw]
    cot, hidden, d_pre, t_buf, w_buf, c_buf, acc, t_sem, w_sem, c_sem = rest[nw:]
    r, c = lax.axis_index("row"), lax.axis_index("col")
    for m, src in enumerate((t0, t1, t2, t3)):
        slot = c ^ m
        pltpu.make_async_copy(src, t_buf.at[slot], t_sem.at[slot]).start()
    if nw == 5:
        own, prev, nxt, far_a, far_b = w_refs
        h = far_a.shape[0]
        width = w_buf.shape[2]
        a, b, d, e = r, (r + 3) & 3, (r + 1) & 3, (r + 2) & 3
        pltpu.make_async_copy(own.at[:, pl.ds(at, width)], w_buf.at[a], w_sem.at[a]).start()
        pltpu.make_async_copy(prev, w_buf.at[b], w_sem.at[b]).start()
        pltpu.make_async_copy(nxt, w_buf.at[d], w_sem.at[d]).start()
        pltpu.make_async_copy(far_a, w_buf.at[e, pl.ds(0, h)], w_sem.at[e]).start()
        pltpu.make_async_copy(far_b, w_buf.at[e, pl.ds(h, h)], w_sem.at[e]).start()
    else:
        own, gathered = w_refs
        width = w_buf.shape[2]
        zs, _, part, _ = gathered.shape
        pltpu.make_async_copy(own.at[:, pl.ds(at, width)], w_buf.at[r], w_sem.at[r]).start()
        for i, d in enumerate((3, 1, 2)):
            slot = (r + d) & 3
            for z in range(zs):
                pltpu.make_async_copy(
                    gathered.at[z, i], w_buf.at[slot, pl.ds(z * part, part)], w_sem.at[slot]
                ).start()
    c_copy = pltpu.make_async_copy(cot.at[:, pl.ds(at, c_buf.shape[1])], c_buf, c_sem)
    c_copy.start()
    rows = t_buf.shape[1]
    tile = min(256, rows)
    for j in range(4):
        pltpu.make_async_copy(t0, t_buf.at[j], t_sem.at[j]).wait()
        pltpu.make_async_copy(own.at[:, pl.ds(at, w_buf.shape[2])], w_buf.at[j], w_sem.at[j]).wait()
        if j == 3:
            c_copy.wait()

        @pl.loop(0, rows // tile)
        def _(i):
            part_rows = pl.ds(pl.multiple_of(i * tile, tile), tile)
            y = jnp.dot(t_buf[j, part_rows, :], w_buf[j], preferred_element_type=jnp.float32)
            if j > 0:
                y = y + acc[part_rows, :]
            if j < 3:
                acc[part_rows, :] = y
            else:
                h_val, slope = gelu_parts(y)
                hidden[part_rows, :] = h_val.astype(hidden.dtype)
                d_pre[part_rows, :] = (c_buf[part_rows, :].astype(jnp.float32) * slope).astype(d_pre.dtype)


def up(tokens, w_pieces, cot, at, width):
    rows, depth = tokens[0].shape
    any_ = pl.BlockSpec(memory_space=pl.ANY)
    out = jax.ShapeDtypeStruct((rows, width), jnp.bfloat16)
    whole = pl.BlockSpec(memory_space=pltpu.VMEM)
    return pl.pallas_call(
        functools.partial(up_kernel, at, len(w_pieces)),
        out_shape=(out, out),
        in_specs=[any_] * (5 + len(w_pieces)),
        out_specs=(whole, whole),
        scratch_shapes=[
            pltpu.VMEM((4, rows, depth), jnp.bfloat16),
            pltpu.VMEM((4, depth, width), jnp.bfloat16),
            pltpu.VMEM((rows, width), jnp.bfloat16),
            pltpu.VMEM((rows, width), jnp.float32),
            pltpu.SemaphoreType.DMA((4,)),
            pltpu.SemaphoreType.DMA((4,)),
            pltpu.SemaphoreType.DMA,
        ],
        compiler_params=pltpu.CompilerParams(vmem_limit_bytes=28 * MIB),
        cost_estimate=pl.CostEstimate(
            flops=8 * rows * depth * width, bytes_accessed=8 * depth * (rows + width), transcendentals=rows * width
        ),
        name="up",
    )(*tokens, *w_pieces, cot)


def down_kernel(own, pair, x_part, z_part, x_pair, z_pair, *rest):
    pieces = rest[:10]
    out, g_buf, w_buf, g_sem, w_sem = rest[10:]
    r, c = lax.axis_index("row"), lax.axis_index("col")
    pltpu.make_async_copy(own, w_buf.at[c], w_sem.at[c]).start()
    pltpu.make_async_copy(pair, w_buf.at[c ^ 1], w_sem.at[c ^ 1]).start()
    h = x_part.shape[0]
    zs, part, _ = z_part.shape
    for m, xs, zp in ((2, x_part, z_part), (3, x_pair, z_pair)):
        slot = c ^ m
        pltpu.make_async_copy(xs, w_buf.at[slot, pl.ds(0, h)], w_sem.at[slot]).start()
        for z in range(zs):
            pltpu.make_async_copy(zp.at[z], w_buf.at[slot, pl.ds(h + z * part, part)], w_sem.at[slot]).start()
    width = pieces[0].shape[1]
    rows = pieces[0].shape[0]
    half = rows // 2
    for k in range(2):
        cols = pl.ds(k * width, width)
        mine, prev, nxt, far_a, far_b = pieces[5 * k : 5 * k + 5]
        for src, d in ((mine, 0), (prev, 3), (nxt, 1)):
            slot = turned_from((r + d) & 3, c)
            pltpu.make_async_copy(src, g_buf.at[slot, :, cols], g_sem.at[slot]).start()
        slot = turned_from((r + 2) & 3, c)
        pltpu.make_async_copy(far_a, g_buf.at[slot, pl.ds(0, half), cols], g_sem.at[slot]).start()
        pltpu.make_async_copy(far_b, g_buf.at[slot, pl.ds(half, half), cols], g_sem.at[slot]).start()
    for j in range(4):
        pltpu.make_async_copy(own, w_buf.at[j], w_sem.at[j]).wait()
        pltpu.make_async_copy(g_buf.at[j], g_buf.at[j], g_sem.at[j]).wait()
    depth = w_buf.shape[1]
    tile = 256

    @pl.loop(0, depth // tile)
    def _(i):
        at = pl.ds(pl.multiple_of(i * tile, tile), tile)
        total = None
        for j in range(4):
            y = lax.dot_general(
                g_buf[j], w_buf[j, at, :], (((1,), (1,)), ((), ())), preferred_element_type=jnp.float32
            )
            total = y if total is None else total + y
        out[:, at] = total.astype(out.dtype)


def down(w_pieces, pieces):
    depth, ff = w_pieces[0].shape
    rows = pieces[0].shape[0]
    any_ = pl.BlockSpec(memory_space=pl.ANY)
    return pl.pallas_call(
        down_kernel,
        out_shape=jax.ShapeDtypeStruct((rows, depth), jnp.bfloat16),
        in_specs=[any_] * 16,
        out_specs=pl.BlockSpec(memory_space=pltpu.VMEM),
        scratch_shapes=[
            pltpu.VMEM((4, rows, ff), jnp.bfloat16),
            pltpu.VMEM((4, depth, ff), jnp.bfloat16),
            pltpu.SemaphoreType.DMA((4,)),
            pltpu.SemaphoreType.DMA((4,)),
        ],
        compiler_params=pltpu.CompilerParams(vmem_limit_bytes=28 * MIB),
        cost_estimate=pl.CostEstimate(
            flops=8 * rows * depth * ff, bytes_accessed=8 * ff * (rows + depth), transcendentals=0
        ),
        name="down",
    )(*w_pieces, *pieces)


def body(tokens, w_up, cotangent):
    depth, ff = w_up.shape
    width = ff // 2
    zs = min(8, lax.axis_size("dp"))
    z = lax.axis_index("dp") % zs
    part = depth // zs
    piece = lax.dynamic_slice(w_up, (z * part, width), (part, width))
    slices = [to_row(piece, 1), to_row(piece, -1), to_row(piece, 2)]
    t_x = col_swap(tokens, 2)
    t_pair = col_swap(tokens, 1)
    late = z_gather(jnp.stack(slices))
    early = ring(w_up[:, :width])
    t_x_pair = col_swap(t_x, 1)
    ts = (tokens, t_pair, t_x, t_x_pair)
    half = depth // 2
    part2 = half // zs
    x_part = col_swap(w_up[:half], 2)
    piece2 = lax.dynamic_slice(w_up, (half + z * part2, 0), (part2, ff))
    z_part = z_gather(col_swap(piece2, 2))
    w_pair = col_swap(w_up, 1)
    x_pair = col_swap(x_part, 1)
    z_pair = col_swap(z_part, 1)

    hidden_a, d_a = up(ts, (w_up,) + early, cotangent, 0, width)
    m_a = mirror(d_a)
    g_a = (m_a,) + ring(m_a)
    hidden_b, d_b = up(ts, (w_up, late), cotangent, width, width)
    m_b = mirror(d_b)
    g_b = (m_b,) + ring(m_b)
    d_tokens = down((w_up, w_pair, x_part, z_part, x_pair, z_pair), g_a + g_b)
    return jnp.concatenate([hidden_a, hidden_b], axis=1), d_tokens


def solution(mesh):
    placed = (P(("dp", "row"), "col"), P("row", "col"), P(("dp", "row"), "col"))
    return jax.shard_map(
        body,
        mesh=mesh,
        in_specs=placed,
        out_specs=(P(("dp", "row"), "col"), P(("dp", "col"), "row")),
        check_vma=False,
    )
```

time: 436 us -> 185 us (0.42)
  waiting for transfers between devices: 352 us -> 90.1 us
  Pallas kernels: 0 us -> 27.4 us
  matrix products: 20.9 us -> 0 us
  between operations: 0.75 us -> 14.2 us
  other arithmetic: 13.1 us -> 1.76 us
  local copies, waits for them, and re-layouts: 1.45 us -> 11.5 us
  starting transfers between devices: 45 us -> 36.1 us
    ppermute x24 -> x25, waiting for transfers between devices: 352 us -> 90.1 us  [the longest x8 35 us: col_swap(): return lax.ppermute(x, 'col', [(i, i ^ m) for i in range(n)])]
    pallas_call x0 -> x3, Pallas kernels: none -> 27.4 us  [the longest x2 16.5 us: up(): pl.pallas_call(functools.partial(up_kernel, at, len(w_pieces)), out_shape...]
    dot_general x8 -> x0, matrix products: 20.9 us -> none  [the longest x4 10.7 us: body(): pre = pre + jnp.dot(x_cur, w_cur, preferred_element_type=jnp.float32)]
    select_n x9 -> x0, other arithmetic: 13.1 us -> none  [the longest x7 13 us: skewed(): block = jnp.where(index >> level & 1 == 1, moved, block)]
    ppermute x24 -> x25, starting transfers between devices: 45 us -> 36.1 us  [the longest x15 25.6 us: to_row(): return lax.ppermute(x, 'row', [(i, (i + d) % n) for i in range(n)])]
    unnamed x4 -> x22, local copies, waits for them, and re-layouts: 1.45 us -> 6.91 us
  transfers between devices with their start and end apart: 24 -> 27, of which waited for: 19 -> 14; matrix products, arithmetic and copies ran while one was open for 6% -> 3% of each run, Pallas kernels for 0% -> 9%
where the time goes in v1:
time: 185 us; the launch traced here: 181 us
  waiting for transfers between devices  90.1 us (49%)
  starting transfers between devices  36.1 us (20%)
  Pallas kernels  27.4 us (15%)
  between operations  14.2 us (8%)
  local copies, waits for them, and re-layouts  11.5 us (6%)
    ppermute x8, waiting for transfers between devices, col_swap(): return lax.ppermute(x, 'col', [(i, i ^ m) for i in range(n)])  35 us
    ppermute x2, waiting for transfers between devices, mirror(): return lax.ppermute(x, ('row', 'col'), route((4, 4), turned))  28.2 us
    ppermute x15, waiting for transfers between devices, to_row(): return lax.ppermute(x, 'row', [(i, (i + d) % n) for i in range(n)])  26.8 us
    ppermute x15, starting transfers between devices, to_row(): return lax.ppermute(x, 'row', [(i, (i + d) % n) for i in range(n)])  25.6 us
    pallas_call x2, Pallas kernels, up(): pl.pallas_call(functools.partial(up_kernel, at, len(w_pieces)), out_shape...  16.5 us
    pallas_call x1, Pallas kernels, down(): pl.pallas_call(down_kernel, out_shape=jax.ShapeDtypeStruct((rows, depth),...  10.9 us
    unnamed x22, local copies, waits for them, and re-layouts  6.91 us
    ppermute x8, starting transfers between devices, col_swap(): return lax.ppermute(x, 'col', [(i, i ^ m) for i in range(n)])  6.09 us
  transfers between devices with their start and end apart: 27, of which 14 were waited for; matrix products, arithmetic and copies ran while one was open for 3% of the time, Pallas kernels for 9%

profile of v1, /device:TPU:4, one launch (start us, length us, event | category | flops | bytes accessed | tf_op | source)
XLA Modules:
  0.0 181.1 jit_solution(1281243344436517364)
XLA Ops:
  7.2 0.9 constant_dynamic-slice_fusion.1
  8.2 2.3 %collective-permute-start.12 = (bf16[96,768]{1,0:T(8,128)(2,1)S(1)}, bf16[96,768]{1,0:T(8,128)(2,1)S(1)}, u32[]{:S(2)}, u32[]{:S(2)}) collective-permute-start(bf16[96,768]{1,0:T(8,128)(2,1)S(1)} %constant_dynamic-slice_fusion.1), channel_id=1, source_target_pairs={{0,2},{1,3},{2,0},{3,1},{4,6},{5,7},{6,4},{7,5},{8,10},{9,11},{10,... | collective-permute-start | bytes 442376 | tf_op jit(solution)/shard_map/ppermute | solution.py:31
  10.5 4.8 %collective-permute-done.12 = bf16[96,768]{1,0:T(8,128)(2,1)S(1)} collective-permute-done((bf16[96,768]{1,0:T(8,128)(2,1)S(1)}, bf16[96,768]{1,0:T(8,128)(2,1)S(1)}, u32[]{:S(2)}, u32[]{:S(2)}) %collective-permute-start.12) | collective-permute-done | bytes 147488 | tf_op jit(solution)/shard_map/ppermute | solution.py:31
  15.3 0.7 copy-done.10
  16.1 0.9 constant_dynamic-slice_fusion
  17.0 3.3 %collective-permute-start.9 = (bf16[192,384]{1,0:T(8,128)(2,1)S(1)}, bf16[192,384]{1,0:T(8,128)(2,1)S(1)}, u32[]{:S(2)}, u32[]{:S(2)}) collective-permute-start(bf16[192,384]{1,0:T(8,128)(2,1)S(1)} %constant_dynamic-slice_fusion), channel_id=1, source_target_pairs={{0,8},{4,12},{8,0},{12,4},{1,9},{5,13},{9,1},{13,5},{2,10},{6,14},... | collective-permute-start | bytes 442376 | tf_op jit(solution)/shard_map/ppermute | solution.py:26
  20.3 1.1 collective-permute-start.8
  21.3 1.0 collective-permute-start.7
  22.3 2.9 %collective-permute-done.9 = bf16[192,384]{1,0:T(8,128)(2,1)S(1)} collective-permute-done((bf16[192,384]{1,0:T(8,128)(2,1)S(1)}, bf16[192,384]{1,0:T(8,128)(2,1)S(1)}, u32[]{:S(2)}, u32[]{:S(2)}) %collective-permute-start.9) | collective-permute-done | bytes 147488 | tf_op jit(solution)/shard_map/ppermute | solution.py:26
  25.2 1.6 collective-permute-done.8
  26.8 0.9 collective-permute-done.7
  27.7 0.8 pad_maximum_fusion.1
  28.5 1.1 collective-permute-start.1
  29.7 1.5 slice.24
  31.2 0.1 collective-permute-start.3
  31.3 3.2 %collective-permute-start.4 = (bf16[1536,384]{1,0:T(8,128)(2,1)S(1)}, bf16[1536,384]{1,0:T(8,128)(2,1)S(1)}, u32[]{:S(2)}, u32[]{:S(2)}) collective-permute-start(bf16[1536,384]{1,0:T(8,128)(2,1)S(1)} %slice.24), channel_id=1, source_target_pairs={{0,12},{4,0},{8,4},{12,8},{1,13},{5,1},{9,5},{13,9},{2,14},{6,2},{... | collective-permute-start | bytes 3538952 | tf_op jit(solution)/shard_map/ppermute | solution.py:26
  34.6 30.2 %collective-permute-done.1.t2 = bf16[512,1536]{1,0:T(8,128)(2,1)S(1)} collective-permute-done((bf16[512,1536]{1,0:T(8,128)(2,1)}, bf16[512,1536]{1,0:T(8,128)(2,1)S(1)}, u32[]{:S(2)}, u32[]{:S(2)}) %collective-permute-start.1) | collective-permute-done | bytes 1572896 | tf_op jit(solution)/shard_map/ppermute | solution.py:31
  64.8 1.6 collective-permute-start.5
  66.4 1.8 %collective-permute-start.6 = (bf16[768,384]{1,0:T(8,128)(2,1)S(1)}, bf16[768,384]{1,0:T(8,128)(2,1)S(1)}, u32[]{:S(2)}, u32[]{:S(2)}) collective-permute-start(bf16[768,384]{1,0:T(8,128)(2,1)S(1)} %slice.33), channel_id=1, source_target_pairs={{0,12},{4,0},{8,4},{12,8},{1,13},{5,1},{9,5},{13,9},{2,14},{6,2},{... | collective-permute-start | bytes 1769480 | tf_op jit(solution)/shard_map/ppermute | solution.py:26
  68.4 2.1 %collective-permute-start.11 = (bf16[768,768]{1,0:T(8,128)(2,1)S(1)}, bf16[768,768]{1,0:T(8,128)(2,1)}, u32[]{:S(2)}, u32[]{:S(2)}) collective-permute-start(bf16[768,768]{1,0:T(8,128)(2,1)S(1)} %slice.27), channel_id=1, source_target_pairs={{0,2},{1,3},{2,0},{3,1},{4,6},{5,7},{6,4},{7,5},{8,10},{9,11},{10,... | collective-permute-start | bytes 3538952 | tf_op jit(solution)/shard_map/ppermute | solution.py:31
  70.5 11.4 %collective-permute-done.5.rest_3_ = bf16[768,384]{1,0:T(8,128)(2,1)S(1)} collective-permute-done((bf16[768,384]{1,0:T(8,128)(2,1)S(1)}, bf16[768,384]{1,0:T(8,128)(2,1)S(1)}, u32[]{:S(2)}, u32[]{:S(2)}) %collective-permute-start.5) | collective-permute-done | bytes 589856 | tf_op jit(solution)/shard_map/ppermute | solution.py:26
  81.8 0.1 collective-permute-done.6.rest_4_
  82.0 6.3 %up.2 = (bf16[512,384]{1,0:T(8,128)(2,1)S(1)}, bf16[512,384]{1,0:T(8,128)(2,1)S(1)}) custom-call(bf16[512,1536]{1,0:T(8,128)(2,1)} %t0.3, bf16[512,1536]{1,0:T(8,128)(2,1)S(1)} %collective-permute-done.t1, bf16[512,1536]{1,0:T(8,128)(2,1)S(1)} %collective-permute-done.1.t2, bf16[512,1536]{1,0:T(8,128)(2,1)S(1)} %collective-permute-done.2.t3, ...), custom_call_target="tpu_custom_call" | custom-call | flops 2415919104 | bytes 11010048 | tf_op jit(solution)/shard_map/up/pallas_call | solution.py:132
  88.3 2.9 %collective-permute-start.15 = (bf16[512,384]{1,0:T(8,128)(2,1)S(1)}, bf16[512,384]{1,0:T(8,128)(2,1)}, u32[]{:S(2)}, u32[]{:S(2)}) collective-permute-start(bf16[512,384]{1,0:T(8,128)(2,1)S(1)} %get-tuple-element.8), channel_id=1, source_target_pairs={{0,12},{1,4},{2,0},{3,8},{4,1},{5,9},{6,5},{7,13},{8,10},{9,2},{10... | collective-permute-start | bytes 1179656 | tf_op jit(solution)/shard_map/ppermute | solution.py:44
  91.3 16.3 %collective-permute-done.15.rest_0_ = bf16[512,384]{1,0:T(8,128)(2,1)} collective-permute-done((bf16[512,384]{1,0:T(8,128)(2,1)S(1)}, bf16[512,384]{1,0:T(8,128)(2,1)}, u32[]{:S(2)}, u32[]{:S(2)}) %collective-permute-start.15) | collective-permute-done | bytes 393248 | tf_op jit(solution)/shard_map/ppermute | solution.py:44
  107.6 0.4 collective-permute-start.13
  108.0 0.1 collective-permute-start.14
  108.1 1.4 copy-done.2
  109.5 1.4 copy-done.4
  110.9 1.4 copy-done.6
  112.3 2.0 %copy-done.7 = bf16[24,192,384]{2,1,0:T(8,128)(2,1)S(1)} copy-done((bf16[24,192,384]{2,1,0:T(8,128)(2,1)S(1)}, bf16[24,192,384]{2,1,0:T(8,128)(2,1)}, u32[]{:S(2)}) %copy-start.7) | copy-done | bytes 3538968
  114.3 10.2 %up.3 = (bf16[512,384]{1,0:T(8,128)(2,1)S(1)}, bf16[512,384]{1,0:T(8,128)(2,1)S(1)}) custom-call(bf16[512,1536]{1,0:T(8,128)(2,1)} %t0.3, bf16[512,1536]{1,0:T(8,128)(2,1)S(1)} %copy-done.4, bf16[512,1536]{1,0:T(8,128)(2,1)S(1)} %copy-done.2, bf16[512,1536]{1,0:T(8,128)(2,1)S(1)} %copy-done.6, bf16[1536,768]{1,0:T(8,128)(2,1)S(1)} %copy-done, ...), custom_call_target="tpu_custom_call" | custom-call | flops 2415919104 | bytes 11010048 | tf_op jit(solution)/shard_map/up/pallas_call | solution.py:132
  124.5 1.4 collective-permute-start.20
  125.9 2.0 %collective-permute-start.17 = (bf16[512,384]{1,0:T(8,128)(2,1)}, bf16[512,384]{1,0:T(8,128)(2,1)S(1)}, u32[]{:S(2)}, u32[]{:S(2)}) collective-permute-start(bf16[512,384]{1,0:T(8,128)(2,1)} %collective-permute-done.15.rest_0_), channel_id=1, source_target_pairs={{0,12},{4,0},{8,4},{12,8},{1,13},{5,1},{9,5},{13,9},{2,14},{6,2},{... | collective-permute-start | bytes 1179656 | tf_op jit(solution)/shard_map/ppermute | solution.py:26
  127.9 11.9 %collective-permute-done.20.rest_5_ = bf16[512,384]{1,0:T(8,128)(2,1)S(1)} collective-permute-done((bf16[512,384]{1,0:T(8,128)(2,1)S(1)}, bf16[512,384]{1,0:T(8,128)(2,1)S(1)}, u32[]{:S(2)}, u32[]{:S(2)}) %collective-permute-start.20) | collective-permute-done | bytes 393248 | tf_op jit(solution)/shard_map/ppermute | solution.py:44
  139.9 6.0 %collective-permute-start.22 = (bf16[512,384]{1,0:T(8,128)(2,1)S(1)}, bf16[512,384]{1,0:T(8,128)(2,1)S(1)}, u32[]{:S(2)}, u32[]{:S(2)}) collective-permute-start(bf16[512,384]{1,0:T(8,128)(2,1)S(1)} %collective-permute-done.20.rest_5_), channel_id=1, source_target_pairs={{0,12},{4,0},{8,4},{12,8},{1,13},{5,1},{9,5},{13,9},{2,14},{6,2},{... | collective-permute-start | bytes 1179656 | tf_op jit(solution)/shard_map/ppermute | solution.py:26
  145.9 0.9 slice.34
  146.9 2.8 %collective-permute-done.21.rest_6_ = bf16[512,384]{1,0:T(8,128)(2,1)S(1)} collective-permute-done((bf16[512,384]{1,0:T(8,128)(2,1)S(1)}, bf16[512,384]{1,0:T(8,128)(2,1)S(1)}, u32[]{:S(2)}, u32[]{:S(2)}) %collective-permute-start.21) | collective-permute-done | bytes 393248 | tf_op jit(solution)/shard_map/ppermute | solution.py:26
  149.6 1.0 collective-permute-start.18
  150.6 3.5 %collective-permute-done.22.rest_7_ = bf16[512,384]{1,0:T(8,128)(2,1)S(1)} collective-permute-done((bf16[512,384]{1,0:T(8,128)(2,1)S(1)}, bf16[512,384]{1,0:T(8,128)(2,1)S(1)}, u32[]{:S(2)}, u32[]{:S(2)}) %collective-permute-start.22) | collective-permute-done | bytes 393248 | tf_op jit(solution)/shard_map/ppermute | solution.py:26
  154.1 1.3 collective-permute-start.19
  155.5 0.8 collective-permute-start.23
  156.3 2.5 %collective-permute-start.24 = (bf16[256,384]{1,0:T(8,128)(2,1)S(1)}, bf16[256,384]{1,0:T(8,128)(2,1)S(1)}, u32[]{:S(2)}, u32[]{:S(2)}) collective-permute-start(bf16[256,384]{1,0:T(8,128)(2,1)S(1)} %slice.37), channel_id=1, source_target_pairs={{0,12},{4,0},{8,4},{12,8},{1,13},{5,1},{9,5},{13,9},{2,14},{6,2},{... | collective-permute-start | bytes 589832 | tf_op jit(solution)/shard_map/ppermute | solution.py:26
  158.8 0.9 pad_maximum_fusion
  159.7 1.6 collective-permute-done.19.rest_4_
  161.3 1.1 collective-permute-done.23.rest_8_
  162.4 1.0 collective-permute-done.24.rest_9_
  163.4 10.9 %down.1 = bf16[512,1536]{1,0:T(8,128)(2,1)} custom-call(bf16[1536,768]{1,0:T(8,128)(2,1)S(1)} %copy-done, bf16[1536,768]{1,0:T(8,128)(2,1)} %collective-permute-done.10.pair, bf16[768,768]{1,0:T(8,128)(2,1)} %collective-permute-done.11.x_part, bf16[8,96,768]{2,1,0:T(8,128)(2,1)S(1)} %bitcast.7, bf16[768,768]{1,0:T(8,128)(2,1)} %collective-permute-done.13.x_pair, ...), custom_call_target="tpu_custom_call" | custom-call | flops 4831838208 | bytes 12582912 | tf_op jit(solution)/shard_map/down/pallas_call | solution.py:201
  (45 shorter events, 0.5 us)
Async XLA Ops:
  7.2 100.8 %all-gather.7.cloned.1.call-start = ((), (), s32[]{:S(2)}) async-start(), calls=%async_computation.1 | async-start | bytes 1327104 | tf_op jit(solution)/shard_map/all_gather | solution.py:64
  8.2 7.2 %collective-permute-start.12 = (bf16[96,768]{1,0:T(8,128)(2,1)S(1)}, bf16[96,768]{1,0:T(8,128)(2,1)S(1)}, u32[]{:S(2)}, u32[]{:S(2)}) collective-permute-start(bf16[96,768]{1,0:T(8,128)(2,1)S(1)} %constant_dynamic-slice_fusion.1), channel_id=1, source_target_pairs={{0,2},{1,3},{2,0},{3,1},{4,6},{5,7},{6,4},{7,5},{8,10},{9,11},{10,... | collective-permute-start | bytes 442376 | tf_op jit(solution)/shard_map/ppermute | solution.py:31
  15.3 0.7 copy-start.10
  16.0 92.1 %all-gather.5.cloned.1.call-start = ((), (), s32[]{:S(2)}) async-start(), calls=%async_computation | async-start | bytes 3981312 | tf_op jit(solution)/shard_map/all_gather | solution.py:64
  17.0 8.2 %collective-permute-start.9 = (bf16[192,384]{1,0:T(8,128)(2,1)S(1)}, bf16[192,384]{1,0:T(8,128)(2,1)S(1)}, u32[]{:S(2)}, u32[]{:S(2)}) collective-permute-start(bf16[192,384]{1,0:T(8,128)(2,1)S(1)} %constant_dynamic-slice_fusion), channel_id=1, source_target_pairs={{0,8},{4,12},{8,0},{12,4},{1,9},{5,13},{9,1},{13,5},{2,10},{6,14},... | collective-permute-start | bytes 442376 | tf_op jit(solution)/shard_map/ppermute | solution.py:26
  20.3 6.5 %collective-permute-start.8 = (bf16[192,384]{1,0:T(8,128)(2,1)S(1)}, bf16[192,384]{1,0:T(8,128)(2,1)S(1)}, u32[]{:S(2)}, u32[]{:S(2)}) collective-permute-start(bf16[192,384]{1,0:T(8,128)(2,1)S(1)} %constant_dynamic-slice_fusion), channel_id=1, source_target_pairs={{0,12},{4,0},{8,4},{12,8},{1,13},{5,1},{9,5},{13,9},{2,14},{6,2},{... | collective-permute-start | bytes 442376 | tf_op jit(solution)/shard_map/ppermute | solution.py:26
  21.3 6.4 %collective-permute-start.7 = (bf16[192,384]{1,0:T(8,128)(2,1)S(1)}, bf16[192,384]{1,0:T(8,128)(2,1)S(1)}, u32[]{:S(2)}, u32[]{:S(2)}) collective-permute-start(bf16[192,384]{1,0:T(8,128)(2,1)S(1)} %constant_dynamic-slice_fusion), channel_id=1, source_target_pairs={{0,4},{4,8},{8,12},{12,0},{1,5},{5,9},{9,13},{13,1},{2,6},{6,10},{... | collective-permute-start | bytes 442376 | tf_op jit(solution)/shard_map/ppermute | solution.py:26
  28.5 36.2 %collective-permute-start.1 = (bf16[512,1536]{1,0:T(8,128)(2,1)}, bf16[512,1536]{1,0:T(8,128)(2,1)S(1)}, u32[]{:S(2)}, u32[]{:S(2)}) collective-permute-start(bf16[512,1536]{1,0:T(8,128)(2,1)} %t0.3), channel_id=1, source_target_pairs={{0,2},{1,3},{2,0},{3,1},{4,6},{5,7},{6,4},{7,5},{8,10},{9,11},{10,... | collective-permute-start | bytes 4718600 | tf_op jit(solution)/shard_map/ppermute | solution.py:31
  29.7 38.7 %collective-permute-start = (bf16[512,1536]{1,0:T(8,128)(2,1)}, bf16[512,1536]{1,0:T(8,128)(2,1)S(1)}, u32[]{:S(2)}, u32[]{:S(2)}) collective-permute-start(bf16[512,1536]{1,0:T(8,128)(2,1)} %t0.3), channel_id=1, source_target_pairs={{0,1},{1,0},{2,3},{3,2},{4,5},{5,4},{6,7},{7,6},{8,9},{9,8},{10,11... | collective-permute-start | bytes 4718600 | tf_op jit(solution)/shard_map/ppermute | solution.py:31
  29.7 38.6 %copy-start = (bf16[1536,768]{1,0:T(8,128)(2,1)S(1)}, bf16[1536,768]{1,0:T(8,128)(2,1)}, u32[]{:S(2)}) copy-start(bf16[1536,768]{1,0:T(8,128)(2,1)} %own.1) | copy-start | bytes 7077892
  31.2 33.5 %collective-permute-start.3 = (bf16[1536,384]{1,0:T(8,128)(2,1)S(1)}, bf16[1536,384]{1,0:T(8,128)(2,1)S(1)}, u32[]{:S(2)}, u32[]{:S(2)}) collective-permute-start(bf16[1536,384]{1,0:T(8,128)(2,1)S(1)} %slice.24), channel_id=1, source_target_pairs={{0,4},{4,8},{8,12},{12,0},{1,5},{5,9},{9,13},{13,1},{2,6},{6,10},{... | collective-permute-start | bytes 3538952 | tf_op jit(solution)/shard_map/ppermute | solution.py:26
  31.3 35.0 %collective-permute-start.4 = (bf16[1536,384]{1,0:T(8,128)(2,1)S(1)}, bf16[1536,384]{1,0:T(8,128)(2,1)S(1)}, u32[]{:S(2)}, u32[]{:S(2)}) collective-permute-start(bf16[1536,384]{1,0:T(8,128)(2,1)S(1)} %slice.24), channel_id=1, source_target_pairs={{0,12},{4,0},{8,4},{12,8},{1,13},{5,1},{9,5},{13,9},{2,14},{6,2},{... | collective-permute-start | bytes 3538952 | tf_op jit(solution)/shard_map/ppermute | solution.py:26
  64.7 17.2 %copy-start.1 = (bf16[512,1536]{1,0:T(8,128)(2,1)}, bf16[512,1536]{1,0:T(8,128)(2,1)S(1)}, u32[]{:S(2)}) copy-start(bf16[512,1536]{1,0:T(8,128)(2,1)S(1)} %collective-permute-done.1.t2) | copy-start | bytes 4718596
  64.7 17.2 %collective-permute-start.2 = (bf16[512,1536]{1,0:T(8,128)(2,1)S(1)}, bf16[512,1536]{1,0:T(8,128)(2,1)S(1)}, u32[]{:S(2)}, u32[]{:S(2)}) collective-permute-start(bf16[512,1536]{1,0:T(8,128)(2,1)S(1)} %collective-permute-done.1.t2), channel_id=1, source_target_pairs={{0,1},{1,0},{2,3},{3,2},{4,5},{5,4},{6,7},{7,6},{8,9},{9,8},{10,11... | collective-permute-start | bytes 4718600 | tf_op jit(solution)/shard_map/ppermute | solution.py:31
  64.8 17.2 %copy-start.8 = (bf16[512,768]{1,0:T(8,128)(2,1)S(1)}, bf16[512,768]{1,0:T(8,128)(2,1)}, u32[]{:S(2)}) copy-start(bf16[512,768]{1,0:T(8,128)(2,1)} %rest_2_.1) | copy-start | bytes 2359300
  64.8 17.0 %collective-permute-start.5 = (bf16[768,384]{1,0:T(8,128)(2,1)S(1)}, bf16[768,384]{1,0:T(8,128)(2,1)S(1)}, u32[]{:S(2)}, u32[]{:S(2)}) collective-permute-start(bf16[768,384]{1,0:T(8,128)(2,1)S(1)} %slice.32), channel_id=1, source_target_pairs={{0,4},{4,8},{8,12},{12,0},{1,5},{5,9},{9,13},{13,1},{2,6},{6,10},{... | collective-permute-start | bytes 1769480 | tf_op jit(solution)/shard_map/ppermute | solution.py:26
  66.4 15.5 %collective-permute-start.6 = (bf16[768,384]{1,0:T(8,128)(2,1)S(1)}, bf16[768,384]{1,0:T(8,128)(2,1)S(1)}, u32[]{:S(2)}, u32[]{:S(2)}) collective-permute-start(bf16[768,384]{1,0:T(8,128)(2,1)S(1)} %slice.33), channel_id=1, source_target_pairs={{0,12},{4,0},{8,4},{12,8},{1,13},{5,1},{9,5},{13,9},{2,14},{6,2},{... | collective-permute-start | bytes 1769480 | tf_op jit(solution)/shard_map/ppermute | solution.py:26
  68.3 87.2 %collective-permute-start.10 = (bf16[1536,768]{1,0:T(8,128)(2,1)S(1)}, bf16[1536,768]{1,0:T(8,128)(2,1)}, u32[]{:S(2)}, u32[]{:S(2)}) collective-permute-start(bf16[1536,768]{1,0:T(8,128)(2,1)S(1)} %copy-done), channel_id=1, source_target_pairs={{0,1},{1,0},{2,3},{3,2},{4,5},{5,4},{6,7},{7,6},{8,9},{9,8},{10,11... | collective-permute-start | bytes 7077896 | tf_op jit(solution)/shard_map/ppermute | solution.py:31
  68.4 20.0 %copy-start.3 = (bf16[512,1536]{1,0:T(8,128)(2,1)}, bf16[512,1536]{1,0:T(8,128)(2,1)S(1)}, u32[]{:S(2)}) copy-start(bf16[512,1536]{1,0:T(8,128)(2,1)S(1)} %collective-permute-done.t1) | copy-start | bytes 4718596
  68.4 39.2 %collective-permute-start.11 = (bf16[768,768]{1,0:T(8,128)(2,1)S(1)}, bf16[768,768]{1,0:T(8,128)(2,1)}, u32[]{:S(2)}, u32[]{:S(2)}) collective-permute-start(bf16[768,768]{1,0:T(8,128)(2,1)S(1)} %slice.27), channel_id=1, source_target_pairs={{0,2},{1,3},{2,0},{3,1},{4,6},{5,7},{6,4},{7,5},{8,10},{9,11},{10,... | collective-permute-start | bytes 3538952 | tf_op jit(solution)/shard_map/ppermute | solution.py:31
  82.0 6.4 %copy-start.5 = (bf16[512,1536]{1,0:T(8,128)(2,1)}, bf16[512,1536]{1,0:T(8,128)(2,1)S(1)}, u32[]{:S(2)}) copy-start(bf16[512,1536]{1,0:T(8,128)(2,1)S(1)} %collective-permute-done.2.t3) | copy-start | bytes 4718596
  88.3 19.2 %collective-permute-start.15 = (bf16[512,384]{1,0:T(8,128)(2,1)S(1)}, bf16[512,384]{1,0:T(8,128)(2,1)}, u32[]{:S(2)}, u32[]{:S(2)}) collective-permute-start(bf16[512,384]{1,0:T(8,128)(2,1)S(1)} %get-tuple-element.8), channel_id=1, source_target_pairs={{0,12},{1,4},{2,0},{3,8},{4,1},{5,9},{6,5},{7,13},{8,10},{9,2},{10... | collective-permute-start | bytes 1179656 | tf_op jit(solution)/shard_map/ppermute | solution.py:44
  107.6 18.3 %collective-permute-start.16 = (bf16[512,384]{1,0:T(8,128)(2,1)}, bf16[512,384]{1,0:T(8,128)(2,1)}, u32[]{:S(2)}, u32[]{:S(2)}) collective-permute-start(bf16[512,384]{1,0:T(8,128)(2,1)} %collective-permute-done.15.rest_0_), channel_id=1, source_target_pairs={{0,4},{4,8},{8,12},{12,0},{1,5},{5,9},{9,13},{13,1},{2,6},{6,10},{... | collective-permute-start | bytes 1179656 | tf_op jit(solution)/shard_map/ppermute | solution.py:26
  107.6 48.7 %collective-permute-start.13 = (bf16[768,768]{1,0:T(8,128)(2,1)}, bf16[768,768]{1,0:T(8,128)(2,1)}, u32[]{:S(2)}, u32[]{:S(2)}) collective-permute-start(bf16[768,768]{1,0:T(8,128)(2,1)} %collective-permute-done.11.x_part), channel_id=1, source_target_pairs={{0,1},{1,0},{2,3},{3,2},{4,5},{5,4},{6,7},{7,6},{8,9},{9,8},{10,11... | collective-permute-start | bytes 3538952 | tf_op jit(solution)/shard_map/ppermute | solution.py:31
  108.0 51.8 %collective-permute-start.14 = (bf16[8,96,768]{2,1,0:T(8,128)(2,1)}, bf16[8,96,768]{2,1,0:T(8,128)(2,1)}, u32[]{:S(2)}, u32[]{:S(2)}) collective-permute-start(bf16[8,96,768]{2,1,0:T(8,128)(2,1)} %bitcast.6), channel_id=1, source_target_pairs={{0,1},{1,0},{2,3},{3,2},{4,5},{5,4},{6,7},{7,6},{8,9},{9,8},{10,11... | collective-permute-start | bytes 3538952 | tf_op jit(solution)/shard_map/ppermute | solution.py:31
  108.1 1.4 copy-start.2
  109.5 1.4 copy-start.4
  110.9 1.4 copy-start.6
  112.3 2.0 %copy-start.7 = (bf16[24,192,384]{2,1,0:T(8,128)(2,1)S(1)}, bf16[24,192,384]{2,1,0:T(8,128)(2,1)}, u32[]{:S(2)}) copy-start(bf16[24,192,384]{2,1,0:T(8,128)(2,1)} %all-gather.5.cloned.1.call-done) | copy-start | bytes 10616836
  124.5 38.9 %copy-start.9 = (bf16[768,768]{1,0:T(8,128)(2,1)S(1)}, bf16[768,768]{1,0:T(8,128)(2,1)}, u32[]{:S(2)}) copy-start(bf16[768,768]{1,0:T(8,128)(2,1)} %all-gather.7.cloned.1.call-done) | copy-start | bytes 3538948
  124.5 15.4 %collective-permute-start.20 = (bf16[512,384]{1,0:T(8,128)(2,1)S(1)}, bf16[512,384]{1,0:T(8,128)(2,1)S(1)}, u32[]{:S(2)}, u32[]{:S(2)}) collective-permute-start(bf16[512,384]{1,0:T(8,128)(2,1)S(1)} %get-tuple-element.9), channel_id=1, source_target_pairs={{0,12},{1,4},{2,0},{3,8},{4,1},{5,9},{6,5},{7,13},{8,10},{9,2},{10... | collective-permute-start | bytes 1179656 | tf_op jit(solution)/shard_map/ppermute | solution.py:44
  125.9 14.0 %collective-permute-start.17 = (bf16[512,384]{1,0:T(8,128)(2,1)}, bf16[512,384]{1,0:T(8,128)(2,1)S(1)}, u32[]{:S(2)}, u32[]{:S(2)}) collective-permute-start(bf16[512,384]{1,0:T(8,128)(2,1)} %collective-permute-done.15.rest_0_), channel_id=1, source_target_pairs={{0,12},{4,0},{8,4},{12,8},{1,13},{5,1},{9,5},{13,9},{2,14},{6,2},{... | collective-permute-start | bytes 1179656 | tf_op jit(solution)/shard_map/ppermute | solution.py:26
  139.9 9.8 %collective-permute-start.21 = (bf16[512,384]{1,0:T(8,128)(2,1)S(1)}, bf16[512,384]{1,0:T(8,128)(2,1)S(1)}, u32[]{:S(2)}, u32[]{:S(2)}) collective-permute-start(bf16[512,384]{1,0:T(8,128)(2,1)S(1)} %collective-permute-done.20.rest_5_), channel_id=1, source_target_pairs={{0,4},{4,8},{8,12},{12,0},{1,5},{5,9},{9,13},{13,1},{2,6},{6,10},{... | collective-permute-start | bytes 1179656 | tf_op jit(solution)/shard_map/ppermute | solution.py:26
  139.9 14.3 %collective-permute-start.22 = (bf16[512,384]{1,0:T(8,128)(2,1)S(1)}, bf16[512,384]{1,0:T(8,128)(2,1)S(1)}, u32[]{:S(2)}, u32[]{:S(2)}) collective-permute-start(bf16[512,384]{1,0:T(8,128)(2,1)S(1)} %collective-permute-done.20.rest_5_), channel_id=1, source_target_pairs={{0,12},{4,0},{8,4},{12,8},{1,13},{5,1},{9,5},{13,9},{2,14},{6,2},{... | collective-permute-start | bytes 1179656 | tf_op jit(solution)/shard_map/ppermute | solution.py:26
  149.6 10.1 %collective-permute-start.18 = (bf16[256,384]{1,0:T(8,128)(2,1)S(1)}, bf16[256,384]{1,0:T(8,128)(2,1)S(1)}, u32[]{:S(2)}, u32[]{:S(2)}) collective-permute-start(bf16[256,384]{1,0:T(8,128)(2,1)S(1)} %slice.34), channel_id=1, source_target_pairs={{0,4},{4,8},{8,12},{12,0},{1,5},{5,9},{9,13},{13,1},{2,6},{6,10},{... | collective-permute-start | bytes 589832 | tf_op jit(solution)/shard_map/ppermute | solution.py:26
  154.1 7.2 %collective-permute-start.19 = (bf16[256,384]{1,0:T(8,128)(2,1)S(1)}, bf16[256,384]{1,0:T(8,128)(2,1)S(1)}, u32[]{:S(2)}, u32[]{:S(2)}) collective-permute-start(bf16[256,384]{1,0:T(8,128)(2,1)S(1)} %slice.35), channel_id=1, source_target_pairs={{0,12},{4,0},{8,4},{12,8},{1,13},{5,1},{9,5},{13,9},{2,14},{6,2},{... | collective-permute-start | bytes 589832 | tf_op jit(solution)/shard_map/ppermute | solution.py:26
  155.5 7.0 %collective-permute-start.23 = (bf16[256,384]{1,0:T(8,128)(2,1)S(1)}, bf16[256,384]{1,0:T(8,128)(2,1)S(1)}, u32[]{:S(2)}, u32[]{:S(2)}) collective-permute-start(bf16[256,384]{1,0:T(8,128)(2,1)S(1)} %slice.36), channel_id=1, source_target_pairs={{0,4},{4,8},{8,12},{12,0},{1,5},{5,9},{9,13},{13,1},{2,6},{6,10},{... | collective-permute-start | bytes 589832 | tf_op jit(solution)/shard_map/ppermute | solution.py:26
  156.3 7.1 %collective-permute-start.24 = (bf16[256,384]{1,0:T(8,128)(2,1)S(1)}, bf16[256,384]{1,0:T(8,128)(2,1)S(1)}, u32[]{:S(2)}, u32[]{:S(2)}) collective-permute-start(bf16[256,384]{1,0:T(8,128)(2,1)S(1)} %slice.37), channel_id=1, source_target_pairs={{0,12},{4,0},{8,4},{12,8},{1,13},{5,1},{9,5},{13,9},{2,14},{6,2},{... | collective-permute-start | bytes 589832 | tf_op jit(solution)/shard_map/ppermute | solution.py:26
Sparse Core Ops, SparseCore 0:
  16.1 41.8 all-gather.6
  60.3 47.1 all-gather.4

commit v2 on v0

v2 whole, which is shorter than its diff:
```python
import functools
import math

import jax
import jax.numpy as jnp
from jax import lax
from jax.experimental import pallas as pl
from jax.experimental.pallas import tpu as pltpu
from jax.sharding import PartitionSpec as P

COEFF = math.sqrt(2.0 / math.pi)
MIB = 1 << 20


ANY = pl.BlockSpec(memory_space=pl.ANY)
VMEM = pl.BlockSpec(memory_space=pltpu.VMEM)


def flat(sizes, target):
    pairs = []
    for i in range(sizes[0]):
        for j in range(sizes[1]):
            a, b = target(i, j)
            pairs.append((i * sizes[1] + j, a * sizes[1] + b))
    return pairs


def y_step(x, back=0):
    sizes = (lax.axis_size("row"), lax.axis_size("col"))
    return lax.ppermute(
        x, ("row", "col"), flat(sizes, lambda r, c: ((r + 1 - 2 * ((c ^ back) & 1)) % sizes[0], c))
    )


def z_size():
    return min(8, lax.axis_size("dp"))


def z_step(x, back=0):
    sizes, n = (lax.axis_size("dp"), lax.axis_size("col")), z_size()
    return lax.ppermute(
        x, ("dp", "col"), flat(sizes, lambda i, c: (i // n * n + (i % n + 1 - 2 * ((c ^ back) & 1)) % n, c))
    )


def opposite(x):
    n = lax.axis_size("row")
    return lax.ppermute(x, "row", [(i, (i + 2) % n) for i in range(n)])


def col_swap(x, m):
    n = lax.axis_size("col")
    return lax.ppermute(x, "col", [(i, i ^ m) for i in range(n)])


def turned(r, c):
    core = c & 1
    if (c >> 1) != (r >> 1):
        step = 2 if core else 0
    else:
        step = 1 if core else -1
    return (r + step) % 4, r


def mirror(x):
    return lax.ppermute(x, ("row", "col"), flat((4, 4), turned))


def turned_from(row, col):
    step = (row - col + 4) & 3
    cross = 1 - (step & 1)
    core = jnp.where((step == 1) | (step == 2), 1, 0)
    return 2 * ((col >> 1) ^ cross) + core


def away(i, s, core):
    return (i + jnp.where(core == 0, 4 - s, s)) & 3


def gelu_parts(pre):
    sq = pre * pre
    t = jnp.tanh(COEFF * (pre + 0.044715 * sq * pre))
    hidden = 0.5 * pre * (1.0 + t)
    slope = 0.5 * (1.0 + t) + 0.5 * pre * (1.0 - t * t) * COEFF * (1.0 + 3.0 * 0.044715 * sq)
    return hidden, slope


def params():
    return pltpu.CompilerParams(vmem_limit_bytes=16 * MIB)


def cost(flops, nbytes, trans=0):
    return pl.CostEstimate(flops=flops, bytes_accessed=nbytes, transcendentals=trans)


def mul(a, b):
    return jnp.dot(a, b, preferred_element_type=jnp.float32)


def sort_tokens_kernel(t0, t1, t2a, t2b, t3a, t3b, out, sem):
    c = lax.axis_index("col")
    h = t2a.shape[0]
    pltpu.make_async_copy(t0, out.at[c], sem).start()
    pltpu.make_async_copy(t1, out.at[c ^ 1], sem).start()
    for m, top, rest in ((2, t2a, t2b), (3, t3a, t3b)):
        pltpu.make_async_copy(top, out.at[c ^ m, pl.ds(0, h)], sem).start()
        pltpu.make_async_copy(rest, out.at[c ^ m, pl.ds(h, rest.shape[0])], sem).start()
    pltpu.make_async_copy(out, out, sem).wait()


def sort_tokens(*ts):
    rows, depth = ts[0].shape
    return pl.pallas_call(
        sort_tokens_kernel,
        out_shape=jax.ShapeDtypeStruct((4, rows, depth), jnp.bfloat16),
        in_specs=[ANY] * 6,
        out_specs=VMEM,
        scratch_shapes=[pltpu.SemaphoreType.DMA],
        compiler_params=params(),
        cost_estimate=cost(0, 16 * rows * depth),
        name="sort_tokens",
    )(*ts)


def up_part_kernel(t, own, w1, w3, p0, p1, p3, acc):
    r, core = lax.axis_index("row"), lax.axis_index("col") & 1
    z = lax.axis_index("dp") & 3
    _, q, width = p0.shape
    first, last = pl.ds(0, width), pl.ds(width, width)
    acc[...] = mul(t[r], own[...])
    for s, w in ((1, w1), (3, w3)):
        acc[:, first] += mul(t[away(r, s, core)], w[...])
    for s in range(1, 4):
        j = away(r, s, core)
        for u, p in ((0, p0), (1, p1), (3, p3)):
            k = pl.ds(pl.multiple_of(away(z, u, core) * q, 128), q)
            acc[:, last] += mul(t[j, :, k], p[s - 1])


def up_rest_kernel(t, so_far, w2, p2, cot, hidden, d_pre, acc):
    r, core = lax.axis_index("row"), lax.axis_index("col") & 1
    z = lax.axis_index("dp") & 3
    _, q, width = p2.shape
    first, last = pl.ds(0, width), pl.ds(width, width)
    acc[:, first] = so_far[:, first] + mul(t[away(r, 2, core)], w2[...])
    k = pl.ds(pl.multiple_of(away(z, 2, core) * q, 128), q)
    y = so_far[:, last]
    for s in range(1, 4):
        y += mul(t[away(r, s, core), :, k], p2[s - 1])
    acc[:, last] = y
    rows = acc.shape[0]
    tile = min(64, rows)

    @pl.loop(0, rows // tile)
    def _(i):
        part = pl.ds(pl.multiple_of(i * tile, tile), tile)
        h_val, slope = gelu_parts(acc[part, :])
        hidden[part, :] = h_val.astype(hidden.dtype)
        d_pre[part, :] = (cot[part, :].astype(jnp.float32) * slope).astype(d_pre.dtype)


def up_part(t, own, *pieces):
    _, rows, depth = t.shape
    width = own.shape[1]
    return pl.pallas_call(
        up_part_kernel,
        out_shape=jax.ShapeDtypeStruct((rows, width), jnp.float32),
        in_specs=[VMEM] * (2 + len(pieces)),
        out_specs=VMEM,
        compiler_params=params(),
        cost_estimate=cost(6 * rows * depth * width, 6 * depth * (rows + width)),
        name="up_part",
    )(t, own, *pieces)


def up_rest(t, so_far, w2, p2, cot):
    _, rows, depth = t.shape
    out = jax.ShapeDtypeStruct(cot.shape, jnp.bfloat16)
    return pl.pallas_call(
        up_rest_kernel,
        out_shape=(out, out),
        in_specs=[VMEM] * 5,
        out_specs=(VMEM, VMEM),
        scratch_shapes=[pltpu.VMEM(cot.shape, jnp.float32)],
        compiler_params=params(),
        cost_estimate=cost(2 * depth * cot.size, 2 * depth * sum(cot.shape), cot.size),
        name="up_rest",
    )(t, so_far, w2, p2, cot)


def sort_w_kernel(own, pair, x0, x1, x2, x3, y013, y2, out, sem):
    c = lax.axis_index("col")
    z = lax.axis_index("dp") & 3
    q = x0.shape[1]
    pltpu.make_async_copy(own, out.at[c], sem).start()
    pltpu.make_async_copy(pair, out.at[c ^ 1], sem).start()
    theirs = (y013.at[0], y013.at[1], y2, y013.at[2])
    for m, srcs, core in ((2, (x0, x1, x2, x3), c & 1), (3, theirs, 1 - (c & 1))):
        for u, src in enumerate(srcs):
            cols = pl.ds(pl.multiple_of(away(z, u, core) * q, 128), q)
            pltpu.make_async_copy(src, out.at[c ^ m, :, cols], sem).start()
    pltpu.make_async_copy(out, out, sem).wait()


def sort_w(*pieces):
    ff, depth = pieces[0].shape
    return pl.pallas_call(
        sort_w_kernel,
        out_shape=jax.ShapeDtypeStruct((4, ff, depth), jnp.bfloat16),
        in_specs=[ANY] * 8,
        out_specs=VMEM,
        scratch_shapes=[pltpu.SemaphoreType.DMA],
        compiler_params=params(),
        cost_estimate=cost(0, 16 * depth * ff),
        name="sort_w",
    )(*pieces)


def down_kernel(plan, w, *rest):
    r, c = lax.axis_index("row"), lax.axis_index("col")
    blocks, so_far, out = rest[: len(plan)], rest[len(plan) : -1], rest[-1]
    tile = 512

    @pl.loop(0, w.shape[2] // tile)
    def _(i):
        cols = pl.ds(pl.multiple_of(i * tile, tile), tile)
        y = so_far[0][:, cols] if so_far else None
        for s, g in zip(plan, blocks):
            part = mul(g[...], w[turned_from(away(r, s, c & 1), c), :, cols])
            y = part if y is None else y + part
        out[:, cols] = y.astype(out.dtype)


def down(w, blocks, plan, so_far, kind):
    _, ff, depth = w.shape
    rows = blocks[0].shape[0]
    more = () if so_far is None else (so_far,)
    return pl.pallas_call(
        functools.partial(down_kernel, plan),
        out_shape=jax.ShapeDtypeStruct((rows, depth), kind),
        in_specs=[VMEM] * (1 + len(blocks) + len(more)),
        out_specs=VMEM,
        compiler_params=params(),
        cost_estimate=cost(2 * len(blocks) * rows * depth * ff, 8 * ff * (rows + depth)),
        name="down",
    )(w, *blocks, *more)


def together(*xs):
    return lax.optimization_barrier(xs)


def body(tokens, w_up, cotangent):
    depth, ff = w_up.shape
    width = ff // 2
    part = depth // 4
    z = lax.axis_index("dp") % 4
    h = tokens.shape[0] // 64 * 24
    piece = lax.dynamic_slice(w_up, (z * part, width), (part, width))
    s1, s2, s3 = y_step(piece), opposite(piece), y_step(piece, 1)
    ta = col_swap(tokens[:h], 2)
    t_pair = col_swap(tokens, 1)
    p0, ta, t_pair, w0, rest, w_t = together(
        jnp.stack([s1, s2, s3]), ta, t_pair, w_up[:, :width], tokens[h:], w_up.T
    )
    p1, p3 = z_step(p0), z_step(p0, 1)
    w1, w3 = y_step(w0), y_step(w0, 1)
    tb = col_swap(rest, 2)
    p1, p3, w1, w3, ta, tb, x0 = together(
        p1, p3, w1, w3, ta, tb, lax.dynamic_slice(w_t, (0, z * part), (ff, part))
    )
    x0 = col_swap(x0, 2)
    p2 = z_step(p1)
    w2 = y_step(w1)
    t = sort_tokens(tokens, t_pair, ta, tb, col_swap(ta, 1), col_swap(tb, 1))
    so_far = up_part(t, w_up, w1, w3, p0, p1, p3)
    p2, w2, so_far, x0 = together(p2, w2, so_far, x0)
    hidden, d_pre = up_rest(t, so_far, w2, p2, cotangent)

    d_pre, x0, w_t2 = together(d_pre, x0, w_t)
    m = mirror(d_pre)
    x1, x3 = z_step(x0), z_step(x0, 1)
    w_pair = col_swap(w_t2, 1)
    m, x1, x3, w_pair = together(m, x1, x3, w_pair)
    g1, g3 = y_step(m), y_step(m, 1)
    x2 = z_step(x1)
    theirs = col_swap(jnp.stack([x0, x1, x3]), 1)
    g1, g3, x2, theirs = together(g1, g3, x2, theirs)
    g2 = y_step(g1)
    w = sort_w(w_t, w_pair, x0, x1, x2, x3, theirs, col_swap(x2, 1))
    total = down(w, (m, g1, g3), (0, 1, 3), None, jnp.float32)
    g2, total = together(g2, total)
    return hidden, down(w, (g2,), (2,), total, jnp.bfloat16)


def solution(mesh):
    placed = (P(("dp", "row"), "col"), P("row", "col"), P(("dp", "row"), "col"))
    return jax.shard_map(
        body,
        mesh=mesh,
        in_specs=placed,
        out_specs=(P(("dp", "row"), "col"), P(("dp", "col"), "row")),
        check_vma=False,
    )
```

time: 436 us -> 140 us (0.32)
  waiting for transfers between devices: 352 us -> 74.3 us
  matrix products: 20.9 us -> 0 us
  Pallas kernels: 0 us -> 18.5 us
  other arithmetic: 13.1 us -> 1.5 us
  starting transfers between devices: 45 us -> 34 us
  local copies, waits for them, and re-layouts: 1.45 us -> 9.89 us
    ppermute x24 -> x25, waiting for transfers between devices: 352 us -> 74.3 us  [the longest x6 44.3 us: z_step(): lax.ppermute(x, ('dp', 'col'), flat(sizes, lambda i, c: (i // n * n + (i...]
    dot_general x8 -> x0, matrix products: 20.9 us -> none  [the longest x4 10.7 us: body(): pre = pre + jnp.dot(x_cur, w_cur, preferred_element_type=jnp.float32)]
    pallas_call x0 -> x6, Pallas kernels: none -> 18.5 us  [the longest x2 7.04 us: down(): pl.pallas_call(functools.partial(down_kernel, plan), out_shape=jax.ShapeD...]
    select_n x9 -> x0, other arithmetic: 13.1 us -> none  [the longest x7 13 us: skewed(): block = jnp.where(index >> level & 1 == 1, moved, block)]
    ppermute x24 -> x25, starting transfers between devices: 45 us -> 34 us  [the longest x9 12.5 us: col_swap(): return lax.ppermute(x, 'col', [(i, i ^ m) for i in range(n)])]
    slice x0 -> x3, local copies, waits for them, and re-layouts: none -> 4.58 us  [the longest x1 2.21 us: body(): tokens[h:]]
  transfers between devices with their start and end apart: 24 -> 25, of which waited for: 19 -> 14; matrix products, arithmetic and copies ran while one was open for 6% -> 8% of each run, Pallas kernels for 0% -> 8%
where the time goes in v2:
time: 140 us; the launch traced here: 139 us
  waiting for transfers between devices  74.3 us (53%)
  starting transfers between devices  34 us (24%)
  Pallas kernels  18.5 us (13%)
  local copies, waits for them, and re-layouts  9.89 us (7%)
  other arithmetic  1.5 us (1%)
    ppermute x6, waiting for transfers between devices, z_step(): lax.ppermute(x, ('dp', 'col'), flat(sizes, lambda i, c: (i // n * n + (i...  44.3 us
    ppermute x8, waiting for transfers between devices, y_step(): lax.ppermute(x, ('row', 'col'), flat(sizes, lambda r, c: ((r + 1 - 2 * ((...  21.4 us
    ppermute x9, starting transfers between devices, col_swap(): return lax.ppermute(x, 'col', [(i, i ^ m) for i in range(n)])  12.5 us
    ppermute x6, starting transfers between devices, z_step(): lax.ppermute(x, ('dp', 'col'), flat(sizes, lambda i, c: (i // n * n + (i...  11.3 us
    ppermute x9, waiting for transfers between devices, col_swap(): return lax.ppermute(x, 'col', [(i, i ^ m) for i in range(n)])  7.1 us
    pallas_call x2, Pallas kernels, down(): pl.pallas_call(functools.partial(down_kernel, plan), out_shape=jax.ShapeD...  7.04 us
    ppermute x8, starting transfers between devices, y_step(): lax.ppermute(x, ('row', 'col'), flat(sizes, lambda r, c: ((r + 1 - 2 * ((...  6.53 us
    pallas_call x1, Pallas kernels, up_part(): pl.pallas_call(up_part_kernel, out_shape=jax.ShapeDtypeStruct((rows, widt...  5.25 us
  transfers between devices with their start and end apart: 25, of which 14 were waited for; matrix products, arithmetic and copies ran while one was open for 8% of the time, Pallas kernels for 8%

profile of v2, /device:TPU:4, one launch (start us, length us, event | category | flops | bytes accessed | tf_op | source)
XLA Modules:
  0.0 139.0 jit_solution(17824929484681126158)
XLA Ops:
  0.6 0.1 collective-permute-start.4
  0.7 1.2 slice.9
  2.0 2.3 %collective-permute-start.3 = (bf16[192,1536]{1,0:T(8,128)(2,1)S(1)}, bf16[192,1536]{1,0:T(8,128)(2,1)S(1)}, u32[]{:S(2)}, u32[]{:S(2)}) collective-permute-start(bf16[192,1536]{1,0:T(8,128)(2,1)S(1)} %slice.9), channel_id=1, source_target_pairs={{0,2},{1,3},{2,0},{3,1},{4,6},{5,7},{6,4},{7,5},{8,10},{9,11},{10,... | collective-permute-start | bytes 1769480 | tf_op jit(solution)/shard_map/ppermute | solution.py:53
  4.3 1.7 %constant_dynamic-slice_fusion = bf16[384,384]{1,0:T(8,128)(2,1)} fusion(bf16[1536,768]{1,0:T(8,128)(2,1)} %own.1, s32[]{:T(128)S(6)} %select_n.12), kind=kLoop, calls=%fused_computation.2 | loop fusion | bytes 589828 | tf_op jit(solution)/shard_map/dynamic_slice | solution.py:259
  6.0 1.3 collective-permute-start.2
  7.3 0.6 collective-permute-start.1
  7.9 1.0 collective-permute-start
  8.9 2.2 %slice.11 = bf16[320,1536]{1,0:T(8,128)(2,1)} slice(bf16[512,1536]{1,0:T(8,128)(2,1)} %t0.1), slice={[192:512], [0:1536]} | slice | bytes 1966080 | tf_op jit(solution)/shard_map/slice | solution.py:264
  11.1 1.1 slice.10
  12.2 2.5 %copy.5 = bf16[1536,768]{0,1:T(8,128)(2,1)} copy(bf16[1536,768]{1,0:T(8,128)(2,1)S(1)} %copy-done) | data formatting | bytes 4718592 | tf_op args[1]
  14.7 4.3 %collective-permute-done.2 = bf16[384,384]{1,0:T(8,128)(2,1)} collective-permute-done((bf16[384,384]{1,0:T(8,128)(2,1)}, bf16[384,384]{1,0:T(8,128)(2,1)}, u32[]{:S(2)}, u32[]{:S(2)}) %collective-permute-start.2) | collective-permute-done | bytes 294944 | tf_op jit(solution)/shard_map/ppermute | solution.py:30
  19.0 0.2 collective-permute-done.1
  19.2 3.7 %collective-permute-done = bf16[384,384]{1,0:T(8,128)(2,1)} collective-permute-done((bf16[384,384]{1,0:T(8,128)(2,1)}, bf16[384,384]{1,0:T(8,128)(2,1)}, u32[]{:S(2)}, u32[]{:S(2)}) %collective-permute-start) | collective-permute-done | bytes 294944 | tf_op jit(solution)/shard_map/ppermute | solution.py:30
  22.9 1.3 pad_maximum_fusion.1.p0
  24.1 1.6 %collective-permute-start.8 = (bf16[1536,384]{1,0:T(8,128)(2,1)}, bf16[1536,384]{1,0:T(8,128)(2,1)S(1)}, u32[]{:S(2)}, u32[]{:S(2)}) collective-permute-start(bf16[1536,384]{1,0:T(8,128)(2,1)} %slice.10), channel_id=1, source_target_pairs={{0,12},{1,5},{2,14},{3,7},{4,0},{5,9},{6,2},{7,11},{8,4},{9,13},{1... | collective-permute-start | bytes 3538952 | tf_op jit(solution)/shard_map/ppermute | solution.py:30
  25.7 0.5 collective-permute-start.7
  26.2 2.5 %collective-permute-start.9 = (bf16[320,1536]{1,0:T(8,128)(2,1)}, bf16[320,1536]{1,0:T(8,128)(2,1)S(1)}, u32[]{:S(2)}, u32[]{:S(2)}) collective-permute-start(bf16[320,1536]{1,0:T(8,128)(2,1)} %slice.11), channel_id=1, source_target_pairs={{0,2},{1,3},{2,0},{3,1},{4,6},{5,7},{6,4},{7,5},{8,10},{9,11},{10,... | collective-permute-start | bytes 2949128 | tf_op jit(solution)/shard_map/ppermute | solution.py:53
  28.8 5.9 %collective-permute-start.6 = (bf16[3,384,384]{2,1,0:T(8,128)(2,1)S(1)}, bf16[3,384,384]{2,1,0:T(8,128)(2,1)S(1)}, u32[]{:S(2)}, u32[]{:S(2)}) collective-permute-start(bf16[3,384,384]{2,1,0:T(8,128)(2,1)S(1)} %pad_maximum_fusion.1.p0), channel_id=1, source_target_pairs={{0,112},{1,17},{2,114},{3,19},{16,0},{17,33},{18,2},{19,35},{32,16... | collective-permute-start | bytes 2654216 | tf_op jit(solution)/shard_map/ppermute | solution.py:41
  34.6 1.1 constant_dynamic-slice_fusion.1
  35.8 17.6 %collective-permute-done.6.p3 = bf16[3,384,384]{2,1,0:T(8,128)(2,1)S(1)} collective-permute-done((bf16[3,384,384]{2,1,0:T(8,128)(2,1)S(1)}, bf16[3,384,384]{2,1,0:T(8,128)(2,1)S(1)}, u32[]{:S(2)}, u32[]{:S(2)}) %collective-permute-start.6) | collective-permute-done | bytes 884768 | tf_op jit(solution)/shard_map/ppermute | solution.py:41
  53.4 0.7 collective-permute-done.5.p1
  54.1 0.1 collective-permute-start.11
  54.2 0.1 collective-permute-start.13
  54.3 1.8 %collective-permute-start.10 = (bf16[192,1536]{1,0:T(8,128)(2,1)S(1)}, bf16[192,1536]{1,0:T(8,128)(2,1)S(1)}, u32[]{:S(2)}, u32[]{:S(2)}) collective-permute-start(bf16[192,1536]{1,0:T(8,128)(2,1)S(1)} %collective-permute-done.3.t2a), channel_id=1, source_target_pairs={{0,1},{1,0},{2,3},{3,2},{4,5},{5,4},{6,7},{7,6},{8,9},{9,8},{10,11... | collective-permute-start | bytes 1769480 | tf_op jit(solution)/shard_map/ppermute | solution.py:53
  56.1 1.3 collective-permute-start.12
  57.4 3.0 %collective-permute-start.14 = (bf16[768,384]{1,0:T(8,128)(2,1)S(1)}, bf16[768,384]{1,0:T(8,128)(2,1)S(1)}, u32[]{:S(2)}, u32[]{:S(2)}) collective-permute-start(bf16[768,384]{1,0:T(8,128)(2,1)S(1)} %constant_dynamic-slice_fusion.1), channel_id=1, source_target_pairs={{0,2},{1,3},{2,0},{3,1},{4,6},{5,7},{6,4},{7,5},{8,10},{9,11},{10,... | collective-permute-start | bytes 1769480 | tf_op jit(solution)/shard_map/ppermute | solution.py:53
  60.5 1.5 %sort_tokens.1.t = bf16[4,512,1536]{2,1,0:T(8,128)(2,1)S(1)} custom-call(bf16[512,1536]{1,0:T(8,128)(2,1)S(1)} %copy-done.2, bf16[512,1536]{1,0:T(8,128)(2,1)} %collective-permute-done.4.t1, bf16[192,1536]{1,0:T(8,128)(2,1)S(1)} %collective-permute-done.3.t2a, bf16[320,1536]{1,0:T(8,128)(2,1)S(1)} %collective-permute-done.9.t2b, ...), custom_call_target="tpu_custom_call" | custom-call | bytes 12582912 | tf_op jit(solution)/shard_map/sort_tokens/pallas_call | solution.py:113
  62.0 5.2 %up_part.1.so_far = f32[512,768]{1,0:T(8,128)S(1)} custom-call(bf16[4,512,1536]{2,1,0:T(8,128)(2,1)S(1)} %sort_tokens.1.t, bf16[1536,768]{1,0:T(8,128)(2,1)S(1)} %copy-done, bf16[1536,384]{1,0:T(8,128)(2,1)S(1)} %collective-permute-done.7.w1, bf16[1536,384]{1,0:T(8,128)(2,1)S(1)} %collective-permute-done.8.w3, ...), custom_call_target="tpu_custom_call" | custom-call | flops 3623878656 | bytes 11796480 | tf_op jit(solution)/shard_map/up_part/pallas_call | solution.py:165
  67.3 5.1 %collective-permute-done.14.x0 = bf16[768,384]{1,0:T(8,128)(2,1)S(1)} collective-permute-done((bf16[768,384]{1,0:T(8,128)(2,1)S(1)}, bf16[768,384]{1,0:T(8,128)(2,1)S(1)}, u32[]{:S(2)}, u32[]{:S(2)}) %collective-permute-start.14) | collective-permute-done | bytes 589856 | tf_op jit(solution)/shard_map/ppermute | solution.py:53
  72.4 3.8 %up_rest.1 = (bf16[512,768]{1,0:T(8,128)(2,1)}, bf16[512,768]{1,0:T(8,128)(2,1)S(1)}) custom-call(bf16[4,512,1536]{2,1,0:T(8,128)(2,1)S(1)} %sort_tokens.1.t, f32[512,768]{1,0:T(8,128)S(1)} %up_part.1.so_far, bf16[1536,384]{1,0:T(8,128)(2,1)S(1)} %collective-permute-done.13.w2, bf16[3,384,384]{2,1,0:T(8,128)(2,1)S(1)} %collective-permute-done.12.p2, ...), custom_call_target="tpu_custom_call" | custom-call | flops 1207959552 | bytes 3932160 | tf_op jit(solution)/shard_map/up_rest/pallas_call | solution.py:179
  76.2 2.6 %collective-permute-start.18 = (bf16[768,1536]{1,0:T(8,128)(2,1)S(1)}, bf16[768,1536]{1,0:T(8,128)(2,1)S(1)}, u32[]{:S(2)}, u32[]{:S(2)}) collective-permute-start(bf16[768,1536]{1,0:T(8,128)(2,1)S(1)} %bitcast.8), channel_id=1, source_target_pairs={{0,1},{1,0},{2,3},{3,2},{4,5},{5,4},{6,7},{7,6},{8,9},{9,8},{10,11... | collective-permute-start | bytes 7077896 | tf_op jit(solution)/shard_map/ppermute | solution.py:53
  78.8 3.0 %collective-permute-start.15 = (bf16[512,768]{1,0:T(8,128)(2,1)S(1)}, bf16[512,768]{1,0:T(8,128)(2,1)S(1)}, u32[]{:S(2)}, u32[]{:S(2)}) collective-permute-start(bf16[512,768]{1,0:T(8,128)(2,1)S(1)} %get-tuple-element.53), channel_id=1, source_target_pairs={{0,12},{1,4},{2,0},{3,8},{4,1},{5,9},{6,5},{7,13},{8,10},{9,2},{10... | collective-permute-start | bytes 2359304 | tf_op jit(solution)/shard_map/ppermute | solution.py:66
  81.8 3.9 %collective-permute-start.17 = (bf16[768,384]{1,0:T(8,128)(2,1)S(1)}, bf16[768,384]{1,0:T(8,128)(2,1)S(1)}, u32[]{:S(2)}, u32[]{:S(2)}) collective-permute-start(bf16[768,384]{1,0:T(8,128)(2,1)S(1)} %collective-permute-done.14.x0), channel_id=1, source_target_pairs={{0,112},{1,17},{2,114},{3,19},{16,0},{17,33},{18,2},{19,35},{32,16... | collective-permute-start | bytes 1769480 | tf_op jit(solution)/shard_map/ppermute | solution.py:41
  85.7 13.6 %collective-permute-done.17.x3 = bf16[768,384]{1,0:T(8,128)(2,1)S(1)} collective-permute-done((bf16[768,384]{1,0:T(8,128)(2,1)S(1)}, bf16[768,384]{1,0:T(8,128)(2,1)S(1)}, u32[]{:S(2)}, u32[]{:S(2)}) %collective-permute-start.17) | collective-permute-done | bytes 589856 | tf_op jit(solution)/shard_map/ppermute | solution.py:41
  99.3 0.7 collective-permute-done.16.x1
  100.0 1.3 collective-permute-done.15.rest_0_
  101.4 0.2 pad_maximum_fusion
  101.6 0.1 collective-permute-start.22
  101.8 2.0 %collective-permute-start.19 = (bf16[512,768]{1,0:T(8,128)(2,1)S(1)}, bf16[512,768]{1,0:T(8,128)(2,1)S(1)}, u32[]{:S(2)}, u32[]{:S(2)}) collective-permute-start(bf16[512,768]{1,0:T(8,128)(2,1)S(1)} %collective-permute-done.15.rest_0_), channel_id=1, source_target_pairs={{0,4},{1,13},{2,6},{3,15},{4,8},{5,1},{6,10},{7,3},{8,12},{9,5},{1... | collective-permute-start | bytes 2359304 | tf_op jit(solution)/shard_map/ppermute | solution.py:30
  103.8 0.2 collective-permute-start.21
  104.0 11.6 %collective-permute-done.21.x2 = bf16[768,384]{1,0:T(8,128)(2,1)S(1)} collective-permute-done((bf16[768,384]{1,0:T(8,128)(2,1)S(1)}, bf16[768,384]{1,0:T(8,128)(2,1)S(1)}, u32[]{:S(2)}, u32[]{:S(2)}) %collective-permute-start.21) | collective-permute-done | bytes 589856 | tf_op jit(solution)/shard_map/ppermute | solution.py:41
  115.6 6.0 %collective-permute-done.20.rest_2_ = bf16[512,768]{1,0:T(8,128)(2,1)S(1)} collective-permute-done((bf16[512,768]{1,0:T(8,128)(2,1)S(1)}, bf16[512,768]{1,0:T(8,128)(2,1)S(1)}, u32[]{:S(2)}, u32[]{:S(2)}) %collective-permute-start.20) | collective-permute-done | bytes 786464 | tf_op jit(solution)/shard_map/ppermute | solution.py:30
  121.7 1.2 collective-permute-done.19.rest_1_
  122.9 2.0 %collective-permute-done.23.y2 = bf16[768,384]{1,0:T(8,128)(2,1)S(1)} collective-permute-done((bf16[768,384]{1,0:T(8,128)(2,1)S(1)}, bf16[768,384]{1,0:T(8,128)(2,1)S(1)}, u32[]{:S(2)}, u32[]{:S(2)}) %collective-permute-start.23) | collective-permute-done | bytes 589856 | tf_op jit(solution)/shard_map/ppermute | solution.py:53
  124.9 0.8 sort_w.1.w
  125.7 4.2 %down.2.rest_1_ = f32[512,1536]{1,0:T(8,128)S(1)} custom-call(bf16[4,768,1536]{2,1,0:T(8,128)(2,1)S(1)} %sort_w.1.w, bf16[512,768]{1,0:T(8,128)(2,1)S(1)} %collective-permute-done.15.rest_0_, bf16[512,768]{1,0:T(8,128)(2,1)S(1)} %collective-permute-done.19.rest_1_, bf16[512,768]{1,0:T(8,128)(2,1)S(1)} %collective-permute-done.20.rest_2_), custom_call_target="tpu_custom_call" | custom-call | flops 3623878656 | bytes 12582912 | tf_op jit(solution)/shard_map/down/pallas_call | solution.py:238
  129.9 6.2 %collective-permute-done.24.rest_0_ = bf16[512,768]{1,0:T(8,128)(2,1)S(1)} collective-permute-done((bf16[512,768]{1,0:T(8,128)(2,1)S(1)}, bf16[512,768]{1,0:T(8,128)(2,1)S(1)}, u32[]{:S(2)}, u32[]{:S(2)}) %collective-permute-start.24) | collective-permute-done | bytes 786464 | tf_op jit(solution)/shard_map/ppermute | solution.py:30
  136.1 2.9 %down.3 = bf16[512,1536]{1,0:T(8,128)(2,1)} custom-call(bf16[4,768,1536]{2,1,0:T(8,128)(2,1)S(1)} %sort_w.1.w, bf16[512,768]{1,0:T(8,128)(2,1)S(1)} %collective-permute-done.24.rest_0_, f32[512,1536]{1,0:T(8,128)S(1)} %down.2.rest_1_), custom_call_target="tpu_custom_call" | custom-call | flops 1207959552 | bytes 12582912 | tf_op jit(solution)/shard_map/down/pallas_call | solution.py:238
  (24 shorter events, 0.1 us)
Async XLA Ops:
  0.6 10.5 %copy-start = (bf16[1536,768]{1,0:T(8,128)(2,1)S(1)}, bf16[1536,768]{1,0:T(8,128)(2,1)}, u32[]{:S(2)}) copy-start(bf16[1536,768]{1,0:T(8,128)(2,1)} %own.1) | copy-start | bytes 7077892
  0.6 23.5 %collective-permute-start.4 = (bf16[512,1536]{1,0:T(8,128)(2,1)}, bf16[512,1536]{1,0:T(8,128)(2,1)}, u32[]{:S(2)}, u32[]{:S(2)}) collective-permute-start(bf16[512,1536]{1,0:T(8,128)(2,1)} %t0.1), channel_id=1, source_target_pairs={{0,1},{1,0},{2,3},{3,2},{4,5},{5,4},{6,7},{7,6},{8,9},{9,8},{10,11... | collective-permute-start | bytes 4718600 | tf_op jit(solution)/shard_map/ppermute | solution.py:53
  2.0 22.1 %collective-permute-start.3 = (bf16[192,1536]{1,0:T(8,128)(2,1)S(1)}, bf16[192,1536]{1,0:T(8,128)(2,1)S(1)}, u32[]{:S(2)}, u32[]{:S(2)}) collective-permute-start(bf16[192,1536]{1,0:T(8,128)(2,1)S(1)} %slice.9), channel_id=1, source_target_pairs={{0,2},{1,3},{2,0},{3,1},{4,6},{5,7},{6,4},{7,5},{8,10},{9,11},{10,... | collective-permute-start | bytes 1769480 | tf_op jit(solution)/shard_map/ppermute | solution.py:53
  6.0 13.0 %collective-permute-start.2 = (bf16[384,384]{1,0:T(8,128)(2,1)}, bf16[384,384]{1,0:T(8,128)(2,1)}, u32[]{:S(2)}, u32[]{:S(2)}) collective-permute-start(bf16[384,384]{1,0:T(8,128)(2,1)} %constant_dynamic-slice_fusion), channel_id=1, source_target_pairs={{0,12},{1,5},{2,14},{3,7},{4,0},{5,9},{6,2},{7,11},{8,4},{9,13},{1... | collective-permute-start | bytes 884744 | tf_op jit(solution)/shard_map/ppermute | solution.py:30
  7.3 11.9 %collective-permute-start.1 = (bf16[384,384]{1,0:T(8,128)(2,1)}, bf16[384,384]{1,0:T(8,128)(2,1)}, u32[]{:S(2)}, u32[]{:S(2)}) collective-permute-start(bf16[384,384]{1,0:T(8,128)(2,1)} %constant_dynamic-slice_fusion), channel_id=1, source_target_pairs={{0,8},{4,12},{8,0},{12,4},{1,9},{5,13},{9,1},{13,5},{2,10},{6,14},... | collective-permute-start | bytes 884744 | tf_op jit(solution)/shard_map/ppermute | solution.py:48
  7.9 14.9 %collective-permute-start = (bf16[384,384]{1,0:T(8,128)(2,1)}, bf16[384,384]{1,0:T(8,128)(2,1)}, u32[]{:S(2)}, u32[]{:S(2)}) collective-permute-start(bf16[384,384]{1,0:T(8,128)(2,1)} %constant_dynamic-slice_fusion), channel_id=1, source_target_pairs={{0,4},{1,13},{2,6},{3,15},{4,8},{5,1},{6,10},{7,3},{8,12},{9,5},{1... | collective-permute-start | bytes 884744 | tf_op jit(solution)/shard_map/ppermute | solution.py:30
  14.7 45.8 %copy-start.2 = (bf16[512,1536]{1,0:T(8,128)(2,1)S(1)}, bf16[512,1536]{1,0:T(8,128)(2,1)}, u32[]{:S(2)}) copy-start(bf16[512,1536]{1,0:T(8,128)(2,1)} %t0.1) | copy-start | bytes 4718596
  24.1 30.0 %collective-permute-start.8 = (bf16[1536,384]{1,0:T(8,128)(2,1)}, bf16[1536,384]{1,0:T(8,128)(2,1)S(1)}, u32[]{:S(2)}, u32[]{:S(2)}) collective-permute-start(bf16[1536,384]{1,0:T(8,128)(2,1)} %slice.10), channel_id=1, source_target_pairs={{0,12},{1,5},{2,14},{3,7},{4,0},{5,9},{6,2},{7,11},{8,4},{9,13},{1... | collective-permute-start | bytes 3538952 | tf_op jit(solution)/shard_map/ppermute | solution.py:30
  25.7 28.4 %collective-permute-start.7 = (bf16[1536,384]{1,0:T(8,128)(2,1)}, bf16[1536,384]{1,0:T(8,128)(2,1)S(1)}, u32[]{:S(2)}, u32[]{:S(2)}) collective-permute-start(bf16[1536,384]{1,0:T(8,128)(2,1)} %slice.10), channel_id=1, source_target_pairs={{0,4},{1,13},{2,6},{3,15},{4,8},{5,1},{6,10},{7,3},{8,12},{9,5},{1... | collective-permute-start | bytes 3538952 | tf_op jit(solution)/shard_map/ppermute | solution.py:30
  26.2 27.9 %collective-permute-start.9 = (bf16[320,1536]{1,0:T(8,128)(2,1)}, bf16[320,1536]{1,0:T(8,128)(2,1)S(1)}, u32[]{:S(2)}, u32[]{:S(2)}) collective-permute-start(bf16[320,1536]{1,0:T(8,128)(2,1)} %slice.11), channel_id=1, source_target_pairs={{0,2},{1,3},{2,0},{3,1},{4,6},{5,7},{6,4},{7,5},{8,10},{9,11},{10,... | collective-permute-start | bytes 2949128 | tf_op jit(solution)/shard_map/ppermute | solution.py:53
  28.8 24.6 %collective-permute-start.6 = (bf16[3,384,384]{2,1,0:T(8,128)(2,1)S(1)}, bf16[3,384,384]{2,1,0:T(8,128)(2,1)S(1)}, u32[]{:S(2)}, u32[]{:S(2)}) collective-permute-start(bf16[3,384,384]{2,1,0:T(8,128)(2,1)S(1)} %pad_maximum_fusion.1.p0), channel_id=1, source_target_pairs={{0,112},{1,17},{2,114},{3,19},{16,0},{17,33},{18,2},{19,35},{32,16... | collective-permute-start | bytes 2654216 | tf_op jit(solution)/shard_map/ppermute | solution.py:41
  34.6 19.5 %collective-permute-start.5 = (bf16[3,384,384]{2,1,0:T(8,128)(2,1)S(1)}, bf16[3,384,384]{2,1,0:T(8,128)(2,1)S(1)}, u32[]{:S(2)}, u32[]{:S(2)}) collective-permute-start(bf16[3,384,384]{2,1,0:T(8,128)(2,1)S(1)} %pad_maximum_fusion.1.p0), channel_id=1, source_target_pairs={{0,16},{1,113},{2,18},{3,115},{16,32},{17,1},{18,34},{19,3},{32,48... | collective-permute-start | bytes 2654216 | tf_op jit(solution)/shard_map/ppermute | solution.py:41
  54.1 6.3 %collective-permute-start.11 = (bf16[320,1536]{1,0:T(8,128)(2,1)S(1)}, bf16[320,1536]{1,0:T(8,128)(2,1)S(1)}, u32[]{:S(2)}, u32[]{:S(2)}) collective-permute-start(bf16[320,1536]{1,0:T(8,128)(2,1)S(1)} %collective-permute-done.9.t2b), channel_id=1, source_target_pairs={{0,1},{1,0},{2,3},{3,2},{4,5},{5,4},{6,7},{7,6},{8,9},{9,8},{10,11... | collective-permute-start | bytes 2949128 | tf_op jit(solution)/shard_map/ppermute | solution.py:53
  54.2 18.2 %collective-permute-start.13 = (bf16[1536,384]{1,0:T(8,128)(2,1)S(1)}, bf16[1536,384]{1,0:T(8,128)(2,1)S(1)}, u32[]{:S(2)}, u32[]{:S(2)}) collective-permute-start(bf16[1536,384]{1,0:T(8,128)(2,1)S(1)} %collective-permute-done.7.w1), channel_id=1, source_target_pairs={{0,4},{1,13},{2,6},{3,15},{4,8},{5,1},{6,10},{7,3},{8,12},{9,5},{1... | collective-permute-start | bytes 3538952 | tf_op jit(solution)/shard_map/ppermute | solution.py:30
  54.3 6.1 %collective-permute-start.10 = (bf16[192,1536]{1,0:T(8,128)(2,1)S(1)}, bf16[192,1536]{1,0:T(8,128)(2,1)S(1)}, u32[]{:S(2)}, u32[]{:S(2)}) collective-permute-start(bf16[192,1536]{1,0:T(8,128)(2,1)S(1)} %collective-permute-done.3.t2a), channel_id=1, source_target_pairs={{0,1},{1,0},{2,3},{3,2},{4,5},{5,4},{6,7},{7,6},{8,9},{9,8},{10,11... | collective-permute-start | bytes 1769480 | tf_op jit(solution)/shard_map/ppermute | solution.py:53
  56.1 16.3 %collective-permute-start.12 = (bf16[3,384,384]{2,1,0:T(8,128)(2,1)S(1)}, bf16[3,384,384]{2,1,0:T(8,128)(2,1)S(1)}, u32[]{:S(2)}, u32[]{:S(2)}) collective-permute-start(bf16[3,384,384]{2,1,0:T(8,128)(2,1)S(1)} %collective-permute-done.5.p1), channel_id=1, source_target_pairs={{0,16},{1,113},{2,18},{3,115},{16,32},{17,1},{18,34},{19,3},{32,48... | collective-permute-start | bytes 2654216 | tf_op jit(solution)/shard_map/ppermute | solution.py:41
  57.4 14.9 %collective-permute-start.14 = (bf16[768,384]{1,0:T(8,128)(2,1)S(1)}, bf16[768,384]{1,0:T(8,128)(2,1)S(1)}, u32[]{:S(2)}, u32[]{:S(2)}) collective-permute-start(bf16[768,384]{1,0:T(8,128)(2,1)S(1)} %constant_dynamic-slice_fusion.1), channel_id=1, source_target_pairs={{0,2},{1,3},{2,0},{3,1},{4,6},{5,7},{6,4},{7,5},{8,10},{9,11},{10,... | collective-permute-start | bytes 1769480 | tf_op jit(solution)/shard_map/ppermute | solution.py:53
  62.0 10.4 %copy-start.3 = (bf16[512,768]{1,0:T(8,128)(2,1)S(1)}, bf16[512,768]{1,0:T(8,128)(2,1)}, u32[]{:S(2)}) copy-start(bf16[512,768]{1,0:T(8,128)(2,1)} %cot.1) | copy-start | bytes 2359300
  67.3 8.9 %copy-start.1 = (bf16[1536,768]{0,1:T(8,128)(2,1)S(1)}, bf16[1536,768]{0,1:T(8,128)(2,1)}, u32[]{:S(2)}) copy-start(bf16[1536,768]{0,1:T(8,128)(2,1)} %copy.5) | copy-start | bytes 7077892
  76.2 25.2 %collective-permute-start.18 = (bf16[768,1536]{1,0:T(8,128)(2,1)S(1)}, bf16[768,1536]{1,0:T(8,128)(2,1)S(1)}, u32[]{:S(2)}, u32[]{:S(2)}) collective-permute-start(bf16[768,1536]{1,0:T(8,128)(2,1)S(1)} %bitcast.8), channel_id=1, source_target_pairs={{0,1},{1,0},{2,3},{3,2},{4,5},{5,4},{6,7},{7,6},{8,9},{9,8},{10,11... | collective-permute-start | bytes 7077896 | tf_op jit(solution)/shard_map/ppermute | solution.py:53
  78.8 22.6 %collective-permute-start.15 = (bf16[512,768]{1,0:T(8,128)(2,1)S(1)}, bf16[512,768]{1,0:T(8,128)(2,1)S(1)}, u32[]{:S(2)}, u32[]{:S(2)}) collective-permute-start(bf16[512,768]{1,0:T(8,128)(2,1)S(1)} %get-tuple-element.53), channel_id=1, source_target_pairs={{0,12},{1,4},{2,0},{3,8},{4,1},{5,9},{6,5},{7,13},{8,10},{9,2},{10... | collective-permute-start | bytes 2359304 | tf_op jit(solution)/shard_map/ppermute | solution.py:66
  81.8 17.5 %collective-permute-start.17 = (bf16[768,384]{1,0:T(8,128)(2,1)S(1)}, bf16[768,384]{1,0:T(8,128)(2,1)S(1)}, u32[]{:S(2)}, u32[]{:S(2)}) collective-permute-start(bf16[768,384]{1,0:T(8,128)(2,1)S(1)} %collective-permute-done.14.x0), channel_id=1, source_target_pairs={{0,112},{1,17},{2,114},{3,19},{16,0},{17,33},{18,2},{19,35},{32,16... | collective-permute-start | bytes 1769480 | tf_op jit(solution)/shard_map/ppermute | solution.py:41
  85.7 14.4 %collective-permute-start.16 = (bf16[768,384]{1,0:T(8,128)(2,1)S(1)}, bf16[768,384]{1,0:T(8,128)(2,1)S(1)}, u32[]{:S(2)}, u32[]{:S(2)}) collective-permute-start(bf16[768,384]{1,0:T(8,128)(2,1)S(1)} %collective-permute-done.14.x0), channel_id=1, source_target_pairs={{0,16},{1,113},{2,18},{3,115},{16,32},{17,1},{18,34},{19,3},{32,48... | collective-permute-start | bytes 1769480 | tf_op jit(solution)/shard_map/ppermute | solution.py:41
  101.6 21.3 %collective-permute-start.22 = (bf16[3,768,384]{2,1,0:T(8,128)(2,1)S(1)}, bf16[3,768,384]{2,1,0:T(8,128)(2,1)S(1)}, u32[]{:S(2)}, u32[]{:S(2)}) collective-permute-start(bf16[3,768,384]{2,1,0:T(8,128)(2,1)S(1)} %pad_maximum_fusion), channel_id=1, source_target_pairs={{0,1},{1,0},{2,3},{3,2},{4,5},{5,4},{6,7},{7,6},{8,9},{9,8},{10,11... | collective-permute-start | bytes 5308424 | tf_op jit(solution)/shard_map/ppermute | solution.py:53
  101.7 20.0 %collective-permute-start.20 = (bf16[512,768]{1,0:T(8,128)(2,1)S(1)}, bf16[512,768]{1,0:T(8,128)(2,1)S(1)}, u32[]{:S(2)}, u32[]{:S(2)}) collective-permute-start(bf16[512,768]{1,0:T(8,128)(2,1)S(1)} %collective-permute-done.15.rest_0_), channel_id=1, source_target_pairs={{0,12},{1,5},{2,14},{3,7},{4,0},{5,9},{6,2},{7,11},{8,4},{9,13},{1... | collective-permute-start | bytes 2359304 | tf_op jit(solution)/shard_map/ppermute | solution.py:30
  101.8 21.1 %collective-permute-start.19 = (bf16[512,768]{1,0:T(8,128)(2,1)S(1)}, bf16[512,768]{1,0:T(8,128)(2,1)S(1)}, u32[]{:S(2)}, u32[]{:S(2)}) collective-permute-start(bf16[512,768]{1,0:T(8,128)(2,1)S(1)} %collective-permute-done.15.rest_0_), channel_id=1, source_target_pairs={{0,4},{1,13},{2,6},{3,15},{4,8},{5,1},{6,10},{7,3},{8,12},{9,5},{1... | collective-permute-start | bytes 2359304 | tf_op jit(solution)/shard_map/ppermute | solution.py:30
  103.8 11.8 %collective-permute-start.21 = (bf16[768,384]{1,0:T(8,128)(2,1)S(1)}, bf16[768,384]{1,0:T(8,128)(2,1)S(1)}, u32[]{:S(2)}, u32[]{:S(2)}) collective-permute-start(bf16[768,384]{1,0:T(8,128)(2,1)S(1)} %collective-permute-done.16.x1), channel_id=1, source_target_pairs={{0,16},{1,113},{2,18},{3,115},{16,32},{17,1},{18,34},{19,3},{32,48... | collective-permute-start | bytes 1769480 | tf_op jit(solution)/shard_map/ppermute | solution.py:41
  122.9 2.0 %collective-permute-start.23 = (bf16[768,384]{1,0:T(8,128)(2,1)S(1)}, bf16[768,384]{1,0:T(8,128)(2,1)S(1)}, u32[]{:S(2)}, u32[]{:S(2)}) collective-permute-start(bf16[768,384]{1,0:T(8,128)(2,1)S(1)} %collective-permute-done.21.x2), channel_id=1, source_target_pairs={{0,1},{1,0},{2,3},{3,2},{4,5},{5,4},{6,7},{7,6},{8,9},{9,8},{10,11... | collective-permute-start | bytes 1769480 | tf_op jit(solution)/shard_map/ppermute | solution.py:53
  122.9 13.2 %collective-permute-start.24 = (bf16[512,768]{1,0:T(8,128)(2,1)S(1)}, bf16[512,768]{1,0:T(8,128)(2,1)S(1)}, u32[]{:S(2)}, u32[]{:S(2)}) collective-permute-start(bf16[512,768]{1,0:T(8,128)(2,1)S(1)} %collective-permute-done.19.rest_1_), channel_id=1, source_target_pairs={{0,4},{1,13},{2,6},{3,15},{4,8},{5,1},{6,10},{7,3},{8,12},{9,5},{1... | collective-permute-start | bytes 2359304 | tf_op jit(solution)/shard_map/ppermute | solution.py:30

commit v3 on v2

--- a/solution.py
+++ b/solution.py
@@ -97,14 +97,10 @@
     return jnp.dot(a, b, preferred_element_type=jnp.float32)
 
 
-def sort_tokens_kernel(t0, t1, t2a, t2b, t3a, t3b, out, sem):
+def sort_tokens_kernel(t0, t1, t2, t3, out, sem):
     c = lax.axis_index("col")
-    h = t2a.shape[0]
-    pltpu.make_async_copy(t0, out.at[c], sem).start()
-    pltpu.make_async_copy(t1, out.at[c ^ 1], sem).start()
-    for m, top, rest in ((2, t2a, t2b), (3, t3a, t3b)):
-        pltpu.make_async_copy(top, out.at[c ^ m, pl.ds(0, h)], sem).start()
-        pltpu.make_async_copy(rest, out.at[c ^ m, pl.ds(h, rest.shape[0])], sem).start()
+    for m, src in enumerate((t0, t1, t2, t3)):
+        pltpu.make_async_copy(src, out.at[c ^ m], sem).start()
     pltpu.make_async_copy(out, out, sem).wait()
 
 
@@ -113,7 +109,7 @@
     return pl.pallas_call(
         sort_tokens_kernel,
         out_shape=jax.ShapeDtypeStruct((4, rows, depth), jnp.bfloat16),
-        in_specs=[ANY] * 6,
+        in_specs=[ANY] * 4,
         out_specs=VMEM,
         scratch_shapes=[pltpu.SemaphoreType.DMA],
         compiler_params=params(),
@@ -137,26 +133,28 @@
             acc[:, last] += mul(t[j, :, k], p[s - 1])
 
 
-def up_rest_kernel(t, so_far, w2, p2, cot, hidden, d_pre, acc):
+def up_rest_kernel(t, so_far, w2, p2, cot, hidden, d_pre, buf, sem):
     r, core = lax.axis_index("row"), lax.axis_index("col") & 1
     z = lax.axis_index("dp") & 3
     _, q, width = p2.shape
-    first, last = pl.ds(0, width), pl.ds(width, width)
-    acc[:, first] = so_far[:, first] + mul(t[away(r, 2, core)], w2[...])
     k = pl.ds(pl.multiple_of(away(z, 2, core) * q, 128), q)
-    y = so_far[:, last]
-    for s in range(1, 4):
-        y += mul(t[away(r, s, core), :, k], p2[s - 1])
-    acc[:, last] = y
-    rows = acc.shape[0]
-    tile = min(64, rows)
-
-    @pl.loop(0, rows // tile)
-    def _(i):
-        part = pl.ds(pl.multiple_of(i * tile, tile), tile)
-        h_val, slope = gelu_parts(acc[part, :])
-        hidden[part, :] = h_val.astype(hidden.dtype)
-        d_pre[part, :] = (cot[part, :].astype(jnp.float32) * slope).astype(d_pre.dtype)
+    rows = buf.shape[0]
+    tile = rows // 4
+    for i in range(4):
+        part = pl.ds(i * tile, tile)
+        first = mul(t[away(r, 2, core), part, :], w2[...])
+        last = mul(t[away(r, 1, core), part, k], p2[0])
+        last += mul(t[away(r, 2, core), part, k], p2[1])
+        last += mul(t[away(r, 3, core), part, k], p2[2])
+        for at, y in ((0, first), (width, last)):
+            cols = pl.ds(at, width)
+            h_val, slope = gelu_parts(so_far[part, cols] + y)
+            buf[part, cols] = h_val.astype(buf.dtype)
+            d_pre[part, cols] = (cot[part, cols].astype(jnp.float32) * slope).astype(d_pre.dtype)
+        pltpu.make_async_copy(buf.at[part], hidden.at[part], sem.at[i]).start()
+    for i in range(4):
+        part = pl.ds(i * tile, tile)
+        pltpu.make_async_copy(buf.at[part], hidden.at[part], sem.at[i]).wait()
 
 
 def up_part(t, own, *pieces):
@@ -180,22 +178,21 @@
         up_rest_kernel,
         out_shape=(out, out),
         in_specs=[VMEM] * 5,
-        out_specs=(VMEM, VMEM),
-        scratch_shapes=[pltpu.VMEM(cot.shape, jnp.float32)],
+        out_specs=(ANY, VMEM),
+        scratch_shapes=[pltpu.VMEM(cot.shape, jnp.bfloat16), pltpu.SemaphoreType.DMA((4,))],
         compiler_params=params(),
         cost_estimate=cost(2 * depth * cot.size, 2 * depth * sum(cot.shape), cot.size),
         name="up_rest",
     )(t, so_far, w2, p2, cot)
 
 
-def sort_w_kernel(own, pair, x0, x1, x2, x3, y013, y2, out, sem):
+def sort_w_kernel(own, pair, x0, x1, x2, x3, y0, y1, y2, y3, out, sem):
     c = lax.axis_index("col")
     z = lax.axis_index("dp") & 3
     q = x0.shape[1]
     pltpu.make_async_copy(own, out.at[c], sem).start()
     pltpu.make_async_copy(pair, out.at[c ^ 1], sem).start()
-    theirs = (y013.at[0], y013.at[1], y2, y013.at[2])
-    for m, srcs, core in ((2, (x0, x1, x2, x3), c & 1), (3, theirs, 1 - (c & 1))):
+    for m, srcs, core in ((2, (x0, x1, x2, x3), c & 1), (3, (y0, y1, y2, y3), 1 - (c & 1))):
         for u, src in enumerate(srcs):
             cols = pl.ds(pl.multiple_of(away(z, u, core) * q, 128), q)
             pltpu.make_async_copy(src, out.at[c ^ m, :, cols], sem).start()
@@ -207,7 +204,7 @@
     return pl.pallas_call(
         sort_w_kernel,
         out_shape=jax.ShapeDtypeStruct((4, ff, depth), jnp.bfloat16),
-        in_specs=[ANY] * 8,
+        in_specs=[ANY] * 10,
         out_specs=VMEM,
         scratch_shapes=[pltpu.SemaphoreType.DMA],
         compiler_params=params(),
@@ -246,6 +243,33 @@
     )(w, *blocks, *more)
 
 
+def down_last_kernel(w, g, so_far, out, buf, sem):
+    r, c = lax.axis_index("row"), lax.axis_index("col")
+    j = turned_from((r + 2) & 3, c)
+    tile = buf.shape[1] // 6
+    copies = []
+    for i in range(6):
+        cols = pl.ds(i * tile, tile)
+        buf[:, cols] = (so_far[:, cols] + mul(g[...], w[j, :, cols])).astype(buf.dtype)
+        copies.append(pltpu.make_async_copy(buf.at[:, cols], out.at[:, cols], sem.at[i]))
+        copies[-1].start()
+    for copy in copies:
+        copy.wait()
+
+
+def down_last(w, g, so_far):
+    return pl.pallas_call(
+        down_last_kernel,
+        out_shape=jax.ShapeDtypeStruct(so_far.shape, jnp.bfloat16),
+        in_specs=[VMEM] * 3,
+        out_specs=ANY,
+        scratch_shapes=[pltpu.VMEM(so_far.shape, jnp.bfloat16), pltpu.SemaphoreType.DMA((6,))],
+        compiler_params=params(),
+        cost_estimate=cost(2 * so_far.size * g.shape[1], 6 * so_far.size),
+        name="down_last",
+    )(w, g, so_far)
+
+
 def together(*xs):
     return lax.optimization_barrier(xs)
 
@@ -255,42 +279,39 @@
     width = ff // 2
     part = depth // 4
     z = lax.axis_index("dp") % 4
-    h = tokens.shape[0] // 64 * 24
     piece = lax.dynamic_slice(w_up, (z * part, width), (part, width))
     s1, s2, s3 = y_step(piece), opposite(piece), y_step(piece, 1)
-    ta = col_swap(tokens[:h], 2)
+    t_x = col_swap(tokens, 2)
     t_pair = col_swap(tokens, 1)
-    p0, ta, t_pair, w0, rest, w_t = together(
-        jnp.stack([s1, s2, s3]), ta, t_pair, w_up[:, :width], tokens[h:], w_up.T
-    )
+    s1, s2, s3, t_pair, w0, w_t = together(s1, s2, s3, t_pair, w_up[:, :width], w_up.T)
+    p0 = jnp.stack([s1, s2, s3])
     p1, p3 = z_step(p0), z_step(p0, 1)
     w1, w3 = y_step(w0), y_step(w0, 1)
-    tb = col_swap(rest, 2)
-    p1, p3, w1, w3, ta, tb, x0 = together(
-        p1, p3, w1, w3, ta, tb, lax.dynamic_slice(w_t, (0, z * part), (ff, part))
+    p0, p1, p3, w1, w3, t_x, x0 = together(
+        p0, p1, p3, w1, w3, t_x, lax.dynamic_slice(w_t, (0, z * part), (ff, part))
     )
     x0 = col_swap(x0, 2)
     p2 = z_step(p1)
     w2 = y_step(w1)
-    t = sort_tokens(tokens, t_pair, ta, tb, col_swap(ta, 1), col_swap(tb, 1))
+    t = sort_tokens(tokens, t_pair, t_x, col_swap(t_x, 1))
     so_far = up_part(t, w_up, w1, w3, p0, p1, p3)
     p2, w2, so_far, x0 = together(p2, w2, so_far, x0)
     hidden, d_pre = up_rest(t, so_far, w2, p2, cotangent)
 
-    d_pre, x0, w_t2 = together(d_pre, x0, w_t)
+    d_pre, x0 = together(d_pre, x0)
     m = mirror(d_pre)
     x1, x3 = z_step(x0), z_step(x0, 1)
-    w_pair = col_swap(w_t2, 1)
-    m, x1, x3, w_pair = together(m, x1, x3, w_pair)
+    y0 = col_swap(x0, 1)
+    m, x1, x3, y0 = together(m, x1, x3, y0)
     g1, g3 = y_step(m), y_step(m, 1)
     x2 = z_step(x1)
-    theirs = col_swap(jnp.stack([x0, x1, x3]), 1)
-    g1, g3, x2, theirs = together(g1, g3, x2, theirs)
+    y1, y3 = col_swap(x1, 1), col_swap(x3, 1)
+    g1, g3, x2, y1, y3, w_t2 = together(g1, g3, x2, y1, y3, w_t)
     g2 = y_step(g1)
-    w = sort_w(w_t, w_pair, x0, x1, x2, x3, theirs, col_swap(x2, 1))
+    w = sort_w(w_t, col_swap(w_t2, 1), x0, x1, x2, x3, y0, y1, col_swap(x2, 1), y3)
     total = down(w, (m, g1, g3), (0, 1, 3), None, jnp.float32)
     g2, total = together(g2, total)
-    return hidden, down(w, (g2,), (2,), total, jnp.bfloat16)
+    return hidden, down_last(w, g2, total)
 
 
 def solution(mesh):

time: 140 us -> 134 us (0.957)
  starting transfers between devices: 34 us -> 30.7 us
  local copies, waits for them, and re-layouts: 9.89 us -> 6.71 us
  waiting for transfers between devices: 74.3 us -> 76.7 us
    ppermute x9, waiting for transfers between devices: 7.1 us -> 15.3 us  [col_swap(): return lax.ppermute(x, 'col', [(i, i ^ m) for i in range(n)])]
    ppermute x6, waiting for transfers between devices: 44.3 us -> 37.2 us  [z_step(): lax.ppermute(x, ('dp', 'col'), flat(sizes, lambda i, c: (i // n * n + (i...]
    ppermute x9, starting transfers between devices: 12.5 us -> 6.48 us  [col_swap(): return lax.ppermute(x, 'col', [(i, i ^ m) for i in range(n)])]
    slice x2 -> x0, local copies, waits for them, and re-layouts: 3.45 us -> none  [the longest x1 2.21 us: body(): tokens[h:]]
    pallas_call x2 -> x1, Pallas kernels: 7.04 us -> 4.17 us  [down(): pl.pallas_call(functools.partial(down_kernel, plan), out_shape=jax.ShapeD...]
    pallas_call x0 -> x1, Pallas kernels: none -> 2.3 us  [down_last(): pl.pallas_call(down_last_kernel, out_shape=jax.ShapeDtypeStruct(so_far.sh...]
    ppermute x1, starting transfers between devices: 0.63 us -> 2.77 us  [opposite(): return lax.ppermute(x, 'row', [(i, (i + 2) % n) for i in range(n)])]
    ppermute x1, waiting for transfers between devices: 1.34 us -> 2.93 us  [mirror(): return lax.ppermute(x, ('row', 'col'), flat((4, 4), turned))]
  transfers between devices with their start and end apart: 25 -> 25, of which waited for: 14 -> 13; matrix products, arithmetic and copies ran while one was open for 8% -> 6% of each run, Pallas kernels for 8% -> 9%
where the time goes in v3:
time: 134 us
  waiting for transfers between devices  76.7 us (57%)
  starting transfers between devices  30.7 us (23%)
  Pallas kernels  17.3 us (13%)
  local copies, waits for them, and re-layouts  6.71 us (5%)
    ppermute x6, waiting for transfers between devices, z_step(): lax.ppermute(x, ('dp', 'col'), flat(sizes, lambda i, c: (i // n * n + (i...  37.2 us
    ppermute x8, waiting for transfers between devices, y_step(): lax.ppermute(x, ('row', 'col'), flat(sizes, lambda r, c: ((r + 1 - 2 * ((...  21.3 us
    ppermute x9, waiting for transfers between devices, col_swap(): return lax.ppermute(x, 'col', [(i, i ^ m) for i in range(n)])  15.3 us
    ppermute x6, starting transfers between devices, z_step(): lax.ppermute(x, ('dp', 'col'), flat(sizes, lambda i, c: (i // n * n + (i...  10.5 us
    ppermute x8, starting transfers between devices, y_step(): lax.ppermute(x, ('row', 'col'), flat(sizes, lambda r, c: ((r + 1 - 2 * ((...  7.97 us
    ppermute x9, starting transfers between devices, col_swap(): return lax.ppermute(x, 'col', [(i, i ^ m) for i in range(n)])  6.48 us
    pallas_call x1, Pallas kernels, up_part(): pl.pallas_call(up_part_kernel, out_shape=jax.ShapeDtypeStruct((rows, widt...  5.22 us
    pallas_call x1, Pallas kernels, down(): pl.pallas_call(functools.partial(down_kernel, plan), out_shape=jax.ShapeD...  4.17 us
  transfers between devices with their start and end apart: 25, of which 13 were waited for; matrix products, arithmetic and copies ran while one was open for 6% of the time, Pallas kernels for 9%

profile of v3, /device:TPU:4, one launch (start us, length us, event | category | flops | bytes accessed | tf_op | source)
XLA Modules:
  0.0 133.7 jit_solution(5077122219468890584)
XLA Ops:
  0.6 0.0 copy-start
  0.6 0.1 collective-permute-start.3
  0.7 2.3 %collective-permute-start.8 = (bf16[512,1536]{1,0:T(8,128)(2,1)}, bf16[512,1536]{1,0:T(8,128)(2,1)}, u32[]{:S(2)}, u32[]{:S(2)}) collective-permute-start(bf16[512,1536]{1,0:T(8,128)(2,1)} %t0.1), channel_id=1, source_target_pairs={{0,2},{1,3},{2,0},{3,1},{4,6},{5,7},{6,4},{7,5},{8,10},{9,11},{10,... | collective-permute-start | bytes 4718600 | tf_op jit(solution)/shard_map/ppermute | solution.py:53
  3.1 1.7 %constant_dynamic-slice_fusion = bf16[384,384]{1,0:T(8,128)(2,1)} fusion(bf16[1536,768]{1,0:T(8,128)(2,1)} %own.1, s32[]{:T(128)S(6)} %select_n.12), kind=kLoop, calls=%fused_computation.1 | loop fusion | bytes 589828 | tf_op jit(solution)/shard_map/dynamic_slice | solution.py:282
  4.8 2.8 %collective-permute-start.1 = (bf16[384,384]{1,0:T(8,128)(2,1)}, bf16[384,384]{1,0:T(8,128)(2,1)}, u32[]{:S(2)}, u32[]{:S(2)}) collective-permute-start(bf16[384,384]{1,0:T(8,128)(2,1)} %constant_dynamic-slice_fusion), channel_id=1, source_target_pairs={{0,8},{4,12},{8,0},{12,4},{1,9},{5,13},{9,1},{13,5},{2,10},{6,14},... | collective-permute-start | bytes 884744 | tf_op jit(solution)/shard_map/ppermute | solution.py:48
  7.5 1.3 %collective-permute-start.2 = (bf16[384,384]{1,0:T(8,128)(2,1)}, bf16[384,384]{1,0:T(8,128)(2,1)}, u32[]{:S(2)}, u32[]{:S(2)}) collective-permute-start(bf16[384,384]{1,0:T(8,128)(2,1)} %constant_dynamic-slice_fusion), channel_id=1, source_target_pairs={{0,12},{1,5},{2,14},{3,7},{4,0},{5,9},{6,2},{7,11},{8,4},{9,13},{1... | collective-permute-start | bytes 884744 | tf_op jit(solution)/shard_map/ppermute | solution.py:30
  8.9 1.4 %slice.3 = bf16[1536,384]{1,0:T(8,128)(2,1)S(1)} slice(bf16[1536,768]{1,0:T(8,128)(2,1)} %own.1), slice={[0:1536], [0:384]} | slice | bytes 2359296 | tf_op jit(solution)/shard_map/slice | solution.py:286
  10.3 2.5 %copy.5 = bf16[1536,768]{0,1:T(8,128)(2,1)} copy(bf16[1536,768]{1,0:T(8,128)(2,1)S(1)} %copy-done) | data formatting | bytes 4718592 | tf_op args[1]
  12.8 9.3 %collective-permute-done = bf16[384,384]{1,0:T(8,128)(2,1)} collective-permute-done((bf16[384,384]{1,0:T(8,128)(2,1)}, bf16[384,384]{1,0:T(8,128)(2,1)}, u32[]{:S(2)}, u32[]{:S(2)}) %collective-permute-start) | collective-permute-done | bytes 294944 | tf_op jit(solution)/shard_map/ppermute | solution.py:30
  22.1 0.0 collective-permute-done.1
  22.1 0.0 collective-permute-done.2
  22.1 0.0 collective-permute-done.3.t1
  22.1 0.1 collective-permute-start.6
  22.2 3.2 %collective-permute-start.7 = (bf16[1536,384]{1,0:T(8,128)(2,1)S(1)}, bf16[1536,384]{1,0:T(8,128)(2,1)S(1)}, u32[]{:S(2)}, u32[]{:S(2)}) collective-permute-start(bf16[1536,384]{1,0:T(8,128)(2,1)S(1)} %slice.3), channel_id=1, source_target_pairs={{0,12},{1,5},{2,14},{3,7},{4,0},{5,9},{6,2},{7,11},{8,4},{9,13},{1... | collective-permute-start | bytes 3538952 | tf_op jit(solution)/shard_map/ppermute | solution.py:30
  25.4 1.3 pad_maximum_fusion.p0
  26.6 1.0 collective-permute-start.4
  27.6 4.0 %collective-permute-start.5 = (bf16[3,384,384]{2,1,0:T(8,128)(2,1)S(1)}, bf16[3,384,384]{2,1,0:T(8,128)(2,1)S(1)}, u32[]{:S(2)}, u32[]{:S(2)}) collective-permute-start(bf16[3,384,384]{2,1,0:T(8,128)(2,1)S(1)} %pad_maximum_fusion.p0), channel_id=1, source_target_pairs={{0,112},{1,17},{2,114},{3,19},{16,0},{17,33},{18,2},{19,35},{32,16... | collective-permute-start | bytes 2654216 | tf_op jit(solution)/shard_map/ppermute | solution.py:41
  31.6 1.1 constant_dynamic-slice_fusion.1
  32.8 6.6 %collective-permute-done.8.t2 = bf16[512,1536]{1,0:T(8,128)(2,1)} collective-permute-done((bf16[512,1536]{1,0:T(8,128)(2,1)}, bf16[512,1536]{1,0:T(8,128)(2,1)}, u32[]{:S(2)}, u32[]{:S(2)}) %collective-permute-start.8) | collective-permute-done | bytes 1572896 | tf_op jit(solution)/shard_map/ppermute | solution.py:53
  39.4 12.6 %collective-permute-done.4.p1 = bf16[3,384,384]{2,1,0:T(8,128)(2,1)S(1)} collective-permute-done((bf16[3,384,384]{2,1,0:T(8,128)(2,1)S(1)}, bf16[3,384,384]{2,1,0:T(8,128)(2,1)S(1)}, u32[]{:S(2)}, u32[]{:S(2)}) %collective-permute-start.4) | collective-permute-done | bytes 884768 | tf_op jit(solution)/shard_map/ppermute | solution.py:41
  52.0 0.1 collective-permute-start.9
  52.1 0.1 collective-permute-start.11
  52.2 0.8 collective-permute-start.10
  53.0 2.9 %collective-permute-start.12 = (bf16[768,384]{1,0:T(8,128)(2,1)S(1)}, bf16[768,384]{1,0:T(8,128)(2,1)S(1)}, u32[]{:S(2)}, u32[]{:S(2)}) collective-permute-start(bf16[768,384]{1,0:T(8,128)(2,1)S(1)} %constant_dynamic-slice_fusion.1), channel_id=1, source_target_pairs={{0,2},{1,3},{2,0},{3,1},{4,6},{5,7},{6,4},{7,5},{8,10},{9,11},{10,... | collective-permute-start | bytes 1769480 | tf_op jit(solution)/shard_map/ppermute | solution.py:53
  55.9 2.0 %sort_tokens.1.t = bf16[4,512,1536]{2,1,0:T(8,128)(2,1)S(1)} custom-call(bf16[512,1536]{1,0:T(8,128)(2,1)S(1)} %copy-done.2, bf16[512,1536]{1,0:T(8,128)(2,1)} %collective-permute-done.3.t1, bf16[512,1536]{1,0:T(8,128)(2,1)} %collective-permute-done.8.t2, bf16[512,1536]{1,0:T(8,128)(2,1)S(1)} %collective-permute-done.9.t3), custom_call_target="tpu_custom_call" | custom-call | bytes 12582912 | tf_op jit(solution)/shard_map/sort_tokens/pallas_call | solution.py:109
  57.9 0.0 copy-start.3
  57.9 5.2 %up_part.1.so_far = f32[512,768]{1,0:T(8,128)S(1)} custom-call(bf16[4,512,1536]{2,1,0:T(8,128)(2,1)S(1)} %sort_tokens.1.t, bf16[1536,768]{1,0:T(8,128)(2,1)S(1)} %copy-done, bf16[1536,384]{1,0:T(8,128)(2,1)S(1)} %collective-permute-done.6.w1, bf16[1536,384]{1,0:T(8,128)(2,1)S(1)} %collective-permute-done.7.w3, bf16[3,384,384]{2,1,0:T(8,128)(2,1)S(1)} %pad_maximum_fusion.p0, ...), custom_call_target="tpu_custom_call" | custom-call | flops 3623878656 | bytes 11796480 | tf_op jit(solution)/shard_map/up_part/pallas_call | solution.py:163
  63.1 3.8 %collective-permute-done.12.x0 = bf16[768,384]{1,0:T(8,128)(2,1)S(1)} collective-permute-done((bf16[768,384]{1,0:T(8,128)(2,1)S(1)}, bf16[768,384]{1,0:T(8,128)(2,1)S(1)}, u32[]{:S(2)}, u32[]{:S(2)}) %collective-permute-start.12) | collective-permute-done | bytes 589856 | tf_op jit(solution)/shard_map/ppermute | solution.py:53
  66.9 1.0 collective-permute-done.10.p2
  67.9 1.7 %collective-permute-done.11.w2 = bf16[1536,384]{1,0:T(8,128)(2,1)S(1)} collective-permute-done((bf16[1536,384]{1,0:T(8,128)(2,1)S(1)}, bf16[1536,384]{1,0:T(8,128)(2,1)S(1)}, u32[]{:S(2)}, u32[]{:S(2)}) %collective-permute-start.11) | collective-permute-done | bytes 1179680 | tf_op jit(solution)/shard_map/ppermute | solution.py:30
  69.6 2.8 %up_rest.1 = (bf16[512,768]{1,0:T(8,128)(2,1)}, bf16[512,768]{1,0:T(8,128)(2,1)S(1)}) custom-call(bf16[4,512,1536]{2,1,0:T(8,128)(2,1)S(1)} %sort_tokens.1.t, f32[512,768]{1,0:T(8,128)S(1)} %up_part.1.so_far, bf16[1536,384]{1,0:T(8,128)(2,1)S(1)} %collective-permute-done.11.w2, bf16[3,384,384]{2,1,0:T(8,128)(2,1)S(1)} %collective-permute-done.10.p2, ...), custom_call_target="tpu_custom_call" | custom-call | flops 1207959552 | bytes 3932160 | tf_op jit(solution)/shard_map/up_rest/pallas_call | solution.py:177
  72.4 3.0 %collective-permute-start.13 = (bf16[512,768]{1,0:T(8,128)(2,1)S(1)}, bf16[512,768]{1,0:T(8,128)(2,1)S(1)}, u32[]{:S(2)}, u32[]{:S(2)}) collective-permute-start(bf16[512,768]{1,0:T(8,128)(2,1)S(1)} %get-tuple-element.54), channel_id=1, source_target_pairs={{0,12},{1,4},{2,0},{3,8},{4,1},{5,9},{6,5},{7,13},{8,10},{9,2},{10... | collective-permute-start | bytes 2359304 | tf_op jit(solution)/shard_map/ppermute | solution.py:66
  75.4 1.5 %collective-permute-start.14 = (bf16[768,384]{1,0:T(8,128)(2,1)S(1)}, bf16[768,384]{1,0:T(8,128)(2,1)S(1)}, u32[]{:S(2)}, u32[]{:S(2)}) collective-permute-start(bf16[768,384]{1,0:T(8,128)(2,1)S(1)} %collective-permute-done.12.x0), channel_id=1, source_target_pairs={{0,16},{1,113},{2,18},{3,115},{16,32},{17,1},{18,34},{19,3},{32,48... | collective-permute-start | bytes 1769480 | tf_op jit(solution)/shard_map/ppermute | solution.py:41
  76.9 3.2 %collective-permute-start.15 = (bf16[768,384]{1,0:T(8,128)(2,1)S(1)}, bf16[768,384]{1,0:T(8,128)(2,1)S(1)}, u32[]{:S(2)}, u32[]{:S(2)}) collective-permute-start(bf16[768,384]{1,0:T(8,128)(2,1)S(1)} %collective-permute-done.12.x0), channel_id=1, source_target_pairs={{0,112},{1,17},{2,114},{3,19},{16,0},{17,33},{18,2},{19,35},{32,16... | collective-permute-start | bytes 1769480 | tf_op jit(solution)/shard_map/ppermute | solution.py:41
  80.1 11.9 %collective-permute-done.14.x1 = bf16[768,384]{1,0:T(8,128)(2,1)S(1)} collective-permute-done((bf16[768,384]{1,0:T(8,128)(2,1)S(1)}, bf16[768,384]{1,0:T(8,128)(2,1)S(1)}, u32[]{:S(2)}, u32[]{:S(2)}) %collective-permute-start.14) | collective-permute-done | bytes 589856 | tf_op jit(solution)/shard_map/ppermute | solution.py:41
  92.0 1.1 collective-permute-done.15.x3
  93.1 2.9 %collective-permute-done.13.rest_0_ = bf16[512,768]{1,0:T(8,128)(2,1)S(1)} collective-permute-done((bf16[512,768]{1,0:T(8,128)(2,1)S(1)}, bf16[512,768]{1,0:T(8,128)(2,1)S(1)}, u32[]{:S(2)}, u32[]{:S(2)}) %collective-permute-start.13) | collective-permute-done | bytes 786464 | tf_op jit(solution)/shard_map/ppermute | solution.py:66
  96.1 3.2 %collective-permute-start.18 = (bf16[512,768]{1,0:T(8,128)(2,1)S(1)}, bf16[512,768]{1,0:T(8,128)(2,1)S(1)}, u32[]{:S(2)}, u32[]{:S(2)}) collective-permute-start(bf16[512,768]{1,0:T(8,128)(2,1)S(1)} %collective-permute-done.13.rest_0_), channel_id=1, source_target_pairs={{0,12},{1,5},{2,14},{3,7},{4,0},{5,9},{6,2},{7,11},{8,4},{9,13},{1... | collective-permute-start | bytes 2359304 | tf_op jit(solution)/shard_map/ppermute | solution.py:30
  99.3 0.2 collective-permute-start.20
  99.5 0.3 collective-permute-start.21
  99.8 10.6 %collective-permute-done.19.x2 = bf16[768,384]{1,0:T(8,128)(2,1)S(1)} collective-permute-done((bf16[768,384]{1,0:T(8,128)(2,1)S(1)}, bf16[768,384]{1,0:T(8,128)(2,1)S(1)}, u32[]{:S(2)}, u32[]{:S(2)}) %collective-permute-start.19) | collective-permute-done | bytes 589856 | tf_op jit(solution)/shard_map/ppermute | solution.py:41
  110.4 7.1 %collective-permute-done.17.rest_1_ = bf16[512,768]{1,0:T(8,128)(2,1)S(1)} collective-permute-done((bf16[512,768]{1,0:T(8,128)(2,1)S(1)}, bf16[512,768]{1,0:T(8,128)(2,1)S(1)}, u32[]{:S(2)}, u32[]{:S(2)}) %collective-permute-start.17) | collective-permute-done | bytes 786464 | tf_op jit(solution)/shard_map/ppermute | solution.py:30
  117.5 0.5 collective-permute-start.23
  118.0 4.9 %collective-permute-done.23.y2 = bf16[768,384]{1,0:T(8,128)(2,1)S(1)} collective-permute-done((bf16[768,384]{1,0:T(8,128)(2,1)S(1)}, bf16[768,384]{1,0:T(8,128)(2,1)S(1)}, u32[]{:S(2)}, u32[]{:S(2)}) %collective-permute-start.23) | collective-permute-done | bytes 589856 | tf_op jit(solution)/shard_map/ppermute | solution.py:53
  122.9 0.8 sort_w.1.w
  123.7 4.2 %down.1.so_far = f32[512,1536]{1,0:T(8,128)S(1)} custom-call(bf16[4,768,1536]{2,1,0:T(8,128)(2,1)S(1)} %sort_w.1.w, bf16[512,768]{1,0:T(8,128)(2,1)S(1)} %collective-permute-done.13.rest_0_, bf16[512,768]{1,0:T(8,128)(2,1)S(1)} %collective-permute-done.17.rest_1_, bf16[512,768]{1,0:T(8,128)(2,1)S(1)} %collective-permute-done.18.rest_2_), custom_call_target="tpu_custom_call" | custom-call | flops 3623878656 | bytes 12582912 | tf_op jit(solution)/shard_map/down/pallas_call | solution.py:235
  127.9 3.3 %collective-permute-done.24.g = bf16[512,768]{1,0:T(8,128)(2,1)S(1)} collective-permute-done((bf16[512,768]{1,0:T(8,128)(2,1)S(1)}, bf16[512,768]{1,0:T(8,128)(2,1)S(1)}, u32[]{:S(2)}, u32[]{:S(2)}) %collective-permute-start.24) | collective-permute-done | bytes 786464 | tf_op jit(solution)/shard_map/ppermute | solution.py:30
  131.2 2.3 %down_last.1 = bf16[512,1536]{1,0:T(8,128)(2,1)} custom-call(bf16[4,768,1536]{2,1,0:T(8,128)(2,1)S(1)} %sort_w.1.w, bf16[512,768]{1,0:T(8,128)(2,1)S(1)} %collective-permute-done.24.g, f32[512,1536]{1,0:T(8,128)S(1)} %down.1.so_far), custom_call_target="tpu_custom_call" | custom-call | flops 1207959552 | bytes 4718592 | tf_op jit(solution)/shard_map/down_last/pallas_call | solution.py:261
  (21 shorter events, 0.1 us)
Async XLA Ops:
  0.6 9.7 %copy-start = (bf16[1536,768]{1,0:T(8,128)(2,1)S(1)}, bf16[1536,768]{1,0:T(8,128)(2,1)}, u32[]{:S(2)}) copy-start(bf16[1536,768]{1,0:T(8,128)(2,1)} %own.1) | copy-start | bytes 7077892
  0.6 21.4 %collective-permute-start.3 = (bf16[512,1536]{1,0:T(8,128)(2,1)}, bf16[512,1536]{1,0:T(8,128)(2,1)}, u32[]{:S(2)}, u32[]{:S(2)}) collective-permute-start(bf16[512,1536]{1,0:T(8,128)(2,1)} %t0.1), channel_id=1, source_target_pairs={{0,1},{1,0},{2,3},{3,2},{4,5},{5,4},{6,7},{7,6},{8,9},{9,8},{10,11... | collective-permute-start | bytes 4718600 | tf_op jit(solution)/shard_map/ppermute | solution.py:53
  0.7 38.6 %collective-permute-start.8 = (bf16[512,1536]{1,0:T(8,128)(2,1)}, bf16[512,1536]{1,0:T(8,128)(2,1)}, u32[]{:S(2)}, u32[]{:S(2)}) collective-permute-start(bf16[512,1536]{1,0:T(8,128)(2,1)} %t0.1), channel_id=1, source_target_pairs={{0,2},{1,3},{2,0},{3,1},{4,6},{5,7},{6,4},{7,5},{8,10},{9,11},{10,... | collective-permute-start | bytes 4718600 | tf_op jit(solution)/shard_map/ppermute | solution.py:53
  4.8 17.3 %collective-permute-start = (bf16[384,384]{1,0:T(8,128)(2,1)}, bf16[384,384]{1,0:T(8,128)(2,1)}, u32[]{:S(2)}, u32[]{:S(2)}) collective-permute-start(bf16[384,384]{1,0:T(8,128)(2,1)} %constant_dynamic-slice_fusion), channel_id=1, source_target_pairs={{0,4},{1,13},{2,6},{3,15},{4,8},{5,1},{6,10},{7,3},{8,12},{9,5},{1... | collective-permute-start | bytes 884744 | tf_op jit(solution)/shard_map/ppermute | solution.py:30
  4.8 17.3 %collective-permute-start.1 = (bf16[384,384]{1,0:T(8,128)(2,1)}, bf16[384,384]{1,0:T(8,128)(2,1)}, u32[]{:S(2)}, u32[]{:S(2)}) collective-permute-start(bf16[384,384]{1,0:T(8,128)(2,1)} %constant_dynamic-slice_fusion), channel_id=1, source_target_pairs={{0,8},{4,12},{8,0},{12,4},{1,9},{5,13},{9,1},{13,5},{2,10},{6,14},... | collective-permute-start | bytes 884744 | tf_op jit(solution)/shard_map/ppermute | solution.py:48
  7.5 14.5 %collective-permute-start.2 = (bf16[384,384]{1,0:T(8,128)(2,1)}, bf16[384,384]{1,0:T(8,128)(2,1)}, u32[]{:S(2)}, u32[]{:S(2)}) collective-permute-start(bf16[384,384]{1,0:T(8,128)(2,1)} %constant_dynamic-slice_fusion), channel_id=1, source_target_pairs={{0,12},{1,5},{2,14},{3,7},{4,0},{5,9},{6,2},{7,11},{8,4},{9,13},{1... | collective-permute-start | bytes 884744 | tf_op jit(solution)/shard_map/ppermute | solution.py:30
  12.8 43.1 %copy-start.2 = (bf16[512,1536]{1,0:T(8,128)(2,1)S(1)}, bf16[512,1536]{1,0:T(8,128)(2,1)}, u32[]{:S(2)}) copy-start(bf16[512,1536]{1,0:T(8,128)(2,1)} %t0.1) | copy-start | bytes 4718596
  22.1 29.9 %collective-permute-start.6 = (bf16[1536,384]{1,0:T(8,128)(2,1)S(1)}, bf16[1536,384]{1,0:T(8,128)(2,1)S(1)}, u32[]{:S(2)}, u32[]{:S(2)}) collective-permute-start(bf16[1536,384]{1,0:T(8,128)(2,1)S(1)} %slice.3), channel_id=1, source_target_pairs={{0,4},{1,13},{2,6},{3,15},{4,8},{5,1},{6,10},{7,3},{8,12},{9,5},{1... | collective-permute-start | bytes 3538952 | tf_op jit(solution)/shard_map/ppermute | solution.py:30
  22.2 29.8 %collective-permute-start.7 = (bf16[1536,384]{1,0:T(8,128)(2,1)S(1)}, bf16[1536,384]{1,0:T(8,128)(2,1)S(1)}, u32[]{:S(2)}, u32[]{:S(2)}) collective-permute-start(bf16[1536,384]{1,0:T(8,128)(2,1)S(1)} %slice.3), channel_id=1, source_target_pairs={{0,12},{1,5},{2,14},{3,7},{4,0},{5,9},{6,2},{7,11},{8,4},{9,13},{1... | collective-permute-start | bytes 3538952 | tf_op jit(solution)/shard_map/ppermute | solution.py:30
  26.6 25.3 %collective-permute-start.4 = (bf16[3,384,384]{2,1,0:T(8,128)(2,1)S(1)}, bf16[3,384,384]{2,1,0:T(8,128)(2,1)S(1)}, u32[]{:S(2)}, u32[]{:S(2)}) collective-permute-start(bf16[3,384,384]{2,1,0:T(8,128)(2,1)S(1)} %pad_maximum_fusion.p0), channel_id=1, source_target_pairs={{0,16},{1,113},{2,18},{3,115},{16,32},{17,1},{18,34},{19,3},{32,48... | collective-permute-start | bytes 2654216 | tf_op jit(solution)/shard_map/ppermute | solution.py:41
  27.6 24.4 %collective-permute-start.5 = (bf16[3,384,384]{2,1,0:T(8,128)(2,1)S(1)}, bf16[3,384,384]{2,1,0:T(8,128)(2,1)S(1)}, u32[]{:S(2)}, u32[]{:S(2)}) collective-permute-start(bf16[3,384,384]{2,1,0:T(8,128)(2,1)S(1)} %pad_maximum_fusion.p0), channel_id=1, source_target_pairs={{0,112},{1,17},{2,114},{3,19},{16,0},{17,33},{18,2},{19,35},{32,16... | collective-permute-start | bytes 2654216 | tf_op jit(solution)/shard_map/ppermute | solution.py:41
  52.0 3.9 %collective-permute-start.9 = (bf16[512,1536]{1,0:T(8,128)(2,1)}, bf16[512,1536]{1,0:T(8,128)(2,1)S(1)}, u32[]{:S(2)}, u32[]{:S(2)}) collective-permute-start(bf16[512,1536]{1,0:T(8,128)(2,1)} %collective-permute-done.8.t2), channel_id=1, source_target_pairs={{0,1},{1,0},{2,3},{3,2},{4,5},{5,4},{6,7},{7,6},{8,9},{9,8},{10,11... | collective-permute-start | bytes 4718600 | tf_op jit(solution)/shard_map/ppermute | solution.py:53
  52.1 17.5 %collective-permute-start.11 = (bf16[1536,384]{1,0:T(8,128)(2,1)S(1)}, bf16[1536,384]{1,0:T(8,128)(2,1)S(1)}, u32[]{:S(2)}, u32[]{:S(2)}) collective-permute-start(bf16[1536,384]{1,0:T(8,128)(2,1)S(1)} %collective-permute-done.6.w1), channel_id=1, source_target_pairs={{0,4},{1,13},{2,6},{3,15},{4,8},{5,1},{6,10},{7,3},{8,12},{9,5},{1... | collective-permute-start | bytes 3538952 | tf_op jit(solution)/shard_map/ppermute | solution.py:30
  52.2 15.7 %collective-permute-start.10 = (bf16[3,384,384]{2,1,0:T(8,128)(2,1)S(1)}, bf16[3,384,384]{2,1,0:T(8,128)(2,1)S(1)}, u32[]{:S(2)}, u32[]{:S(2)}) collective-permute-start(bf16[3,384,384]{2,1,0:T(8,128)(2,1)S(1)} %collective-permute-done.4.p1), channel_id=1, source_target_pairs={{0,16},{1,113},{2,18},{3,115},{16,32},{17,1},{18,34},{19,3},{32,48... | collective-permute-start | bytes 2654216 | tf_op jit(solution)/shard_map/ppermute | solution.py:41
  53.0 13.9 %collective-permute-start.12 = (bf16[768,384]{1,0:T(8,128)(2,1)S(1)}, bf16[768,384]{1,0:T(8,128)(2,1)S(1)}, u32[]{:S(2)}, u32[]{:S(2)}) collective-permute-start(bf16[768,384]{1,0:T(8,128)(2,1)S(1)} %constant_dynamic-slice_fusion.1), channel_id=1, source_target_pairs={{0,2},{1,3},{2,0},{3,1},{4,6},{5,7},{6,4},{7,5},{8,10},{9,11},{10,... | collective-permute-start | bytes 1769480 | tf_op jit(solution)/shard_map/ppermute | solution.py:53
  57.9 11.7 %copy-start.3 = (bf16[512,768]{1,0:T(8,128)(2,1)S(1)}, bf16[512,768]{1,0:T(8,128)(2,1)}, u32[]{:S(2)}) copy-start(bf16[512,768]{1,0:T(8,128)(2,1)} %cot.1) | copy-start | bytes 2359300
  63.1 54.4 %copy-start.1 = (bf16[1536,768]{0,1:T(8,128)(2,1)S(1)}, bf16[1536,768]{0,1:T(8,128)(2,1)}, u32[]{:S(2)}) copy-start(bf16[1536,768]{0,1:T(8,128)(2,1)} %copy.5) | copy-start | bytes 7077892
  72.4 23.6 %collective-permute-start.13 = (bf16[512,768]{1,0:T(8,128)(2,1)S(1)}, bf16[512,768]{1,0:T(8,128)(2,1)S(1)}, u32[]{:S(2)}, u32[]{:S(2)}) collective-permute-start(bf16[512,768]{1,0:T(8,128)(2,1)S(1)} %get-tuple-element.54), channel_id=1, source_target_pairs={{0,12},{1,4},{2,0},{3,8},{4,1},{5,9},{6,5},{7,13},{8,10},{9,2},{10... | collective-permute-start | bytes 2359304 | tf_op jit(solution)/shard_map/ppermute | solution.py:66
  75.4 16.6 %collective-permute-start.14 = (bf16[768,384]{1,0:T(8,128)(2,1)S(1)}, bf16[768,384]{1,0:T(8,128)(2,1)S(1)}, u32[]{:S(2)}, u32[]{:S(2)}) collective-permute-start(bf16[768,384]{1,0:T(8,128)(2,1)S(1)} %collective-permute-done.12.x0), channel_id=1, source_target_pairs={{0,16},{1,113},{2,18},{3,115},{16,32},{17,1},{18,34},{19,3},{32,48... | collective-permute-start | bytes 1769480 | tf_op jit(solution)/shard_map/ppermute | solution.py:41
  76.9 16.2 %collective-permute-start.15 = (bf16[768,384]{1,0:T(8,128)(2,1)S(1)}, bf16[768,384]{1,0:T(8,128)(2,1)S(1)}, u32[]{:S(2)}, u32[]{:S(2)}) collective-permute-start(bf16[768,384]{1,0:T(8,128)(2,1)S(1)} %collective-permute-done.12.x0), channel_id=1, source_target_pairs={{0,112},{1,17},{2,114},{3,19},{16,0},{17,33},{18,2},{19,35},{32,16... | collective-permute-start | bytes 1769480 | tf_op jit(solution)/shard_map/ppermute | solution.py:41
  80.1 13.0 %collective-permute-start.16 = (bf16[768,384]{1,0:T(8,128)(2,1)S(1)}, bf16[768,384]{1,0:T(8,128)(2,1)S(1)}, u32[]{:S(2)}, u32[]{:S(2)}) collective-permute-start(bf16[768,384]{1,0:T(8,128)(2,1)S(1)} %collective-permute-done.12.x0), channel_id=1, source_target_pairs={{0,1},{1,0},{2,3},{3,2},{4,5},{5,4},{6,7},{7,6},{8,9},{9,8},{10,11... | collective-permute-start | bytes 1769480 | tf_op jit(solution)/shard_map/ppermute | solution.py:53
  96.1 21.4 %collective-permute-start.17 = (bf16[512,768]{1,0:T(8,128)(2,1)S(1)}, bf16[512,768]{1,0:T(8,128)(2,1)S(1)}, u32[]{:S(2)}, u32[]{:S(2)}) collective-permute-start(bf16[512,768]{1,0:T(8,128)(2,1)S(1)} %collective-permute-done.13.rest_0_), channel_id=1, source_target_pairs={{0,4},{1,13},{2,6},{3,15},{4,8},{5,1},{6,10},{7,3},{8,12},{9,5},{1... | collective-permute-start | bytes 2359304 | tf_op jit(solution)/shard_map/ppermute | solution.py:30
  96.1 21.4 %collective-permute-start.18 = (bf16[512,768]{1,0:T(8,128)(2,1)S(1)}, bf16[512,768]{1,0:T(8,128)(2,1)S(1)}, u32[]{:S(2)}, u32[]{:S(2)}) collective-permute-start(bf16[512,768]{1,0:T(8,128)(2,1)S(1)} %collective-permute-done.13.rest_0_), channel_id=1, source_target_pairs={{0,12},{1,5},{2,14},{3,7},{4,0},{5,9},{6,2},{7,11},{8,4},{9,13},{1... | collective-permute-start | bytes 2359304 | tf_op jit(solution)/shard_map/ppermute | solution.py:30
  99.3 11.1 %collective-permute-start.19 = (bf16[768,384]{1,0:T(8,128)(2,1)S(1)}, bf16[768,384]{1,0:T(8,128)(2,1)S(1)}, u32[]{:S(2)}, u32[]{:S(2)}) collective-permute-start(bf16[768,384]{1,0:T(8,128)(2,1)S(1)} %collective-permute-done.14.x1), channel_id=1, source_target_pairs={{0,16},{1,113},{2,18},{3,115},{16,32},{17,1},{18,34},{19,3},{32,48... | collective-permute-start | bytes 1769480 | tf_op jit(solution)/shard_map/ppermute | solution.py:41
  99.3 11.1 %collective-permute-start.20 = (bf16[768,384]{1,0:T(8,128)(2,1)S(1)}, bf16[768,384]{1,0:T(8,128)(2,1)S(1)}, u32[]{:S(2)}, u32[]{:S(2)}) collective-permute-start(bf16[768,384]{1,0:T(8,128)(2,1)S(1)} %collective-permute-done.14.x1), channel_id=1, source_target_pairs={{0,1},{1,0},{2,3},{3,2},{4,5},{5,4},{6,7},{7,6},{8,9},{9,8},{10,11... | collective-permute-start | bytes 1769480 | tf_op jit(solution)/shard_map/ppermute | solution.py:53
  99.5 10.9 %collective-permute-start.21 = (bf16[768,384]{1,0:T(8,128)(2,1)S(1)}, bf16[768,384]{1,0:T(8,128)(2,1)S(1)}, u32[]{:S(2)}, u32[]{:S(2)}) collective-permute-start(bf16[768,384]{1,0:T(8,128)(2,1)S(1)} %collective-permute-done.15.x3), channel_id=1, source_target_pairs={{0,1},{1,0},{2,3},{3,2},{4,5},{5,4},{6,7},{7,6},{8,9},{9,8},{10,11... | collective-permute-start | bytes 1769480 | tf_op jit(solution)/shard_map/ppermute | solution.py:53
  117.5 5.4 %collective-permute-start.22 = (bf16[768,1536]{1,0:T(8,128)(2,1)S(1)}, bf16[768,1536]{1,0:T(8,128)(2,1)S(1)}, u32[]{:S(2)}, u32[]{:S(2)}) collective-permute-start(bf16[768,1536]{1,0:T(8,128)(2,1)S(1)} %bitcast.5), channel_id=1, source_target_pairs={{0,1},{1,0},{2,3},{3,2},{4,5},{5,4},{6,7},{7,6},{8,9},{9,8},{10,11... | collective-permute-start | bytes 7077896 | tf_op jit(solution)/shard_map/ppermute | solution.py:53
  117.5 5.4 %collective-permute-start.23 = (bf16[768,384]{1,0:T(8,128)(2,1)S(1)}, bf16[768,384]{1,0:T(8,128)(2,1)S(1)}, u32[]{:S(2)}, u32[]{:S(2)}) collective-permute-start(bf16[768,384]{1,0:T(8,128)(2,1)S(1)} %collective-permute-done.19.x2), channel_id=1, source_target_pairs={{0,1},{1,0},{2,3},{3,2},{4,5},{5,4},{6,7},{7,6},{8,9},{9,8},{10,11... | collective-permute-start | bytes 1769480 | tf_op jit(solution)/shard_map/ppermute | solution.py:53
  118.0 13.2 %collective-permute-start.24 = (bf16[512,768]{1,0:T(8,128)(2,1)S(1)}, bf16[512,768]{1,0:T(8,128)(2,1)S(1)}, u32[]{:S(2)}, u32[]{:S(2)}) collective-permute-start(bf16[512,768]{1,0:T(8,128)(2,1)S(1)} %collective-permute-done.17.rest_1_), channel_id=1, source_target_pairs={{0,4},{1,13},{2,6},{3,15},{4,8},{5,1},{6,10},{7,3},{8,12},{9,5},{1... | collective-permute-start | bytes 2359304 | tf_op jit(solution)/shard_map/ppermute | solution.py:30

commit v4 on v3

--- a/solution.py
+++ b/solution.py
@@ -95,6 +95,27 @@
 
 def mul(a, b):
     return jnp.dot(a, b, preferred_element_type=jnp.float32)
+
+
+def cut_kernel(at, w, out, sem):
+    rows, cols = out.shape
+    z = lax.axis_index("dp") & 3
+    copy = pltpu.make_async_copy(w.at[pl.ds(pl.multiple_of(z * rows, 16), rows), pl.ds(at, cols)], out, sem)
+    copy.start()
+    copy.wait()
+
+
+def cut(w, rows, cols, at):
+    return pl.pallas_call(
+        functools.partial(cut_kernel, at),
+        out_shape=jax.ShapeDtypeStruct((rows, cols), w.dtype),
+        in_specs=[ANY],
+        out_specs=VMEM,
+        scratch_shapes=[pltpu.SemaphoreType.DMA],
+        compiler_params=params(),
+        cost_estimate=cost(0, 4 * rows * cols),
+        name="cut",
+    )(w)
 
 
 def sort_tokens_kernel(t0, t1, t2, t3, out, sem):
@@ -186,12 +207,14 @@
     )(t, so_far, w2, p2, cot)
 
 
-def sort_w_kernel(own, pair, x0, x1, x2, x3, y0, y1, y2, y3, out, sem):
+def sort_w_kernel(own, c0, c1, c2, c3, x0, x1, x2, x3, y0, y1, y2, y3, out, sem):
     c = lax.axis_index("col")
     z = lax.axis_index("dp") & 3
     q = x0.shape[1]
     pltpu.make_async_copy(own, out.at[c], sem).start()
-    pltpu.make_async_copy(pair, out.at[c ^ 1], sem).start()
+    h = c0.shape[0]
+    for i, src in enumerate((c0, c1, c2, c3)):
+        pltpu.make_async_copy(src, out.at[c ^ 1, pl.ds(i * h, h)], sem).start()
     for m, srcs, core in ((2, (x0, x1, x2, x3), c & 1), (3, (y0, y1, y2, y3), 1 - (c & 1))):
         for u, src in enumerate(srcs):
             cols = pl.ds(pl.multiple_of(away(z, u, core) * q, 128), q)
@@ -204,7 +227,7 @@
     return pl.pallas_call(
         sort_w_kernel,
         out_shape=jax.ShapeDtypeStruct((4, ff, depth), jnp.bfloat16),
-        in_specs=[ANY] * 10,
+        in_specs=[ANY] * 13,
         out_specs=VMEM,
         scratch_shapes=[pltpu.SemaphoreType.DMA],
         compiler_params=params(),
@@ -279,11 +302,14 @@
     width = ff // 2
     part = depth // 4
     z = lax.axis_index("dp") % 4
-    piece = lax.dynamic_slice(w_up, (z * part, width), (part, width))
+    piece = cut(w_up, part, width, width)
     s1, s2, s3 = y_step(piece), opposite(piece), y_step(piece, 1)
     t_x = col_swap(tokens, 2)
     t_pair = col_swap(tokens, 1)
-    s1, s2, s3, t_pair, w0, w_t = together(s1, s2, s3, t_pair, w_up[:, :width], w_up.T)
+    w_t = w_up.T
+    s1, s2, s3, t_pair, w0, w_t, *quarters = together(
+        s1, s2, s3, t_pair, w_up[:, :width], w_t, *jnp.split(w_t, 4)
+    )
     p0 = jnp.stack([s1, s2, s3])
     p1, p3 = z_step(p0), z_step(p0, 1)
     w1, w3 = y_step(w0), y_step(w0, 1)
@@ -298,17 +324,17 @@
     p2, w2, so_far, x0 = together(p2, w2, so_far, x0)
     hidden, d_pre = up_rest(t, so_far, w2, p2, cotangent)
 
-    d_pre, x0 = together(d_pre, x0)
+    d_pre, x0, *quarters = together(d_pre, x0, *quarters)
     m = mirror(d_pre)
     x1, x3 = z_step(x0), z_step(x0, 1)
-    y0 = col_swap(x0, 1)
-    m, x1, x3, y0 = together(m, x1, x3, y0)
+    y0, c0 = col_swap(x0, 1), col_swap(quarters[0], 1)
+    m, x1, x3, y0, c0 = together(m, x1, x3, y0, c0)
     g1, g3 = y_step(m), y_step(m, 1)
     x2 = z_step(x1)
     y1, y3 = col_swap(x1, 1), col_swap(x3, 1)
-    g1, g3, x2, y1, y3, w_t2 = together(g1, g3, x2, y1, y3, w_t)
+    g1, g3, x2, y1, y3, *quarters = together(g1, g3, x2, y1, y3, *quarters[1:])
     g2 = y_step(g1)
-    w = sort_w(w_t, col_swap(w_t2, 1), x0, x1, x2, x3, y0, y1, col_swap(x2, 1), y3)
+    w = sort_w(w_t, c0, *[col_swap(x, 1) for x in quarters], x0, x1, x2, x3, y0, y1, col_swap(x2, 1), y3)
     total = down(w, (m, g1, g3), (0, 1, 3), None, jnp.float32)
     g2, total = together(g2, total)
     return hidden, down_last(w, g2, total)

time: 134 us -> 132 us (0.985)
  waiting for transfers between devices: 76.7 us -> 69.7 us
  local copies, waits for them, and re-layouts: 6.71 us -> 10.8 us
  Pallas kernels: 17.3 us -> 19.9 us
    ppermute x8, waiting for transfers between devices: 21.3 us -> 11.1 us  [y_step(): lax.ppermute(x, ('row', 'col'), flat(sizes, lambda r, c: ((r + 1 - 2 * ((...]
    ppermute x6, waiting for transfers between devices: 37.2 us -> 31.2 us  [z_step(): lax.ppermute(x, ('dp', 'col'), flat(sizes, lambda i, c: (i // n * n + (i...]
    ppermute x1, waiting for transfers between devices: 0.01 us -> 4.42 us  [opposite(): return lax.ppermute(x, 'row', [(i, (i + 2) % n) for i in range(n)])]
    ppermute x9 -> x12, waiting for transfers between devices: 15.3 us -> 19 us  [col_swap(): return lax.ppermute(x, 'col', [(i, i ^ m) for i in range(n)])]
    unnamed x9 -> x23, local copies, waits for them, and re-layouts: 2.49 us -> 5.54 us
    split x0 -> x1, local copies, waits for them, and re-layouts: none -> 3.02 us  [body(): jnp.split(w_t, 4)]
    ppermute x9 -> x12, starting transfers between devices: 6.48 us -> 3.57 us  [col_swap(): return lax.ppermute(x, 'col', [(i, i ^ m) for i in range(n)])]
    pallas_call x1, Pallas kernels: 5.22 us -> 7.43 us  [up_part(): pl.pallas_call(up_part_kernel, out_shape=jax.ShapeDtypeStruct((rows, widt...]
  transfers between devices with their start and end apart: 25 -> 28, of which waited for: 13 -> 17; matrix products, arithmetic and copies ran while one was open for 6% -> 7% of each run, Pallas kernels for 9% -> 11%
where the time goes in v4:
time: 132 us
  waiting for transfers between devices  69.7 us (53%)
  starting transfers between devices  29.5 us (22%)
  Pallas kernels  19.9 us (15%)
  local copies, waits for them, and re-layouts  10.8 us (8%)
    ppermute x6, waiting for transfers between devices, z_step(): lax.ppermute(x, ('dp', 'col'), flat(sizes, lambda i, c: (i // n * n + (i...  31.2 us
    ppermute x12, waiting for transfers between devices, col_swap(): return lax.ppermute(x, 'col', [(i, i ^ m) for i in range(n)])  19 us
    ppermute x6, starting transfers between devices, z_step(): lax.ppermute(x, ('dp', 'col'), flat(sizes, lambda i, c: (i // n * n + (i...  12.3 us
    ppermute x8, waiting for transfers between devices, y_step(): lax.ppermute(x, ('row', 'col'), flat(sizes, lambda r, c: ((r + 1 - 2 * ((...  11.1 us
    ppermute x8, starting transfers between devices, y_step(): lax.ppermute(x, ('row', 'col'), flat(sizes, lambda r, c: ((r + 1 - 2 * ((...  9.55 us
    pallas_call x1, Pallas kernels, up_part(): pl.pallas_call(up_part_kernel, out_shape=jax.ShapeDtypeStruct((rows, widt...  7.43 us
    unnamed x23, local copies, waits for them, and re-layouts  5.54 us
    ppermute x1, waiting for transfers between devices, opposite(): return lax.ppermute(x, 'row', [(i, (i + 2) % n) for i in range(n)])  4.42 us
  transfers between devices with their start and end apart: 28, of which 17 were waited for; matrix products, arithmetic and copies ran while one was open for 7% of the time, Pallas kernels for 11%

profile of v4, /device:TPU:4, one launch (start us, length us, event | category | flops | bytes accessed | tf_op | source)
XLA Modules:
  0.0 132.1 jit_solution(16316833418056616480)
XLA Ops:
  0.7 1.7 %copy-done = bf16[1536,768]{1,0:T(8,128)(2,1)S(1)} copy-done((bf16[1536,768]{1,0:T(8,128)(2,1)S(1)}, bf16[1536,768]{1,0:T(8,128)(2,1)}, u32[]{:S(2)}) %copy-start) | copy-done | bytes 2359320
  2.5 1.7 %collective-permute-start = (bf16[384,384]{1,0:T(8,128)(2,1)S(1)}, bf16[384,384]{1,0:T(8,128)(2,1)S(1)}, u32[]{:S(2)}, u32[]{:S(2)}) collective-permute-start(bf16[384,384]{1,0:T(8,128)(2,1)S(1)} %cut.1), channel_id=1, source_target_pairs={{0,4},{1,13},{2,6},{3,15},{4,8},{5,1},{6,10},{7,3},{8,12},{9,5},{1... | collective-permute-start | bytes 884744 | tf_op jit(solution)/shard_map/ppermute | solution.py:30
  4.1 2.9 %collective-permute-start.1 = (bf16[384,384]{1,0:T(8,128)(2,1)S(1)}, bf16[384,384]{1,0:T(8,128)(2,1)S(1)}, u32[]{:S(2)}, u32[]{:S(2)}) collective-permute-start(bf16[384,384]{1,0:T(8,128)(2,1)S(1)} %cut.1), channel_id=1, source_target_pairs={{0,8},{4,12},{8,0},{12,4},{1,9},{5,13},{9,1},{13,5},{2,10},{6,14},... | collective-permute-start | bytes 884744 | tf_op jit(solution)/shard_map/ppermute | solution.py:48
  7.0 1.3 %collective-permute-start.2 = (bf16[384,384]{1,0:T(8,128)(2,1)S(1)}, bf16[384,384]{1,0:T(8,128)(2,1)S(1)}, u32[]{:S(2)}, u32[]{:S(2)}) collective-permute-start(bf16[384,384]{1,0:T(8,128)(2,1)S(1)} %cut.1), channel_id=1, source_target_pairs={{0,12},{1,5},{2,14},{3,7},{4,0},{5,9},{6,2},{7,11},{8,4},{9,13},{1... | collective-permute-start | bytes 884744 | tf_op jit(solution)/shard_map/ppermute | solution.py:30
  8.4 0.5 collective-permute-start.8
  8.9 1.1 slice.3
  10.0 2.4 %copy.5 = bf16[1536,768]{0,1:T(8,128)(2,1)} copy(bf16[1536,768]{1,0:T(8,128)(2,1)S(1)} %copy-done.1) | data formatting | bytes 4718592 | tf_op args[1]
  12.4 3.0 %fusion = (bf16[192,1536]{1,0:T(8,128)(2,1)}, bf16[192,1536]{1,0:T(8,128)(2,1)}, bf16[192,1536]{1,0:T(8,128)(2,1)}, bf16[192,1536]{1,0:T(8,128)(2,1)}) fusion(bf16[768,1536]{1,0:T(8,128)(2,1)} %bitcast.4), kind=kLoop, calls=%fused_computation.2 | loop fusion | bytes 4718592 | tf_op jit(solution)/shard_map/split | solution.py:311
  15.5 4.4 %collective-permute-done.1 = bf16[384,384]{1,0:T(8,128)(2,1)S(1)} collective-permute-done((bf16[384,384]{1,0:T(8,128)(2,1)S(1)}, bf16[384,384]{1,0:T(8,128)(2,1)S(1)}, u32[]{:S(2)}, u32[]{:S(2)}) %collective-permute-start.1) | collective-permute-done | bytes 294944 | tf_op jit(solution)/shard_map/ppermute | solution.py:48
  20.0 3.2 %collective-permute-start.7 = (bf16[1536,384]{1,0:T(8,128)(2,1)}, bf16[1536,384]{1,0:T(8,128)(2,1)}, u32[]{:S(2)}, u32[]{:S(2)}) collective-permute-start(bf16[1536,384]{1,0:T(8,128)(2,1)} %slice.3), channel_id=1, source_target_pairs={{0,12},{1,5},{2,14},{3,7},{4,0},{5,9},{6,2},{7,11},{8,4},{9,13},{1... | collective-permute-start | bytes 3538952 | tf_op jit(solution)/shard_map/ppermute | solution.py:30
  23.2 1.2 pad_maximum_fusion.p0
  24.4 2.0 %collective-permute-start.4 = (bf16[3,384,384]{2,1,0:T(8,128)(2,1)S(1)}, bf16[3,384,384]{2,1,0:T(8,128)(2,1)}, u32[]{:S(2)}, u32[]{:S(2)}) collective-permute-start(bf16[3,384,384]{2,1,0:T(8,128)(2,1)S(1)} %pad_maximum_fusion.p0), channel_id=1, source_target_pairs={{0,16},{1,113},{2,18},{3,115},{16,32},{17,1},{18,34},{19,3},{32,48... | collective-permute-start | bytes 2654216 | tf_op jit(solution)/shard_map/ppermute | solution.py:41
  26.4 4.0 %collective-permute-start.5 = (bf16[3,384,384]{2,1,0:T(8,128)(2,1)S(1)}, bf16[3,384,384]{2,1,0:T(8,128)(2,1)}, u32[]{:S(2)}, u32[]{:S(2)}) collective-permute-start(bf16[3,384,384]{2,1,0:T(8,128)(2,1)S(1)} %pad_maximum_fusion.p0), channel_id=1, source_target_pairs={{0,112},{1,17},{2,114},{3,19},{16,0},{17,33},{18,2},{19,35},{32,16... | collective-permute-start | bytes 2654216 | tf_op jit(solution)/shard_map/ppermute | solution.py:41
  30.4 1.1 constant_dynamic-slice_fusion
  31.5 13.4 %collective-permute-done.8.t2 = bf16[512,1536]{1,0:T(8,128)(2,1)} collective-permute-done((bf16[512,1536]{1,0:T(8,128)(2,1)}, bf16[512,1536]{1,0:T(8,128)(2,1)}, u32[]{:S(2)}, u32[]{:S(2)}) %collective-permute-start.8) | collective-permute-done | bytes 1572896 | tf_op jit(solution)/shard_map/ppermute | solution.py:53
  44.9 5.6 %collective-permute-done.4.p1 = bf16[3,384,384]{2,1,0:T(8,128)(2,1)} collective-permute-done((bf16[3,384,384]{2,1,0:T(8,128)(2,1)S(1)}, bf16[3,384,384]{2,1,0:T(8,128)(2,1)}, u32[]{:S(2)}, u32[]{:S(2)}) %collective-permute-start.4) | collective-permute-done | bytes 884768 | tf_op jit(solution)/shard_map/ppermute | solution.py:41
  50.8 1.3 %collective-permute-start.10 = (bf16[3,384,384]{2,1,0:T(8,128)(2,1)}, bf16[3,384,384]{2,1,0:T(8,128)(2,1)S(1)}, u32[]{:S(2)}, u32[]{:S(2)}) collective-permute-start(bf16[3,384,384]{2,1,0:T(8,128)(2,1)} %collective-permute-done.4.p1), channel_id=1, source_target_pairs={{0,16},{1,113},{2,18},{3,115},{16,32},{17,1},{18,34},{19,3},{32,48... | collective-permute-start | bytes 2654216 | tf_op jit(solution)/shard_map/ppermute | solution.py:41
  52.1 0.5 collective-permute-start.12
  52.6 1.6 %collective-permute-done.9.t3 = bf16[512,1536]{1,0:T(8,128)(2,1)S(1)} collective-permute-done((bf16[512,1536]{1,0:T(8,128)(2,1)}, bf16[512,1536]{1,0:T(8,128)(2,1)S(1)}, u32[]{:S(2)}, u32[]{:S(2)}) %collective-permute-start.9) | collective-permute-done | bytes 1572896 | tf_op jit(solution)/shard_map/ppermute | solution.py:53
  54.2 1.4 %copy-done.3 = bf16[512,1536]{1,0:T(8,128)(2,1)S(1)} copy-done((bf16[512,1536]{1,0:T(8,128)(2,1)S(1)}, bf16[512,1536]{1,0:T(8,128)(2,1)}, u32[]{:S(2)}) %copy-start.3) | copy-done | bytes 1572888
  55.6 2.0 %sort_tokens.1.t = bf16[4,512,1536]{2,1,0:T(8,128)(2,1)S(1)} custom-call(bf16[512,1536]{1,0:T(8,128)(2,1)S(1)} %copy-done.3, bf16[512,1536]{1,0:T(8,128)(2,1)} %collective-permute-done.3.t1, bf16[512,1536]{1,0:T(8,128)(2,1)} %collective-permute-done.8.t2, bf16[512,1536]{1,0:T(8,128)(2,1)S(1)} %collective-permute-done.9.t3), custom_call_target="tpu_custom_call" | custom-call | bytes 12582912 | tf_op jit(solution)/shard_map/sort_tokens/pallas_call | solution.py:130
  57.6 7.4 %up_part.1.so_far = f32[512,768]{1,0:T(8,128)S(1)} custom-call(bf16[4,512,1536]{2,1,0:T(8,128)(2,1)S(1)} %sort_tokens.1.t, bf16[1536,768]{1,0:T(8,128)(2,1)S(1)} %copy-done.1, bf16[1536,384]{1,0:T(8,128)(2,1)} %collective-permute-done.6.w1, bf16[1536,384]{1,0:T(8,128)(2,1)} %collective-permute-done.7.w3, bf16[3,384,384]{2,1,0:T(8,128)(2,1)S(1)} %pad_maximum_fusion.p0, ...), custom_call_target="tpu_custom_call" | custom-call | flops 3623878656 | bytes 11796480 | tf_op jit(solution)/shard_map/up_part/pallas_call | solution.py:184
  65.1 0.4 collective-permute-done.12.x0
  65.5 1.7 %collective-permute-done.10.p2 = bf16[3,384,384]{2,1,0:T(8,128)(2,1)S(1)} collective-permute-done((bf16[3,384,384]{2,1,0:T(8,128)(2,1)}, bf16[3,384,384]{2,1,0:T(8,128)(2,1)S(1)}, u32[]{:S(2)}, u32[]{:S(2)}) %collective-permute-start.10) | collective-permute-done | bytes 884768 | tf_op jit(solution)/shard_map/ppermute | solution.py:41
  67.2 1.1 collective-permute-done.11.w2
  68.4 2.8 %up_rest.1 = (bf16[512,768]{1,0:T(8,128)(2,1)}, bf16[512,768]{1,0:T(8,128)(2,1)S(1)}) custom-call(bf16[4,512,1536]{2,1,0:T(8,128)(2,1)S(1)} %sort_tokens.1.t, f32[512,768]{1,0:T(8,128)S(1)} %up_part.1.so_far, bf16[1536,384]{1,0:T(8,128)(2,1)S(1)} %collective-permute-done.11.w2, bf16[3,384,384]{2,1,0:T(8,128)(2,1)S(1)} %collective-permute-done.10.p2, ...), custom_call_target="tpu_custom_call" | custom-call | flops 1207959552 | bytes 3932160 | tf_op jit(solution)/shard_map/up_rest/pallas_call | solution.py:198
  71.2 1.2 collective-permute-start.13
  72.4 1.4 %collective-permute-start.14 = (bf16[768,384]{1,0:T(8,128)(2,1)S(1)}, bf16[768,384]{1,0:T(8,128)(2,1)S(1)}, u32[]{:S(2)}, u32[]{:S(2)}) collective-permute-start(bf16[768,384]{1,0:T(8,128)(2,1)S(1)} %collective-permute-done.12.x0), channel_id=1, source_target_pairs={{0,16},{1,113},{2,18},{3,115},{16,32},{17,1},{18,34},{19,3},{32,48... | collective-permute-start | bytes 1769480 | tf_op jit(solution)/shard_map/ppermute | solution.py:41
  73.8 3.3 %collective-permute-start.15 = (bf16[768,384]{1,0:T(8,128)(2,1)S(1)}, bf16[768,384]{1,0:T(8,128)(2,1)S(1)}, u32[]{:S(2)}, u32[]{:S(2)}) collective-permute-start(bf16[768,384]{1,0:T(8,128)(2,1)S(1)} %collective-permute-done.12.x0), channel_id=1, source_target_pairs={{0,112},{1,17},{2,114},{3,19},{16,0},{17,33},{18,2},{19,35},{32,16... | collective-permute-start | bytes 1769480 | tf_op jit(solution)/shard_map/ppermute | solution.py:41
  77.1 0.5 collective-permute-start.17
  77.6 11.3 %collective-permute-done.14.x1 = bf16[768,384]{1,0:T(8,128)(2,1)S(1)} collective-permute-done((bf16[768,384]{1,0:T(8,128)(2,1)S(1)}, bf16[768,384]{1,0:T(8,128)(2,1)S(1)}, u32[]{:S(2)}, u32[]{:S(2)}) %collective-permute-start.14) | collective-permute-done | bytes 589856 | tf_op jit(solution)/shard_map/ppermute | solution.py:41
  88.8 1.3 collective-permute-done.15.x3
  90.1 4.0 %collective-permute-done.13.rest_0_ = bf16[512,768]{1,0:T(8,128)(2,1)S(1)} collective-permute-done((bf16[512,768]{1,0:T(8,128)(2,1)S(1)}, bf16[512,768]{1,0:T(8,128)(2,1)S(1)}, u32[]{:S(2)}, u32[]{:S(2)}) %collective-permute-start.13) | collective-permute-done | bytes 786464 | tf_op jit(solution)/shard_map/ppermute | solution.py:66
  94.2 3.2 %collective-permute-start.19 = (bf16[512,768]{1,0:T(8,128)(2,1)S(1)}, bf16[512,768]{1,0:T(8,128)(2,1)S(1)}, u32[]{:S(2)}, u32[]{:S(2)}) collective-permute-start(bf16[512,768]{1,0:T(8,128)(2,1)S(1)} %collective-permute-done.13.rest_0_), channel_id=1, source_target_pairs={{0,12},{1,5},{2,14},{3,7},{4,0},{5,9},{6,2},{7,11},{8,4},{9,13},{1... | collective-permute-start | bytes 2359304 | tf_op jit(solution)/shard_map/ppermute | solution.py:30
  97.4 0.3 collective-permute-start.20
  97.7 0.7 collective-permute-start.21
  98.4 11.4 %collective-permute-done.20.x2 = bf16[768,384]{1,0:T(8,128)(2,1)S(1)} collective-permute-done((bf16[768,384]{1,0:T(8,128)(2,1)S(1)}, bf16[768,384]{1,0:T(8,128)(2,1)S(1)}, u32[]{:S(2)}, u32[]{:S(2)}) %collective-permute-start.20) | collective-permute-done | bytes 589856 | tf_op jit(solution)/shard_map/ppermute | solution.py:41
  109.8 5.7 %collective-permute-done.18.rest_1_ = bf16[512,768]{1,0:T(8,128)(2,1)S(1)} collective-permute-done((bf16[512,768]{1,0:T(8,128)(2,1)S(1)}, bf16[512,768]{1,0:T(8,128)(2,1)S(1)}, u32[]{:S(2)}, u32[]{:S(2)}) %collective-permute-start.18) | collective-permute-done | bytes 786464 | tf_op jit(solution)/shard_map/ppermute | solution.py:30
  115.6 0.3 collective-permute-start.24
  116.1 0.3 collective-permute-start.26
  116.5 1.0 collective-permute-done.23.c1
  117.4 0.8 collective-permute-done.24.c2
  118.3 0.8 collective-permute-done.25.c3
  119.1 0.8 collective-permute-done.26.y2
  120.0 1.2 sort_w.1.w
  121.2 4.2 %down.1.so_far = f32[512,1536]{1,0:T(8,128)S(1)} custom-call(bf16[4,768,1536]{2,1,0:T(8,128)(2,1)S(1)} %sort_w.1.w, bf16[512,768]{1,0:T(8,128)(2,1)S(1)} %collective-permute-done.13.rest_0_, bf16[512,768]{1,0:T(8,128)(2,1)S(1)} %collective-permute-done.18.rest_1_, bf16[512,768]{1,0:T(8,128)(2,1)S(1)} %collective-permute-done.19.rest_2_), custom_call_target="tpu_custom_call" | custom-call | flops 3623878656 | bytes 12582912 | tf_op jit(solution)/shard_map/down/pallas_call | solution.py:258
  125.3 4.3 %collective-permute-done.27.g = bf16[512,768]{1,0:T(8,128)(2,1)S(1)} collective-permute-done((bf16[512,768]{1,0:T(8,128)(2,1)S(1)}, bf16[512,768]{1,0:T(8,128)(2,1)S(1)}, u32[]{:S(2)}, u32[]{:S(2)}) %collective-permute-start.27) | collective-permute-done | bytes 786464 | tf_op jit(solution)/shard_map/ppermute | solution.py:30
  129.7 2.3 %down_last.1 = bf16[512,1536]{1,0:T(8,128)(2,1)} custom-call(bf16[4,768,1536]{2,1,0:T(8,128)(2,1)S(1)} %sort_w.1.w, bf16[512,768]{1,0:T(8,128)(2,1)S(1)} %collective-permute-done.27.g, f32[512,1536]{1,0:T(8,128)S(1)} %down.1.so_far), custom_call_target="tpu_custom_call" | custom-call | flops 1207959552 | bytes 4718592 | tf_op jit(solution)/shard_map/down_last/pallas_call | solution.py:284
  (42 shorter events, 1.0 us)
Async XLA Ops:
  0.6 19.3 %collective-permute-start.3 = (bf16[512,1536]{1,0:T(8,128)(2,1)}, bf16[512,1536]{1,0:T(8,128)(2,1)}, u32[]{:S(2)}, u32[]{:S(2)}) collective-permute-start(bf16[512,1536]{1,0:T(8,128)(2,1)} %t0.1), channel_id=1, source_target_pairs={{0,1},{1,0},{2,3},{3,2},{4,5},{5,4},{6,7},{7,6},{8,9},{9,8},{10,11... | collective-permute-start | bytes 4718600 | tf_op jit(solution)/shard_map/ppermute | solution.py:53
  0.7 1.7 %copy-start = (bf16[1536,768]{1,0:T(8,128)(2,1)S(1)}, bf16[1536,768]{1,0:T(8,128)(2,1)}, u32[]{:S(2)}) copy-start(bf16[1536,768]{1,0:T(8,128)(2,1)} %own.1) | copy-start | bytes 7077892
  2.4 6.5 %copy-start.1 = (bf16[1536,768]{1,0:T(8,128)(2,1)S(1)}, bf16[1536,768]{1,0:T(8,128)(2,1)}, u32[]{:S(2)}) copy-start(bf16[1536,768]{1,0:T(8,128)(2,1)} %own.1) | copy-start | bytes 7077892
  2.5 13.0 %collective-permute-start = (bf16[384,384]{1,0:T(8,128)(2,1)S(1)}, bf16[384,384]{1,0:T(8,128)(2,1)S(1)}, u32[]{:S(2)}, u32[]{:S(2)}) collective-permute-start(bf16[384,384]{1,0:T(8,128)(2,1)S(1)} %cut.1), channel_id=1, source_target_pairs={{0,4},{1,13},{2,6},{3,15},{4,8},{5,1},{6,10},{7,3},{8,12},{9,5},{1... | collective-permute-start | bytes 884744 | tf_op jit(solution)/shard_map/ppermute | solution.py:30
  4.1 15.8 %collective-permute-start.1 = (bf16[384,384]{1,0:T(8,128)(2,1)S(1)}, bf16[384,384]{1,0:T(8,128)(2,1)S(1)}, u32[]{:S(2)}, u32[]{:S(2)}) collective-permute-start(bf16[384,384]{1,0:T(8,128)(2,1)S(1)} %cut.1), channel_id=1, source_target_pairs={{0,8},{4,12},{8,0},{12,4},{1,9},{5,13},{9,1},{13,5},{2,10},{6,14},... | collective-permute-start | bytes 884744 | tf_op jit(solution)/shard_map/ppermute | solution.py:48
  7.0 12.9 %collective-permute-start.2 = (bf16[384,384]{1,0:T(8,128)(2,1)S(1)}, bf16[384,384]{1,0:T(8,128)(2,1)S(1)}, u32[]{:S(2)}, u32[]{:S(2)}) collective-permute-start(bf16[384,384]{1,0:T(8,128)(2,1)S(1)} %cut.1), channel_id=1, source_target_pairs={{0,12},{1,5},{2,14},{3,7},{4,0},{5,9},{6,2},{7,11},{8,4},{9,13},{1... | collective-permute-start | bytes 884744 | tf_op jit(solution)/shard_map/ppermute | solution.py:30
  8.4 36.6 %collective-permute-start.8 = (bf16[512,1536]{1,0:T(8,128)(2,1)}, bf16[512,1536]{1,0:T(8,128)(2,1)}, u32[]{:S(2)}, u32[]{:S(2)}) collective-permute-start(bf16[512,1536]{1,0:T(8,128)(2,1)} %t0.1), channel_id=1, source_target_pairs={{0,2},{1,3},{2,0},{3,1},{4,6},{5,7},{6,4},{7,5},{8,10},{9,11},{10,... | collective-permute-start | bytes 4718600 | tf_op jit(solution)/shard_map/ppermute | solution.py:53
  19.9 3.3 %copy-start.9 = (bf16[384,384]{1,0:T(8,128)(2,1)}, bf16[384,384]{1,0:T(8,128)(2,1)S(1)}, u32[]{:S(2)}) copy-start(bf16[384,384]{1,0:T(8,128)(2,1)S(1)} %collective-permute-done.1) | copy-start | bytes 884740
  19.9 3.3 %copy-start.10 = (bf16[384,384]{1,0:T(8,128)(2,1)}, bf16[384,384]{1,0:T(8,128)(2,1)S(1)}, u32[]{:S(2)}) copy-start(bf16[384,384]{1,0:T(8,128)(2,1)S(1)} %collective-permute-done.2) | copy-start | bytes 884740
  19.9 30.6 %collective-permute-start.6 = (bf16[1536,384]{1,0:T(8,128)(2,1)}, bf16[1536,384]{1,0:T(8,128)(2,1)}, u32[]{:S(2)}, u32[]{:S(2)}) collective-permute-start(bf16[1536,384]{1,0:T(8,128)(2,1)} %slice.3), channel_id=1, source_target_pairs={{0,4},{1,13},{2,6},{3,15},{4,8},{5,1},{6,10},{7,3},{8,12},{9,5},{1... | collective-permute-start | bytes 3538952 | tf_op jit(solution)/shard_map/ppermute | solution.py:30
  20.0 30.5 %collective-permute-start.7 = (bf16[1536,384]{1,0:T(8,128)(2,1)}, bf16[1536,384]{1,0:T(8,128)(2,1)}, u32[]{:S(2)}, u32[]{:S(2)}) collective-permute-start(bf16[1536,384]{1,0:T(8,128)(2,1)} %slice.3), channel_id=1, source_target_pairs={{0,12},{1,5},{2,14},{3,7},{4,0},{5,9},{6,2},{7,11},{8,4},{9,13},{1... | collective-permute-start | bytes 3538952 | tf_op jit(solution)/shard_map/ppermute | solution.py:30
  24.4 26.1 %collective-permute-start.4 = (bf16[3,384,384]{2,1,0:T(8,128)(2,1)S(1)}, bf16[3,384,384]{2,1,0:T(8,128)(2,1)}, u32[]{:S(2)}, u32[]{:S(2)}) collective-permute-start(bf16[3,384,384]{2,1,0:T(8,128)(2,1)S(1)} %pad_maximum_fusion.p0), channel_id=1, source_target_pairs={{0,16},{1,113},{2,18},{3,115},{16,32},{17,1},{18,34},{19,3},{32,48... | collective-permute-start | bytes 2654216 | tf_op jit(solution)/shard_map/ppermute | solution.py:41
  26.4 24.1 %collective-permute-start.5 = (bf16[3,384,384]{2,1,0:T(8,128)(2,1)S(1)}, bf16[3,384,384]{2,1,0:T(8,128)(2,1)}, u32[]{:S(2)}, u32[]{:S(2)}) collective-permute-start(bf16[3,384,384]{2,1,0:T(8,128)(2,1)S(1)} %pad_maximum_fusion.p0), channel_id=1, source_target_pairs={{0,112},{1,17},{2,114},{3,19},{16,0},{17,33},{18,2},{19,35},{32,16... | collective-permute-start | bytes 2654216 | tf_op jit(solution)/shard_map/ppermute | solution.py:41
  50.5 3.7 %collective-permute-start.9 = (bf16[512,1536]{1,0:T(8,128)(2,1)}, bf16[512,1536]{1,0:T(8,128)(2,1)S(1)}, u32[]{:S(2)}, u32[]{:S(2)}) collective-permute-start(bf16[512,1536]{1,0:T(8,128)(2,1)} %collective-permute-done.8.t2), channel_id=1, source_target_pairs={{0,1},{1,0},{2,3},{3,2},{4,5},{5,4},{6,7},{7,6},{8,9},{9,8},{10,11... | collective-permute-start | bytes 4718600 | tf_op jit(solution)/shard_map/ppermute | solution.py:53
  50.8 17.6 %collective-permute-start.11 = (bf16[1536,384]{1,0:T(8,128)(2,1)}, bf16[1536,384]{1,0:T(8,128)(2,1)S(1)}, u32[]{:S(2)}, u32[]{:S(2)}) collective-permute-start(bf16[1536,384]{1,0:T(8,128)(2,1)} %collective-permute-done.6.w1), channel_id=1, source_target_pairs={{0,4},{1,13},{2,6},{3,15},{4,8},{5,1},{6,10},{7,3},{8,12},{9,5},{1... | collective-permute-start | bytes 3538952 | tf_op jit(solution)/shard_map/ppermute | solution.py:30
  50.8 16.5 %collective-permute-start.10 = (bf16[3,384,384]{2,1,0:T(8,128)(2,1)}, bf16[3,384,384]{2,1,0:T(8,128)(2,1)S(1)}, u32[]{:S(2)}, u32[]{:S(2)}) collective-permute-start(bf16[3,384,384]{2,1,0:T(8,128)(2,1)} %collective-permute-done.4.p1), channel_id=1, source_target_pairs={{0,16},{1,113},{2,18},{3,115},{16,32},{17,1},{18,34},{19,3},{32,48... | collective-permute-start | bytes 2654216 | tf_op jit(solution)/shard_map/ppermute | solution.py:41
  52.1 13.5 %collective-permute-start.12 = (bf16[768,384]{1,0:T(8,128)(2,1)S(1)}, bf16[768,384]{1,0:T(8,128)(2,1)S(1)}, u32[]{:S(2)}, u32[]{:S(2)}) collective-permute-start(bf16[768,384]{1,0:T(8,128)(2,1)S(1)} %constant_dynamic-slice_fusion), channel_id=1, source_target_pairs={{0,2},{1,3},{2,0},{3,1},{4,6},{5,7},{6,4},{7,5},{8,10},{9,11},{10,... | collective-permute-start | bytes 1769480 | tf_op jit(solution)/shard_map/ppermute | solution.py:53
  54.2 1.4 %copy-start.3 = (bf16[512,1536]{1,0:T(8,128)(2,1)S(1)}, bf16[512,1536]{1,0:T(8,128)(2,1)}, u32[]{:S(2)}) copy-start(bf16[512,1536]{1,0:T(8,128)(2,1)} %t0.1) | copy-start | bytes 4718596
  57.6 10.8 %copy-start.4 = (bf16[512,768]{1,0:T(8,128)(2,1)S(1)}, bf16[512,768]{1,0:T(8,128)(2,1)}, u32[]{:S(2)}) copy-start(bf16[512,768]{1,0:T(8,128)(2,1)} %cot.1) | copy-start | bytes 2359300
  65.1 12.0 %copy-start.8 = (bf16[192,1536]{1,0:T(8,128)(2,1)S(1)}, bf16[192,1536]{1,0:T(8,128)(2,1)}, u32[]{:S(2)}) copy-start(bf16[192,1536]{1,0:T(8,128)(2,1)} %get-tuple-element.71) | copy-start | bytes 1769476
  65.1 50.4 %copy-start.7 = (bf16[192,1536]{1,0:T(8,128)(2,1)S(1)}, bf16[192,1536]{1,0:T(8,128)(2,1)}, u32[]{:S(2)}) copy-start(bf16[192,1536]{1,0:T(8,128)(2,1)} %get-tuple-element.79) | copy-start | bytes 1769476
  65.1 50.5 %copy-start.6 = (bf16[192,1536]{1,0:T(8,128)(2,1)S(1)}, bf16[192,1536]{1,0:T(8,128)(2,1)}, u32[]{:S(2)}) copy-start(bf16[192,1536]{1,0:T(8,128)(2,1)} %get-tuple-element.80) | copy-start | bytes 1769476
  65.1 50.9 %copy-start.5 = (bf16[192,1536]{1,0:T(8,128)(2,1)S(1)}, bf16[192,1536]{1,0:T(8,128)(2,1)}, u32[]{:S(2)}) copy-start(bf16[192,1536]{1,0:T(8,128)(2,1)} %get-tuple-element.81) | copy-start | bytes 1769476
  68.4 51.6 %copy-start.2 = (bf16[1536,768]{0,1:T(8,128)(2,1)S(1)}, bf16[1536,768]{0,1:T(8,128)(2,1)}, u32[]{:S(2)}) copy-start(bf16[1536,768]{0,1:T(8,128)(2,1)} %copy.5) | copy-start | bytes 7077892
  71.2 22.9 %collective-permute-start.13 = (bf16[512,768]{1,0:T(8,128)(2,1)S(1)}, bf16[512,768]{1,0:T(8,128)(2,1)S(1)}, u32[]{:S(2)}, u32[]{:S(2)}) collective-permute-start(bf16[512,768]{1,0:T(8,128)(2,1)S(1)} %get-tuple-element.69), channel_id=1, source_target_pairs={{0,12},{1,4},{2,0},{3,8},{4,1},{5,9},{6,5},{7,13},{8,10},{9,2},{10... | collective-permute-start | bytes 2359304 | tf_op jit(solution)/shard_map/ppermute | solution.py:66
  72.4 16.4 %collective-permute-start.14 = (bf16[768,384]{1,0:T(8,128)(2,1)S(1)}, bf16[768,384]{1,0:T(8,128)(2,1)S(1)}, u32[]{:S(2)}, u32[]{:S(2)}) collective-permute-start(bf16[768,384]{1,0:T(8,128)(2,1)S(1)} %collective-permute-done.12.x0), channel_id=1, source_target_pairs={{0,16},{1,113},{2,18},{3,115},{16,32},{17,1},{18,34},{19,3},{32,48... | collective-permute-start | bytes 1769480 | tf_op jit(solution)/shard_map/ppermute | solution.py:41
  73.8 16.4 %collective-permute-start.15 = (bf16[768,384]{1,0:T(8,128)(2,1)S(1)}, bf16[768,384]{1,0:T(8,128)(2,1)S(1)}, u32[]{:S(2)}, u32[]{:S(2)}) collective-permute-start(bf16[768,384]{1,0:T(8,128)(2,1)S(1)} %collective-permute-done.12.x0), channel_id=1, source_target_pairs={{0,112},{1,17},{2,114},{3,19},{16,0},{17,33},{18,2},{19,35},{32,16... | collective-permute-start | bytes 1769480 | tf_op jit(solution)/shard_map/ppermute | solution.py:41
  77.0 13.1 %collective-permute-start.16 = (bf16[768,384]{1,0:T(8,128)(2,1)S(1)}, bf16[768,384]{1,0:T(8,128)(2,1)S(1)}, u32[]{:S(2)}, u32[]{:S(2)}) collective-permute-start(bf16[768,384]{1,0:T(8,128)(2,1)S(1)} %collective-permute-done.12.x0), channel_id=1, source_target_pairs={{0,1},{1,0},{2,3},{3,2},{4,5},{5,4},{6,7},{7,6},{8,9},{9,8},{10,11... | collective-permute-start | bytes 1769480 | tf_op jit(solution)/shard_map/ppermute | solution.py:53
  77.1 13.0 %collective-permute-start.17 = (bf16[192,1536]{1,0:T(8,128)(2,1)S(1)}, bf16[192,1536]{1,0:T(8,128)(2,1)S(1)}, u32[]{:S(2)}, u32[]{:S(2)}) collective-permute-start(bf16[192,1536]{1,0:T(8,128)(2,1)S(1)} %copy-done.8), channel_id=1, source_target_pairs={{0,1},{1,0},{2,3},{3,2},{4,5},{5,4},{6,7},{7,6},{8,9},{9,8},{10,11... | collective-permute-start | bytes 1769480 | tf_op jit(solution)/shard_map/ppermute | solution.py:53
  94.2 21.3 %collective-permute-start.18 = (bf16[512,768]{1,0:T(8,128)(2,1)S(1)}, bf16[512,768]{1,0:T(8,128)(2,1)S(1)}, u32[]{:S(2)}, u32[]{:S(2)}) collective-permute-start(bf16[512,768]{1,0:T(8,128)(2,1)S(1)} %collective-permute-done.13.rest_0_), channel_id=1, source_target_pairs={{0,4},{1,13},{2,6},{3,15},{4,8},{5,1},{6,10},{7,3},{8,12},{9,5},{1... | collective-permute-start | bytes 2359304 | tf_op jit(solution)/shard_map/ppermute | solution.py:30
  94.2 21.3 %collective-permute-start.19 = (bf16[512,768]{1,0:T(8,128)(2,1)S(1)}, bf16[512,768]{1,0:T(8,128)(2,1)S(1)}, u32[]{:S(2)}, u32[]{:S(2)}) collective-permute-start(bf16[512,768]{1,0:T(8,128)(2,1)S(1)} %collective-permute-done.13.rest_0_), channel_id=1, source_target_pairs={{0,12},{1,5},{2,14},{3,7},{4,0},{5,9},{6,2},{7,11},{8,4},{9,13},{1... | collective-permute-start | bytes 2359304 | tf_op jit(solution)/shard_map/ppermute | solution.py:30
  97.4 12.4 %collective-permute-start.20 = (bf16[768,384]{1,0:T(8,128)(2,1)S(1)}, bf16[768,384]{1,0:T(8,128)(2,1)S(1)}, u32[]{:S(2)}, u32[]{:S(2)}) collective-permute-start(bf16[768,384]{1,0:T(8,128)(2,1)S(1)} %collective-permute-done.14.x1), channel_id=1, source_target_pairs={{0,16},{1,113},{2,18},{3,115},{16,32},{17,1},{18,34},{19,3},{32,48... | collective-permute-start | bytes 1769480 | tf_op jit(solution)/shard_map/ppermute | solution.py:41
  97.7 12.0 %collective-permute-start.21 = (bf16[768,384]{1,0:T(8,128)(2,1)S(1)}, bf16[768,384]{1,0:T(8,128)(2,1)S(1)}, u32[]{:S(2)}, u32[]{:S(2)}) collective-permute-start(bf16[768,384]{1,0:T(8,128)(2,1)S(1)} %collective-permute-done.14.x1), channel_id=1, source_target_pairs={{0,1},{1,0},{2,3},{3,2},{4,5},{5,4},{6,7},{7,6},{8,9},{9,8},{10,11... | collective-permute-start | bytes 1769480 | tf_op jit(solution)/shard_map/ppermute | solution.py:53
  98.4 11.4 %collective-permute-start.22 = (bf16[768,384]{1,0:T(8,128)(2,1)S(1)}, bf16[768,384]{1,0:T(8,128)(2,1)S(1)}, u32[]{:S(2)}, u32[]{:S(2)}) collective-permute-start(bf16[768,384]{1,0:T(8,128)(2,1)S(1)} %collective-permute-done.15.x3), channel_id=1, source_target_pairs={{0,1},{1,0},{2,3},{3,2},{4,5},{5,4},{6,7},{7,6},{8,9},{9,8},{10,11... | collective-permute-start | bytes 1769480 | tf_op jit(solution)/shard_map/ppermute | solution.py:53
  115.4 2.0 %collective-permute-start.23 = (bf16[192,1536]{1,0:T(8,128)(2,1)S(1)}, bf16[192,1536]{1,0:T(8,128)(2,1)S(1)}, u32[]{:S(2)}, u32[]{:S(2)}) collective-permute-start(bf16[192,1536]{1,0:T(8,128)(2,1)S(1)} %copy-done.7), channel_id=1, source_target_pairs={{0,1},{1,0},{2,3},{3,2},{4,5},{5,4},{6,7},{7,6},{8,9},{9,8},{10,11... | collective-permute-start | bytes 1769480 | tf_op jit(solution)/shard_map/ppermute | solution.py:53
  115.6 2.7 %collective-permute-start.24 = (bf16[192,1536]{1,0:T(8,128)(2,1)S(1)}, bf16[192,1536]{1,0:T(8,128)(2,1)S(1)}, u32[]{:S(2)}, u32[]{:S(2)}) collective-permute-start(bf16[192,1536]{1,0:T(8,128)(2,1)S(1)} %copy-done.6), channel_id=1, source_target_pairs={{0,1},{1,0},{2,3},{3,2},{4,5},{5,4},{6,7},{7,6},{8,9},{9,8},{10,11... | collective-permute-start | bytes 1769480 | tf_op jit(solution)/shard_map/ppermute | solution.py:53
  116.0 3.2 %collective-permute-start.25 = (bf16[192,1536]{1,0:T(8,128)(2,1)S(1)}, bf16[192,1536]{1,0:T(8,128)(2,1)S(1)}, u32[]{:S(2)}, u32[]{:S(2)}) collective-permute-start(bf16[192,1536]{1,0:T(8,128)(2,1)S(1)} %copy-done.5), channel_id=1, source_target_pairs={{0,1},{1,0},{2,3},{3,2},{4,5},{5,4},{6,7},{7,6},{8,9},{9,8},{10,11... | collective-permute-start | bytes 1769480 | tf_op jit(solution)/shard_map/ppermute | solution.py:53
  116.1 3.8 %collective-permute-start.26 = (bf16[768,384]{1,0:T(8,128)(2,1)S(1)}, bf16[768,384]{1,0:T(8,128)(2,1)S(1)}, u32[]{:S(2)}, u32[]{:S(2)}) collective-permute-start(bf16[768,384]{1,0:T(8,128)(2,1)S(1)} %collective-permute-done.20.x2), channel_id=1, source_target_pairs={{0,1},{1,0},{2,3},{3,2},{4,5},{5,4},{6,7},{7,6},{8,9},{9,8},{10,11... | collective-permute-start | bytes 1769480 | tf_op jit(solution)/shard_map/ppermute | solution.py:53
  116.5 13.2 %collective-permute-start.27 = (bf16[512,768]{1,0:T(8,128)(2,1)S(1)}, bf16[512,768]{1,0:T(8,128)(2,1)S(1)}, u32[]{:S(2)}, u32[]{:S(2)}) collective-permute-start(bf16[512,768]{1,0:T(8,128)(2,1)S(1)} %collective-permute-done.18.rest_1_), channel_id=1, source_target_pairs={{0,4},{1,13},{2,6},{3,15},{4,8},{5,1},{6,10},{7,3},{8,12},{9,5},{1... | collective-permute-start | bytes 2359304 | tf_op jit(solution)/shard_map/ppermute | solution.py:30

commit v5 on v4

--- a/solution.py
+++ b/solution.py
@@ -79,10 +79,9 @@
 
 def gelu_parts(pre):
     sq = pre * pre
-    t = jnp.tanh(COEFF * (pre + 0.044715 * sq * pre))
-    hidden = 0.5 * pre * (1.0 + t)
-    slope = 0.5 * (1.0 + t) + 0.5 * pre * (1.0 - t * t) * COEFF * (1.0 + 3.0 * 0.044715 * sq)
-    return hidden, slope
+    g = 0.5 + 0.5 * jnp.tanh(pre * (COEFF + 0.044715 * COEFF * sq))
+    slope = g * (1.0 + (1.0 - g) * (pre * (2.0 * COEFF + 6.0 * 0.044715 * COEFF * sq)))
+    return pre * g, slope
 
 
 def params():
@@ -231,7 +230,7 @@
         out_specs=VMEM,
         scratch_shapes=[pltpu.SemaphoreType.DMA],
         compiler_params=params(),
-        cost_estimate=cost(0, 16 * depth * ff),
+        cost_estimate=cost(0, 16 * depth),
         name="sort_w",
     )(*pieces)
 
@@ -261,7 +260,7 @@
         in_specs=[VMEM] * (1 + len(blocks) + len(more)),
         out_specs=VMEM,
         compiler_params=params(),
-        cost_estimate=cost(2 * len(blocks) * rows * depth * ff, 8 * ff * (rows + depth)),
+        cost_estimate=cost(2 * rows * depth, 8 * (rows + depth)),
         name="down",
     )(w, *blocks, *more)
 

time: 132 us -> 131 us (level)
  no operation moved by 1% of the time
where the time goes in v5:
time: 131 us
  waiting for transfers between devices  68.6 us (52%)
  starting transfers between devices  29.6 us (23%)
  Pallas kernels  19.8 us (15%)
  local copies, waits for them, and re-layouts  10.8 us (8%)
    ppermute x6, waiting for transfers between devices, z_step(): lax.ppermute(x, ('dp', 'col'), flat(sizes, lambda i, c: (i // n * n + (i...  31.2 us
    ppermute x12, waiting for transfers between devices, col_swap(): return lax.ppermute(x, 'col', [(i, i ^ m) for i in range(n)])  19 us
    ppermute x6, starting transfers between devices, z_step(): lax.ppermute(x, ('dp', 'col'), flat(sizes, lambda i, c: (i // n * n + (i...  12.3 us
    ppermute x8, waiting for transfers between devices, y_step(): lax.ppermute(x, ('row', 'col'), flat(sizes, lambda r, c: ((r + 1 - 2 * ((...  10 us
    ppermute x8, starting transfers between devices, y_step(): lax.ppermute(x, ('row', 'col'), flat(sizes, lambda r, c: ((r + 1 - 2 * ((...  9.55 us
    pallas_call x1, Pallas kernels, up_part(): pl.pallas_call(up_part_kernel, out_shape=jax.ShapeDtypeStruct((rows, widt...  7.43 us
    unnamed x23, local copies, waits for them, and re-layouts  5.54 us
    ppermute x1, waiting for transfers between devices, opposite(): return lax.ppermute(x, 'row', [(i, (i + 2) % n) for i in range(n)])  4.42 us
  transfers between devices with their start and end apart: 28, of which 17 were waited for; matrix products, arithmetic and copies ran while one was open for 7% of the time, Pallas kernels for 11%

profile of v5, /device:TPU:4, one launch (start us, length us, event | category | flops | bytes accessed | tf_op | source)
XLA Modules:
  0.0 131.0 jit_solution(18229625183766026867)
XLA Ops:
  0.7 1.7 %copy-done = bf16[1536,768]{1,0:T(8,128)(2,1)S(1)} copy-done((bf16[1536,768]{1,0:T(8,128)(2,1)S(1)}, bf16[1536,768]{1,0:T(8,128)(2,1)}, u32[]{:S(2)}) %copy-start) | copy-done | bytes 2359320
  2.5 1.7 %collective-permute-start = (bf16[384,384]{1,0:T(8,128)(2,1)S(1)}, bf16[384,384]{1,0:T(8,128)(2,1)S(1)}, u32[]{:S(2)}, u32[]{:S(2)}) collective-permute-start(bf16[384,384]{1,0:T(8,128)(2,1)S(1)} %cut.1), channel_id=1, source_target_pairs={{0,4},{1,13},{2,6},{3,15},{4,8},{5,1},{6,10},{7,3},{8,12},{9,5},{1... | collective-permute-start | bytes 884744 | tf_op jit(solution)/shard_map/ppermute | solution.py:30
  4.1 2.9 %collective-permute-start.1 = (bf16[384,384]{1,0:T(8,128)(2,1)S(1)}, bf16[384,384]{1,0:T(8,128)(2,1)S(1)}, u32[]{:S(2)}, u32[]{:S(2)}) collective-permute-start(bf16[384,384]{1,0:T(8,128)(2,1)S(1)} %cut.1), channel_id=1, source_target_pairs={{0,8},{4,12},{8,0},{12,4},{1,9},{5,13},{9,1},{13,5},{2,10},{6,14},... | collective-permute-start | bytes 884744 | tf_op jit(solution)/shard_map/ppermute | solution.py:48
  7.0 1.3 %collective-permute-start.2 = (bf16[384,384]{1,0:T(8,128)(2,1)S(1)}, bf16[384,384]{1,0:T(8,128)(2,1)S(1)}, u32[]{:S(2)}, u32[]{:S(2)}) collective-permute-start(bf16[384,384]{1,0:T(8,128)(2,1)S(1)} %cut.1), channel_id=1, source_target_pairs={{0,12},{1,5},{2,14},{3,7},{4,0},{5,9},{6,2},{7,11},{8,4},{9,13},{1... | collective-permute-start | bytes 884744 | tf_op jit(solution)/shard_map/ppermute | solution.py:30
  8.4 0.5 collective-permute-start.8
  8.9 1.1 slice.3
  10.0 2.4 %copy.5 = bf16[1536,768]{0,1:T(8,128)(2,1)} copy(bf16[1536,768]{1,0:T(8,128)(2,1)S(1)} %copy-done.1) | data formatting | bytes 4718592 | tf_op args[1]
  12.4 3.0 %fusion = (bf16[192,1536]{1,0:T(8,128)(2,1)}, bf16[192,1536]{1,0:T(8,128)(2,1)}, bf16[192,1536]{1,0:T(8,128)(2,1)}, bf16[192,1536]{1,0:T(8,128)(2,1)}) fusion(bf16[768,1536]{1,0:T(8,128)(2,1)} %bitcast.4), kind=kLoop, calls=%fused_computation.2 | loop fusion | bytes 4718592 | tf_op jit(solution)/shard_map/split | solution.py:310
  15.5 4.4 %collective-permute-done.1 = bf16[384,384]{1,0:T(8,128)(2,1)S(1)} collective-permute-done((bf16[384,384]{1,0:T(8,128)(2,1)S(1)}, bf16[384,384]{1,0:T(8,128)(2,1)S(1)}, u32[]{:S(2)}, u32[]{:S(2)}) %collective-permute-start.1) | collective-permute-done | bytes 294944 | tf_op jit(solution)/shard_map/ppermute | solution.py:48
  20.0 3.2 %collective-permute-start.7 = (bf16[1536,384]{1,0:T(8,128)(2,1)}, bf16[1536,384]{1,0:T(8,128)(2,1)}, u32[]{:S(2)}, u32[]{:S(2)}) collective-permute-start(bf16[1536,384]{1,0:T(8,128)(2,1)} %slice.3), channel_id=1, source_target_pairs={{0,12},{1,5},{2,14},{3,7},{4,0},{5,9},{6,2},{7,11},{8,4},{9,13},{1... | collective-permute-start | bytes 3538952 | tf_op jit(solution)/shard_map/ppermute | solution.py:30
  23.2 1.2 pad_maximum_fusion.p0
  24.4 2.0 %collective-permute-start.4 = (bf16[3,384,384]{2,1,0:T(8,128)(2,1)S(1)}, bf16[3,384,384]{2,1,0:T(8,128)(2,1)}, u32[]{:S(2)}, u32[]{:S(2)}) collective-permute-start(bf16[3,384,384]{2,1,0:T(8,128)(2,1)S(1)} %pad_maximum_fusion.p0), channel_id=1, source_target_pairs={{0,16},{1,113},{2,18},{3,115},{16,32},{17,1},{18,34},{19,3},{32,48... | collective-permute-start | bytes 2654216 | tf_op jit(solution)/shard_map/ppermute | solution.py:41
  26.4 4.0 %collective-permute-start.5 = (bf16[3,384,384]{2,1,0:T(8,128)(2,1)S(1)}, bf16[3,384,384]{2,1,0:T(8,128)(2,1)}, u32[]{:S(2)}, u32[]{:S(2)}) collective-permute-start(bf16[3,384,384]{2,1,0:T(8,128)(2,1)S(1)} %pad_maximum_fusion.p0), channel_id=1, source_target_pairs={{0,112},{1,17},{2,114},{3,19},{16,0},{17,33},{18,2},{19,35},{32,16... | collective-permute-start | bytes 2654216 | tf_op jit(solution)/shard_map/ppermute | solution.py:41
  30.4 1.1 constant_dynamic-slice_fusion
  31.5 13.4 %collective-permute-done.8.t2 = bf16[512,1536]{1,0:T(8,128)(2,1)} collective-permute-done((bf16[512,1536]{1,0:T(8,128)(2,1)}, bf16[512,1536]{1,0:T(8,128)(2,1)}, u32[]{:S(2)}, u32[]{:S(2)}) %collective-permute-start.8) | collective-permute-done | bytes 1572896 | tf_op jit(solution)/shard_map/ppermute | solution.py:53
  44.9 5.6 %collective-permute-done.4.p1 = bf16[3,384,384]{2,1,0:T(8,128)(2,1)} collective-permute-done((bf16[3,384,384]{2,1,0:T(8,128)(2,1)S(1)}, bf16[3,384,384]{2,1,0:T(8,128)(2,1)}, u32[]{:S(2)}, u32[]{:S(2)}) %collective-permute-start.4) | collective-permute-done | bytes 884768 | tf_op jit(solution)/shard_map/ppermute | solution.py:41
  50.8 1.3 %collective-permute-start.10 = (bf16[3,384,384]{2,1,0:T(8,128)(2,1)}, bf16[3,384,384]{2,1,0:T(8,128)(2,1)S(1)}, u32[]{:S(2)}, u32[]{:S(2)}) collective-permute-start(bf16[3,384,384]{2,1,0:T(8,128)(2,1)} %collective-permute-done.4.p1), channel_id=1, source_target_pairs={{0,16},{1,113},{2,18},{3,115},{16,32},{17,1},{18,34},{19,3},{32,48... | collective-permute-start | bytes 2654216 | tf_op jit(solution)/shard_map/ppermute | solution.py:41
  52.1 0.5 collective-permute-start.12
  52.6 1.6 %collective-permute-done.9.t3 = bf16[512,1536]{1,0:T(8,128)(2,1)S(1)} collective-permute-done((bf16[512,1536]{1,0:T(8,128)(2,1)}, bf16[512,1536]{1,0:T(8,128)(2,1)S(1)}, u32[]{:S(2)}, u32[]{:S(2)}) %collective-permute-start.9) | collective-permute-done | bytes 1572896 | tf_op jit(solution)/shard_map/ppermute | solution.py:53
  54.2 1.4 %copy-done.3 = bf16[512,1536]{1,0:T(8,128)(2,1)S(1)} copy-done((bf16[512,1536]{1,0:T(8,128)(2,1)S(1)}, bf16[512,1536]{1,0:T(8,128)(2,1)}, u32[]{:S(2)}) %copy-start.3) | copy-done | bytes 1572888
  55.6 2.0 %sort_tokens.1.t = bf16[4,512,1536]{2,1,0:T(8,128)(2,1)S(1)} custom-call(bf16[512,1536]{1,0:T(8,128)(2,1)S(1)} %copy-done.3, bf16[512,1536]{1,0:T(8,128)(2,1)} %collective-permute-done.3.t1, bf16[512,1536]{1,0:T(8,128)(2,1)} %collective-permute-done.8.t2, bf16[512,1536]{1,0:T(8,128)(2,1)S(1)} %collective-permute-done.9.t3), custom_call_target="tpu_custom_call" | custom-call | bytes 12582912 | tf_op jit(solution)/shard_map/sort_tokens/pallas_call | solution.py:129
  57.6 7.4 %up_part.1.so_far = f32[512,768]{1,0:T(8,128)S(1)} custom-call(bf16[4,512,1536]{2,1,0:T(8,128)(2,1)S(1)} %sort_tokens.1.t, bf16[1536,768]{1,0:T(8,128)(2,1)S(1)} %copy-done.1, bf16[1536,384]{1,0:T(8,128)(2,1)} %collective-permute-done.6.w1, bf16[1536,384]{1,0:T(8,128)(2,1)} %collective-permute-done.7.w3, bf16[3,384,384]{2,1,0:T(8,128)(2,1)S(1)} %pad_maximum_fusion.p0, ...), custom_call_target="tpu_custom_call" | custom-call | flops 3623878656 | bytes 11796480 | tf_op jit(solution)/shard_map/up_part/pallas_call | solution.py:183
  65.1 0.4 collective-permute-done.12.x0
  65.5 1.7 %collective-permute-done.10.p2 = bf16[3,384,384]{2,1,0:T(8,128)(2,1)S(1)} collective-permute-done((bf16[3,384,384]{2,1,0:T(8,128)(2,1)}, bf16[3,384,384]{2,1,0:T(8,128)(2,1)S(1)}, u32[]{:S(2)}, u32[]{:S(2)}) %collective-permute-start.10) | collective-permute-done | bytes 884768 | tf_op jit(solution)/shard_map/ppermute | solution.py:41
  67.2 1.1 collective-permute-done.11.w2
  68.4 2.7 %up_rest.1 = (bf16[512,768]{1,0:T(8,128)(2,1)}, bf16[512,768]{1,0:T(8,128)(2,1)S(1)}) custom-call(bf16[4,512,1536]{2,1,0:T(8,128)(2,1)S(1)} %sort_tokens.1.t, f32[512,768]{1,0:T(8,128)S(1)} %up_part.1.so_far, bf16[1536,384]{1,0:T(8,128)(2,1)S(1)} %collective-permute-done.11.w2, bf16[3,384,384]{2,1,0:T(8,128)(2,1)S(1)} %collective-permute-done.10.p2, ...), custom_call_target="tpu_custom_call" | custom-call | flops 1207959552 | bytes 3932160 | tf_op jit(solution)/shard_map/up_rest/pallas_call | solution.py:197
  71.1 1.2 collective-permute-start.13
  72.3 1.4 %collective-permute-start.14 = (bf16[768,384]{1,0:T(8,128)(2,1)S(1)}, bf16[768,384]{1,0:T(8,128)(2,1)S(1)}, u32[]{:S(2)}, u32[]{:S(2)}) collective-permute-start(bf16[768,384]{1,0:T(8,128)(2,1)S(1)} %collective-permute-done.12.x0), channel_id=1, source_target_pairs={{0,16},{1,113},{2,18},{3,115},{16,32},{17,1},{18,34},{19,3},{32,48... | collective-permute-start | bytes 1769480 | tf_op jit(solution)/shard_map/ppermute | solution.py:41
  73.7 3.3 %collective-permute-start.15 = (bf16[768,384]{1,0:T(8,128)(2,1)S(1)}, bf16[768,384]{1,0:T(8,128)(2,1)S(1)}, u32[]{:S(2)}, u32[]{:S(2)}) collective-permute-start(bf16[768,384]{1,0:T(8,128)(2,1)S(1)} %collective-permute-done.12.x0), channel_id=1, source_target_pairs={{0,112},{1,17},{2,114},{3,19},{16,0},{17,33},{18,2},{19,35},{32,16... | collective-permute-start | bytes 1769480 | tf_op jit(solution)/shard_map/ppermute | solution.py:41
  77.0 0.5 collective-permute-start.17
  77.5 11.3 %collective-permute-done.14.x1 = bf16[768,384]{1,0:T(8,128)(2,1)S(1)} collective-permute-done((bf16[768,384]{1,0:T(8,128)(2,1)S(1)}, bf16[768,384]{1,0:T(8,128)(2,1)S(1)}, u32[]{:S(2)}, u32[]{:S(2)}) %collective-permute-start.14) | collective-permute-done | bytes 589856 | tf_op jit(solution)/shard_map/ppermute | solution.py:41
  88.7 1.3 collective-permute-done.15.x3
  90.0 4.0 %collective-permute-done.13.rest_0_ = bf16[512,768]{1,0:T(8,128)(2,1)S(1)} collective-permute-done((bf16[512,768]{1,0:T(8,128)(2,1)S(1)}, bf16[512,768]{1,0:T(8,128)(2,1)S(1)}, u32[]{:S(2)}, u32[]{:S(2)}) %collective-permute-start.13) | collective-permute-done | bytes 786464 | tf_op jit(solution)/shard_map/ppermute | solution.py:66
  94.1 3.2 %collective-permute-start.19 = (bf16[512,768]{1,0:T(8,128)(2,1)S(1)}, bf16[512,768]{1,0:T(8,128)(2,1)S(1)}, u32[]{:S(2)}, u32[]{:S(2)}) collective-permute-start(bf16[512,768]{1,0:T(8,128)(2,1)S(1)} %collective-permute-done.13.rest_0_), channel_id=1, source_target_pairs={{0,12},{1,5},{2,14},{3,7},{4,0},{5,9},{6,2},{7,11},{8,4},{9,13},{1... | collective-permute-start | bytes 2359304 | tf_op jit(solution)/shard_map/ppermute | solution.py:30
  97.3 0.3 collective-permute-start.20
  97.6 0.6 collective-permute-start.21
  98.3 11.4 %collective-permute-done.20.x2 = bf16[768,384]{1,0:T(8,128)(2,1)S(1)} collective-permute-done((bf16[768,384]{1,0:T(8,128)(2,1)S(1)}, bf16[768,384]{1,0:T(8,128)(2,1)S(1)}, u32[]{:S(2)}, u32[]{:S(2)}) %collective-permute-start.20) | collective-permute-done | bytes 589856 | tf_op jit(solution)/shard_map/ppermute | solution.py:41
  109.7 5.7 %collective-permute-done.18.rest_1_ = bf16[512,768]{1,0:T(8,128)(2,1)S(1)} collective-permute-done((bf16[512,768]{1,0:T(8,128)(2,1)S(1)}, bf16[512,768]{1,0:T(8,128)(2,1)S(1)}, u32[]{:S(2)}, u32[]{:S(2)}) %collective-permute-start.18) | collective-permute-done | bytes 786464 | tf_op jit(solution)/shard_map/ppermute | solution.py:30
  115.5 0.4 collective-permute-start.24
  116.1 0.4 collective-permute-start.26
  116.5 1.0 collective-permute-done.23.c1
  117.4 0.8 collective-permute-done.24.c2
  118.3 0.8 collective-permute-done.25.c3
  119.1 0.8 collective-permute-done.26.y2
  120.0 1.2 sort_w.1.w
  121.2 4.2 %down.1.so_far = f32[512,1536]{1,0:T(8,128)S(1)} custom-call(bf16[4,768,1536]{2,1,0:T(8,128)(2,1)S(1)} %sort_w.1.w, bf16[512,768]{1,0:T(8,128)(2,1)S(1)} %collective-permute-done.13.rest_0_, bf16[512,768]{1,0:T(8,128)(2,1)S(1)} %collective-permute-done.18.rest_1_, bf16[512,768]{1,0:T(8,128)(2,1)S(1)} %collective-permute-done.19.rest_2_), custom_call_target="tpu_custom_call" | custom-call | flops 1572864 | bytes 16384 | tf_op jit(solution)/shard_map/down/pallas_call | solution.py:257
  125.3 3.2 %collective-permute-done.27.g = bf16[512,768]{1,0:T(8,128)(2,1)S(1)} collective-permute-done((bf16[512,768]{1,0:T(8,128)(2,1)S(1)}, bf16[512,768]{1,0:T(8,128)(2,1)S(1)}, u32[]{:S(2)}, u32[]{:S(2)}) %collective-permute-start.27) | collective-permute-done | bytes 786464 | tf_op jit(solution)/shard_map/ppermute | solution.py:30
  128.5 2.3 %down_last.1 = bf16[512,1536]{1,0:T(8,128)(2,1)} custom-call(bf16[4,768,1536]{2,1,0:T(8,128)(2,1)S(1)} %sort_w.1.w, bf16[512,768]{1,0:T(8,128)(2,1)S(1)} %collective-permute-done.27.g, f32[512,1536]{1,0:T(8,128)S(1)} %down.1.so_far), custom_call_target="tpu_custom_call" | custom-call | flops 1207959552 | bytes 4718592 | tf_op jit(solution)/shard_map/down_last/pallas_call | solution.py:283
  (42 shorter events, 0.9 us)
Async XLA Ops:
  0.6 19.3 %collective-permute-start.3 = (bf16[512,1536]{1,0:T(8,128)(2,1)}, bf16[512,1536]{1,0:T(8,128)(2,1)}, u32[]{:S(2)}, u32[]{:S(2)}) collective-permute-start(bf16[512,1536]{1,0:T(8,128)(2,1)} %t0.1), channel_id=1, source_target_pairs={{0,1},{1,0},{2,3},{3,2},{4,5},{5,4},{6,7},{7,6},{8,9},{9,8},{10,11... | collective-permute-start | bytes 4718600 | tf_op jit(solution)/shard_map/ppermute | solution.py:53
  0.7 1.7 %copy-start = (bf16[1536,768]{1,0:T(8,128)(2,1)S(1)}, bf16[1536,768]{1,0:T(8,128)(2,1)}, u32[]{:S(2)}) copy-start(bf16[1536,768]{1,0:T(8,128)(2,1)} %own.1) | copy-start | bytes 7077892
  2.4 6.5 %copy-start.1 = (bf16[1536,768]{1,0:T(8,128)(2,1)S(1)}, bf16[1536,768]{1,0:T(8,128)(2,1)}, u32[]{:S(2)}) copy-start(bf16[1536,768]{1,0:T(8,128)(2,1)} %own.1) | copy-start | bytes 7077892
  2.5 13.0 %collective-permute-start = (bf16[384,384]{1,0:T(8,128)(2,1)S(1)}, bf16[384,384]{1,0:T(8,128)(2,1)S(1)}, u32[]{:S(2)}, u32[]{:S(2)}) collective-permute-start(bf16[384,384]{1,0:T(8,128)(2,1)S(1)} %cut.1), channel_id=1, source_target_pairs={{0,4},{1,13},{2,6},{3,15},{4,8},{5,1},{6,10},{7,3},{8,12},{9,5},{1... | collective-permute-start | bytes 884744 | tf_op jit(solution)/shard_map/ppermute | solution.py:30
  4.1 15.8 %collective-permute-start.1 = (bf16[384,384]{1,0:T(8,128)(2,1)S(1)}, bf16[384,384]{1,0:T(8,128)(2,1)S(1)}, u32[]{:S(2)}, u32[]{:S(2)}) collective-permute-start(bf16[384,384]{1,0:T(8,128)(2,1)S(1)} %cut.1), channel_id=1, source_target_pairs={{0,8},{4,12},{8,0},{12,4},{1,9},{5,13},{9,1},{13,5},{2,10},{6,14},... | collective-permute-start | bytes 884744 | tf_op jit(solution)/shard_map/ppermute | solution.py:48
  7.0 12.9 %collective-permute-start.2 = (bf16[384,384]{1,0:T(8,128)(2,1)S(1)}, bf16[384,384]{1,0:T(8,128)(2,1)S(1)}, u32[]{:S(2)}, u32[]{:S(2)}) collective-permute-start(bf16[384,384]{1,0:T(8,128)(2,1)S(1)} %cut.1), channel_id=1, source_target_pairs={{0,12},{1,5},{2,14},{3,7},{4,0},{5,9},{6,2},{7,11},{8,4},{9,13},{1... | collective-permute-start | bytes 884744 | tf_op jit(solution)/shard_map/ppermute | solution.py:30
  8.4 36.6 %collective-permute-start.8 = (bf16[512,1536]{1,0:T(8,128)(2,1)}, bf16[512,1536]{1,0:T(8,128)(2,1)}, u32[]{:S(2)}, u32[]{:S(2)}) collective-permute-start(bf16[512,1536]{1,0:T(8,128)(2,1)} %t0.1), channel_id=1, source_target_pairs={{0,2},{1,3},{2,0},{3,1},{4,6},{5,7},{6,4},{7,5},{8,10},{9,11},{10,... | collective-permute-start | bytes 4718600 | tf_op jit(solution)/shard_map/ppermute | solution.py:53
  19.9 3.3 %copy-start.9 = (bf16[384,384]{1,0:T(8,128)(2,1)}, bf16[384,384]{1,0:T(8,128)(2,1)S(1)}, u32[]{:S(2)}) copy-start(bf16[384,384]{1,0:T(8,128)(2,1)S(1)} %collective-permute-done.1) | copy-start | bytes 884740
  19.9 3.3 %copy-start.10 = (bf16[384,384]{1,0:T(8,128)(2,1)}, bf16[384,384]{1,0:T(8,128)(2,1)S(1)}, u32[]{:S(2)}) copy-start(bf16[384,384]{1,0:T(8,128)(2,1)S(1)} %collective-permute-done.2) | copy-start | bytes 884740
  19.9 30.6 %collective-permute-start.6 = (bf16[1536,384]{1,0:T(8,128)(2,1)}, bf16[1536,384]{1,0:T(8,128)(2,1)}, u32[]{:S(2)}, u32[]{:S(2)}) collective-permute-start(bf16[1536,384]{1,0:T(8,128)(2,1)} %slice.3), channel_id=1, source_target_pairs={{0,4},{1,13},{2,6},{3,15},{4,8},{5,1},{6,10},{7,3},{8,12},{9,5},{1... | collective-permute-start | bytes 3538952 | tf_op jit(solution)/shard_map/ppermute | solution.py:30
  20.0 30.5 %collective-permute-start.7 = (bf16[1536,384]{1,0:T(8,128)(2,1)}, bf16[1536,384]{1,0:T(8,128)(2,1)}, u32[]{:S(2)}, u32[]{:S(2)}) collective-permute-start(bf16[1536,384]{1,0:T(8,128)(2,1)} %slice.3), channel_id=1, source_target_pairs={{0,12},{1,5},{2,14},{3,7},{4,0},{5,9},{6,2},{7,11},{8,4},{9,13},{1... | collective-permute-start | bytes 3538952 | tf_op jit(solution)/shard_map/ppermute | solution.py:30
  24.4 26.1 %collective-permute-start.4 = (bf16[3,384,384]{2,1,0:T(8,128)(2,1)S(1)}, bf16[3,384,384]{2,1,0:T(8,128)(2,1)}, u32[]{:S(2)}, u32[]{:S(2)}) collective-permute-start(bf16[3,384,384]{2,1,0:T(8,128)(2,1)S(1)} %pad_maximum_fusion.p0), channel_id=1, source_target_pairs={{0,16},{1,113},{2,18},{3,115},{16,32},{17,1},{18,34},{19,3},{32,48... | collective-permute-start | bytes 2654216 | tf_op jit(solution)/shard_map/ppermute | solution.py:41
  26.4 24.1 %collective-permute-start.5 = (bf16[3,384,384]{2,1,0:T(8,128)(2,1)S(1)}, bf16[3,384,384]{2,1,0:T(8,128)(2,1)}, u32[]{:S(2)}, u32[]{:S(2)}) collective-permute-start(bf16[3,384,384]{2,1,0:T(8,128)(2,1)S(1)} %pad_maximum_fusion.p0), channel_id=1, source_target_pairs={{0,112},{1,17},{2,114},{3,19},{16,0},{17,33},{18,2},{19,35},{32,16... | collective-permute-start | bytes 2654216 | tf_op jit(solution)/shard_map/ppermute | solution.py:41
  50.5 3.7 %collective-permute-start.9 = (bf16[512,1536]{1,0:T(8,128)(2,1)}, bf16[512,1536]{1,0:T(8,128)(2,1)S(1)}, u32[]{:S(2)}, u32[]{:S(2)}) collective-permute-start(bf16[512,1536]{1,0:T(8,128)(2,1)} %collective-permute-done.8.t2), channel_id=1, source_target_pairs={{0,1},{1,0},{2,3},{3,2},{4,5},{5,4},{6,7},{7,6},{8,9},{9,8},{10,11... | collective-permute-start | bytes 4718600 | tf_op jit(solution)/shard_map/ppermute | solution.py:53
  50.8 17.6 %collective-permute-start.11 = (bf16[1536,384]{1,0:T(8,128)(2,1)}, bf16[1536,384]{1,0:T(8,128)(2,1)S(1)}, u32[]{:S(2)}, u32[]{:S(2)}) collective-permute-start(bf16[1536,384]{1,0:T(8,128)(2,1)} %collective-permute-done.6.w1), channel_id=1, source_target_pairs={{0,4},{1,13},{2,6},{3,15},{4,8},{5,1},{6,10},{7,3},{8,12},{9,5},{1... | collective-permute-start | bytes 3538952 | tf_op jit(solution)/shard_map/ppermute | solution.py:30
  50.8 16.5 %collective-permute-start.10 = (bf16[3,384,384]{2,1,0:T(8,128)(2,1)}, bf16[3,384,384]{2,1,0:T(8,128)(2,1)S(1)}, u32[]{:S(2)}, u32[]{:S(2)}) collective-permute-start(bf16[3,384,384]{2,1,0:T(8,128)(2,1)} %collective-permute-done.4.p1), channel_id=1, source_target_pairs={{0,16},{1,113},{2,18},{3,115},{16,32},{17,1},{18,34},{19,3},{32,48... | collective-permute-start | bytes 2654216 | tf_op jit(solution)/shard_map/ppermute | solution.py:41
  52.1 13.5 %collective-permute-start.12 = (bf16[768,384]{1,0:T(8,128)(2,1)S(1)}, bf16[768,384]{1,0:T(8,128)(2,1)S(1)}, u32[]{:S(2)}, u32[]{:S(2)}) collective-permute-start(bf16[768,384]{1,0:T(8,128)(2,1)S(1)} %constant_dynamic-slice_fusion), channel_id=1, source_target_pairs={{0,2},{1,3},{2,0},{3,1},{4,6},{5,7},{6,4},{7,5},{8,10},{9,11},{10,... | collective-permute-start | bytes 1769480 | tf_op jit(solution)/shard_map/ppermute | solution.py:53
  54.2 1.4 %copy-start.3 = (bf16[512,1536]{1,0:T(8,128)(2,1)S(1)}, bf16[512,1536]{1,0:T(8,128)(2,1)}, u32[]{:S(2)}) copy-start(bf16[512,1536]{1,0:T(8,128)(2,1)} %t0.1) | copy-start | bytes 4718596
  57.6 10.8 %copy-start.4 = (bf16[512,768]{1,0:T(8,128)(2,1)S(1)}, bf16[512,768]{1,0:T(8,128)(2,1)}, u32[]{:S(2)}) copy-start(bf16[512,768]{1,0:T(8,128)(2,1)} %cot.1) | copy-start | bytes 2359300
  65.1 12.0 %copy-start.8 = (bf16[192,1536]{1,0:T(8,128)(2,1)S(1)}, bf16[192,1536]{1,0:T(8,128)(2,1)}, u32[]{:S(2)}) copy-start(bf16[192,1536]{1,0:T(8,128)(2,1)} %get-tuple-element.71) | copy-start | bytes 1769476
  65.1 50.3 %copy-start.7 = (bf16[192,1536]{1,0:T(8,128)(2,1)S(1)}, bf16[192,1536]{1,0:T(8,128)(2,1)}, u32[]{:S(2)}) copy-start(bf16[192,1536]{1,0:T(8,128)(2,1)} %get-tuple-element.79) | copy-start | bytes 1769476
  65.1 50.5 %copy-start.6 = (bf16[192,1536]{1,0:T(8,128)(2,1)S(1)}, bf16[192,1536]{1,0:T(8,128)(2,1)}, u32[]{:S(2)}) copy-start(bf16[192,1536]{1,0:T(8,128)(2,1)} %get-tuple-element.80) | copy-start | bytes 1769476
  65.1 50.9 %copy-start.5 = (bf16[192,1536]{1,0:T(8,128)(2,1)S(1)}, bf16[192,1536]{1,0:T(8,128)(2,1)}, u32[]{:S(2)}) copy-start(bf16[192,1536]{1,0:T(8,128)(2,1)} %get-tuple-element.81) | copy-start | bytes 1769476
  68.4 51.6 %copy-start.2 = (bf16[1536,768]{0,1:T(8,128)(2,1)S(1)}, bf16[1536,768]{0,1:T(8,128)(2,1)}, u32[]{:S(2)}) copy-start(bf16[1536,768]{0,1:T(8,128)(2,1)} %copy.5) | copy-start | bytes 7077892
  71.1 22.9 %collective-permute-start.13 = (bf16[512,768]{1,0:T(8,128)(2,1)S(1)}, bf16[512,768]{1,0:T(8,128)(2,1)S(1)}, u32[]{:S(2)}, u32[]{:S(2)}) collective-permute-start(bf16[512,768]{1,0:T(8,128)(2,1)S(1)} %get-tuple-element.69), channel_id=1, source_target_pairs={{0,12},{1,4},{2,0},{3,8},{4,1},{5,9},{6,5},{7,13},{8,10},{9,2},{10... | collective-permute-start | bytes 2359304 | tf_op jit(solution)/shard_map/ppermute | solution.py:66
  72.3 16.4 %collective-permute-start.14 = (bf16[768,384]{1,0:T(8,128)(2,1)S(1)}, bf16[768,384]{1,0:T(8,128)(2,1)S(1)}, u32[]{:S(2)}, u32[]{:S(2)}) collective-permute-start(bf16[768,384]{1,0:T(8,128)(2,1)S(1)} %collective-permute-done.12.x0), channel_id=1, source_target_pairs={{0,16},{1,113},{2,18},{3,115},{16,32},{17,1},{18,34},{19,3},{32,48... | collective-permute-start | bytes 1769480 | tf_op jit(solution)/shard_map/ppermute | solution.py:41
  73.7 16.4 %collective-permute-start.15 = (bf16[768,384]{1,0:T(8,128)(2,1)S(1)}, bf16[768,384]{1,0:T(8,128)(2,1)S(1)}, u32[]{:S(2)}, u32[]{:S(2)}) collective-permute-start(bf16[768,384]{1,0:T(8,128)(2,1)S(1)} %collective-permute-done.12.x0), channel_id=1, source_target_pairs={{0,112},{1,17},{2,114},{3,19},{16,0},{17,33},{18,2},{19,35},{32,16... | collective-permute-start | bytes 1769480 | tf_op jit(solution)/shard_map/ppermute | solution.py:41
  76.9 13.1 %collective-permute-start.16 = (bf16[768,384]{1,0:T(8,128)(2,1)S(1)}, bf16[768,384]{1,0:T(8,128)(2,1)S(1)}, u32[]{:S(2)}, u32[]{:S(2)}) collective-permute-start(bf16[768,384]{1,0:T(8,128)(2,1)S(1)} %collective-permute-done.12.x0), channel_id=1, source_target_pairs={{0,1},{1,0},{2,3},{3,2},{4,5},{5,4},{6,7},{7,6},{8,9},{9,8},{10,11... | collective-permute-start | bytes 1769480 | tf_op jit(solution)/shard_map/ppermute | solution.py:53
  77.0 13.0 %collective-permute-start.17 = (bf16[192,1536]{1,0:T(8,128)(2,1)S(1)}, bf16[192,1536]{1,0:T(8,128)(2,1)S(1)}, u32[]{:S(2)}, u32[]{:S(2)}) collective-permute-start(bf16[192,1536]{1,0:T(8,128)(2,1)S(1)} %copy-done.8), channel_id=1, source_target_pairs={{0,1},{1,0},{2,3},{3,2},{4,5},{5,4},{6,7},{7,6},{8,9},{9,8},{10,11... | collective-permute-start | bytes 1769480 | tf_op jit(solution)/shard_map/ppermute | solution.py:53
  94.1 21.3 %collective-permute-start.18 = (bf16[512,768]{1,0:T(8,128)(2,1)S(1)}, bf16[512,768]{1,0:T(8,128)(2,1)S(1)}, u32[]{:S(2)}, u32[]{:S(2)}) collective-permute-start(bf16[512,768]{1,0:T(8,128)(2,1)S(1)} %collective-permute-done.13.rest_0_), channel_id=1, source_target_pairs={{0,4},{1,13},{2,6},{3,15},{4,8},{5,1},{6,10},{7,3},{8,12},{9,5},{1... | collective-permute-start | bytes 2359304 | tf_op jit(solution)/shard_map/ppermute | solution.py:30
  94.1 21.3 %collective-permute-start.19 = (bf16[512,768]{1,0:T(8,128)(2,1)S(1)}, bf16[512,768]{1,0:T(8,128)(2,1)S(1)}, u32[]{:S(2)}, u32[]{:S(2)}) collective-permute-start(bf16[512,768]{1,0:T(8,128)(2,1)S(1)} %collective-permute-done.13.rest_0_), channel_id=1, source_target_pairs={{0,12},{1,5},{2,14},{3,7},{4,0},{5,9},{6,2},{7,11},{8,4},{9,13},{1... | collective-permute-start | bytes 2359304 | tf_op jit(solution)/shard_map/ppermute | solution.py:30
  97.3 12.4 %collective-permute-start.20 = (bf16[768,384]{1,0:T(8,128)(2,1)S(1)}, bf16[768,384]{1,0:T(8,128)(2,1)S(1)}, u32[]{:S(2)}, u32[]{:S(2)}) collective-permute-start(bf16[768,384]{1,0:T(8,128)(2,1)S(1)} %collective-permute-done.14.x1), channel_id=1, source_target_pairs={{0,16},{1,113},{2,18},{3,115},{16,32},{17,1},{18,34},{19,3},{32,48... | collective-permute-start | bytes 1769480 | tf_op jit(solution)/shard_map/ppermute | solution.py:41
  97.6 12.0 %collective-permute-start.21 = (bf16[768,384]{1,0:T(8,128)(2,1)S(1)}, bf16[768,384]{1,0:T(8,128)(2,1)S(1)}, u32[]{:S(2)}, u32[]{:S(2)}) collective-permute-start(bf16[768,384]{1,0:T(8,128)(2,1)S(1)} %collective-permute-done.14.x1), channel_id=1, source_target_pairs={{0,1},{1,0},{2,3},{3,2},{4,5},{5,4},{6,7},{7,6},{8,9},{9,8},{10,11... | collective-permute-start | bytes 1769480 | tf_op jit(solution)/shard_map/ppermute | solution.py:53
  98.3 11.4 %collective-permute-start.22 = (bf16[768,384]{1,0:T(8,128)(2,1)S(1)}, bf16[768,384]{1,0:T(8,128)(2,1)S(1)}, u32[]{:S(2)}, u32[]{:S(2)}) collective-permute-start(bf16[768,384]{1,0:T(8,128)(2,1)S(1)} %collective-permute-done.15.x3), channel_id=1, source_target_pairs={{0,1},{1,0},{2,3},{3,2},{4,5},{5,4},{6,7},{7,6},{8,9},{9,8},{10,11... | collective-permute-start | bytes 1769480 | tf_op jit(solution)/shard_map/ppermute | solution.py:53
  115.3 13.2 %collective-permute-start.27 = (bf16[512,768]{1,0:T(8,128)(2,1)S(1)}, bf16[512,768]{1,0:T(8,128)(2,1)S(1)}, u32[]{:S(2)}, u32[]{:S(2)}) collective-permute-start(bf16[512,768]{1,0:T(8,128)(2,1)S(1)} %collective-permute-done.18.rest_1_), channel_id=1, source_target_pairs={{0,4},{1,13},{2,6},{3,15},{4,8},{5,1},{6,10},{7,3},{8,12},{9,5},{1... | collective-permute-start | bytes 2359304 | tf_op jit(solution)/shard_map/ppermute | solution.py:30
  115.3 2.1 %collective-permute-start.23 = (bf16[192,1536]{1,0:T(8,128)(2,1)S(1)}, bf16[192,1536]{1,0:T(8,128)(2,1)S(1)}, u32[]{:S(2)}, u32[]{:S(2)}) collective-permute-start(bf16[192,1536]{1,0:T(8,128)(2,1)S(1)} %copy-done.7), channel_id=1, source_target_pairs={{0,1},{1,0},{2,3},{3,2},{4,5},{5,4},{6,7},{7,6},{8,9},{9,8},{10,11... | collective-permute-start | bytes 1769480 | tf_op jit(solution)/shard_map/ppermute | solution.py:53
  115.5 2.8 %collective-permute-start.24 = (bf16[192,1536]{1,0:T(8,128)(2,1)S(1)}, bf16[192,1536]{1,0:T(8,128)(2,1)S(1)}, u32[]{:S(2)}, u32[]{:S(2)}) collective-permute-start(bf16[192,1536]{1,0:T(8,128)(2,1)S(1)} %copy-done.6), channel_id=1, source_target_pairs={{0,1},{1,0},{2,3},{3,2},{4,5},{5,4},{6,7},{7,6},{8,9},{9,8},{10,11... | collective-permute-start | bytes 1769480 | tf_op jit(solution)/shard_map/ppermute | solution.py:53
  116.0 3.2 %collective-permute-start.25 = (bf16[192,1536]{1,0:T(8,128)(2,1)S(1)}, bf16[192,1536]{1,0:T(8,128)(2,1)S(1)}, u32[]{:S(2)}, u32[]{:S(2)}) collective-permute-start(bf16[192,1536]{1,0:T(8,128)(2,1)S(1)} %copy-done.5), channel_id=1, source_target_pairs={{0,1},{1,0},{2,3},{3,2},{4,5},{5,4},{6,7},{7,6},{8,9},{9,8},{10,11... | collective-permute-start | bytes 1769480 | tf_op jit(solution)/shard_map/ppermute | solution.py:53
  116.1 3.9 %collective-permute-start.26 = (bf16[768,384]{1,0:T(8,128)(2,1)S(1)}, bf16[768,384]{1,0:T(8,128)(2,1)S(1)}, u32[]{:S(2)}, u32[]{:S(2)}) collective-permute-start(bf16[768,384]{1,0:T(8,128)(2,1)S(1)} %collective-permute-done.20.x2), channel_id=1, source_target_pairs={{0,1},{1,0},{2,3},{3,2},{4,5},{5,4},{6,7},{7,6},{8,9},{9,8},{10,11... | collective-permute-start | bytes 1769480 | tf_op jit(solution)/shard_map/ppermute | solution.py:53

commit v6 on v5

--- a/solution.py
+++ b/solution.py
@@ -268,9 +268,9 @@
 def down_last_kernel(w, g, so_far, out, buf, sem):
     r, c = lax.axis_index("row"), lax.axis_index("col")
     j = turned_from((r + 2) & 3, c)
-    tile = buf.shape[1] // 6
+    tile = buf.shape[1] // 3
     copies = []
-    for i in range(6):
+    for i in range(3):
         cols = pl.ds(i * tile, tile)
         buf[:, cols] = (so_far[:, cols] + mul(g[...], w[j, :, cols])).astype(buf.dtype)
         copies.append(pltpu.make_async_copy(buf.at[:, cols], out.at[:, cols], sem.at[i]))
@@ -285,7 +285,7 @@
         out_shape=jax.ShapeDtypeStruct(so_far.shape, jnp.bfloat16),
         in_specs=[VMEM] * 3,
         out_specs=ANY,
-        scratch_shapes=[pltpu.VMEM(so_far.shape, jnp.bfloat16), pltpu.SemaphoreType.DMA((6,))],
+        scratch_shapes=[pltpu.VMEM(so_far.shape, jnp.bfloat16), pltpu.SemaphoreType.DMA((3,))],
         compiler_params=params(),
         cost_estimate=cost(2 * so_far.size * g.shape[1], 6 * so_far.size),
         name="down_last",
@@ -320,7 +320,7 @@
     w2 = y_step(w1)
     t = sort_tokens(tokens, t_pair, t_x, col_swap(t_x, 1))
     so_far = up_part(t, w_up, w1, w3, p0, p1, p3)
-    p2, w2, so_far, x0 = together(p2, w2, so_far, x0)
+    p2, w2, so_far = together(p2, w2, so_far)
     hidden, d_pre = up_rest(t, so_far, w2, p2, cotangent)
 
     d_pre, x0, *quarters = together(d_pre, x0, *quarters)

time: 131 us -> 130 us (level)
  transfers between devices with their start and end apart: 28 -> 28, of which waited for: 17 -> 15; matrix products, arithmetic and copies ran while one was open for 7% -> 7% of each run, Pallas kernels for 11% -> 14%
where the time goes in v6:
time: 130 us
  waiting for transfers between devices  68.1 us (52%)
  starting transfers between devices  29.1 us (22%)
  Pallas kernels  19.8 us (15%)
  local copies, waits for them, and re-layouts  10.8 us (8%)
    ppermute x6, waiting for transfers between devices, z_step(): lax.ppermute(x, ('dp', 'col'), flat(sizes, lambda i, c: (i // n * n + (i...  31.2 us
    ppermute x12, waiting for transfers between devices, col_swap(): return lax.ppermute(x, 'col', [(i, i ^ m) for i in range(n)])  18.5 us
    ppermute x6, starting transfers between devices, z_step(): lax.ppermute(x, ('dp', 'col'), flat(sizes, lambda i, c: (i // n * n + (i...  12 us
    ppermute x8, waiting for transfers between devices, y_step(): lax.ppermute(x, ('row', 'col'), flat(sizes, lambda r, c: ((r + 1 - 2 * ((...  10.2 us
    ppermute x8, starting transfers between devices, y_step(): lax.ppermute(x, ('row', 'col'), flat(sizes, lambda r, c: ((r + 1 - 2 * ((...  9.55 us
    pallas_call x1, Pallas kernels, up_part(): pl.pallas_call(up_part_kernel, out_shape=jax.ShapeDtypeStruct((rows, widt...  7.43 us
    unnamed x23, local copies, waits for them, and re-layouts  5.54 us
    ppermute x1, waiting for transfers between devices, opposite(): return lax.ppermute(x, 'row', [(i, (i + 2) % n) for i in range(n)])  4.42 us
  transfers between devices with their start and end apart: 28, of which 15 were waited for; matrix products, arithmetic and copies ran while one was open for 7% of the time, Pallas kernels for 14%

profile of v6, /device:TPU:4, one launch (start us, length us, event | category | flops | bytes accessed | tf_op | source)
XLA Modules:
  0.0 129.9 jit_solution(14120934215472690713)
XLA Ops:
  0.6 0.1 collective-permute-start.3
  0.7 1.7 %copy-done = bf16[1536,768]{1,0:T(8,128)(2,1)S(1)} copy-done((bf16[1536,768]{1,0:T(8,128)(2,1)S(1)}, bf16[1536,768]{1,0:T(8,128)(2,1)}, u32[]{:S(2)}) %copy-start) | copy-done | bytes 2359320
  2.5 1.7 %collective-permute-start = (bf16[384,384]{1,0:T(8,128)(2,1)S(1)}, bf16[384,384]{1,0:T(8,128)(2,1)S(1)}, u32[]{:S(2)}, u32[]{:S(2)}) collective-permute-start(bf16[384,384]{1,0:T(8,128)(2,1)S(1)} %cut.1), channel_id=1, source_target_pairs={{0,4},{1,13},{2,6},{3,15},{4,8},{5,1},{6,10},{7,3},{8,12},{9,5},{1... | collective-permute-start | bytes 884744 | tf_op jit(solution)/shard_map/ppermute | solution.py:30
  4.1 2.9 %collective-permute-start.1 = (bf16[384,384]{1,0:T(8,128)(2,1)S(1)}, bf16[384,384]{1,0:T(8,128)(2,1)S(1)}, u32[]{:S(2)}, u32[]{:S(2)}) collective-permute-start(bf16[384,384]{1,0:T(8,128)(2,1)S(1)} %cut.1), channel_id=1, source_target_pairs={{0,8},{4,12},{8,0},{12,4},{1,9},{5,13},{9,1},{13,5},{2,10},{6,14},... | collective-permute-start | bytes 884744 | tf_op jit(solution)/shard_map/ppermute | solution.py:48
  7.0 1.3 %collective-permute-start.2 = (bf16[384,384]{1,0:T(8,128)(2,1)S(1)}, bf16[384,384]{1,0:T(8,128)(2,1)S(1)}, u32[]{:S(2)}, u32[]{:S(2)}) collective-permute-start(bf16[384,384]{1,0:T(8,128)(2,1)S(1)} %cut.1), channel_id=1, source_target_pairs={{0,12},{1,5},{2,14},{3,7},{4,0},{5,9},{6,2},{7,11},{8,4},{9,13},{1... | collective-permute-start | bytes 884744 | tf_op jit(solution)/shard_map/ppermute | solution.py:30
  8.4 0.5 collective-permute-start.8
  8.9 1.1 slice.3
  10.0 2.4 %copy.5 = bf16[1536,768]{0,1:T(8,128)(2,1)} copy(bf16[1536,768]{1,0:T(8,128)(2,1)S(1)} %copy-done.1) | data formatting | bytes 4718592 | tf_op args[1]
  12.4 3.0 %fusion = (bf16[192,1536]{1,0:T(8,128)(2,1)}, bf16[192,1536]{1,0:T(8,128)(2,1)}, bf16[192,1536]{1,0:T(8,128)(2,1)}, bf16[192,1536]{1,0:T(8,128)(2,1)}) fusion(bf16[768,1536]{1,0:T(8,128)(2,1)} %bitcast.4), kind=kLoop, calls=%fused_computation.2 | loop fusion | bytes 4718592 | tf_op jit(solution)/shard_map/split | solution.py:310
  15.5 4.4 %collective-permute-done.1 = bf16[384,384]{1,0:T(8,128)(2,1)S(1)} collective-permute-done((bf16[384,384]{1,0:T(8,128)(2,1)S(1)}, bf16[384,384]{1,0:T(8,128)(2,1)S(1)}, u32[]{:S(2)}, u32[]{:S(2)}) %collective-permute-start.1) | collective-permute-done | bytes 294944 | tf_op jit(solution)/shard_map/ppermute | solution.py:48
  20.0 3.2 %collective-permute-start.7 = (bf16[1536,384]{1,0:T(8,128)(2,1)}, bf16[1536,384]{1,0:T(8,128)(2,1)}, u32[]{:S(2)}, u32[]{:S(2)}) collective-permute-start(bf16[1536,384]{1,0:T(8,128)(2,1)} %slice.3), channel_id=1, source_target_pairs={{0,12},{1,5},{2,14},{3,7},{4,0},{5,9},{6,2},{7,11},{8,4},{9,13},{1... | collective-permute-start | bytes 3538952 | tf_op jit(solution)/shard_map/ppermute | solution.py:30
  23.2 1.2 pad_maximum_fusion.p0
  24.4 2.0 %collective-permute-start.4 = (bf16[3,384,384]{2,1,0:T(8,128)(2,1)S(1)}, bf16[3,384,384]{2,1,0:T(8,128)(2,1)}, u32[]{:S(2)}, u32[]{:S(2)}) collective-permute-start(bf16[3,384,384]{2,1,0:T(8,128)(2,1)S(1)} %pad_maximum_fusion.p0), channel_id=1, source_target_pairs={{0,16},{1,113},{2,18},{3,115},{16,32},{17,1},{18,34},{19,3},{32,48... | collective-permute-start | bytes 2654216 | tf_op jit(solution)/shard_map/ppermute | solution.py:41
  26.4 4.0 %collective-permute-start.5 = (bf16[3,384,384]{2,1,0:T(8,128)(2,1)S(1)}, bf16[3,384,384]{2,1,0:T(8,128)(2,1)}, u32[]{:S(2)}, u32[]{:S(2)}) collective-permute-start(bf16[3,384,384]{2,1,0:T(8,128)(2,1)S(1)} %pad_maximum_fusion.p0), channel_id=1, source_target_pairs={{0,112},{1,17},{2,114},{3,19},{16,0},{17,33},{18,2},{19,35},{32,16... | collective-permute-start | bytes 2654216 | tf_op jit(solution)/shard_map/ppermute | solution.py:41
  30.4 1.1 constant_dynamic-slice_fusion
  31.5 13.4 %collective-permute-done.8.t2 = bf16[512,1536]{1,0:T(8,128)(2,1)} collective-permute-done((bf16[512,1536]{1,0:T(8,128)(2,1)}, bf16[512,1536]{1,0:T(8,128)(2,1)}, u32[]{:S(2)}, u32[]{:S(2)}) %collective-permute-start.8) | collective-permute-done | bytes 1572896 | tf_op jit(solution)/shard_map/ppermute | solution.py:53
  44.9 5.6 %collective-permute-done.4.p1 = bf16[3,384,384]{2,1,0:T(8,128)(2,1)} collective-permute-done((bf16[3,384,384]{2,1,0:T(8,128)(2,1)S(1)}, bf16[3,384,384]{2,1,0:T(8,128)(2,1)}, u32[]{:S(2)}, u32[]{:S(2)}) %collective-permute-start.4) | collective-permute-done | bytes 884768 | tf_op jit(solution)/shard_map/ppermute | solution.py:41
  50.5 0.3 collective-permute-start.9
  50.8 1.3 %collective-permute-start.10 = (bf16[3,384,384]{2,1,0:T(8,128)(2,1)}, bf16[3,384,384]{2,1,0:T(8,128)(2,1)S(1)}, u32[]{:S(2)}, u32[]{:S(2)}) collective-permute-start(bf16[3,384,384]{2,1,0:T(8,128)(2,1)} %collective-permute-done.4.p1), channel_id=1, source_target_pairs={{0,16},{1,113},{2,18},{3,115},{16,32},{17,1},{18,34},{19,3},{32,48... | collective-permute-start | bytes 2654216 | tf_op jit(solution)/shard_map/ppermute | solution.py:41
  52.1 0.5 collective-permute-start.12
  52.6 1.6 %collective-permute-done.9.t3 = bf16[512,1536]{1,0:T(8,128)(2,1)S(1)} collective-permute-done((bf16[512,1536]{1,0:T(8,128)(2,1)}, bf16[512,1536]{1,0:T(8,128)(2,1)S(1)}, u32[]{:S(2)}, u32[]{:S(2)}) %collective-permute-start.9) | collective-permute-done | bytes 1572896 | tf_op jit(solution)/shard_map/ppermute | solution.py:53
  54.2 1.4 %copy-done.3 = bf16[512,1536]{1,0:T(8,128)(2,1)S(1)} copy-done((bf16[512,1536]{1,0:T(8,128)(2,1)S(1)}, bf16[512,1536]{1,0:T(8,128)(2,1)}, u32[]{:S(2)}) %copy-start.3) | copy-done | bytes 1572888
  55.6 2.0 %sort_tokens.1.t = bf16[4,512,1536]{2,1,0:T(8,128)(2,1)S(1)} custom-call(bf16[512,1536]{1,0:T(8,128)(2,1)S(1)} %copy-done.3, bf16[512,1536]{1,0:T(8,128)(2,1)} %collective-permute-done.3.t1, bf16[512,1536]{1,0:T(8,128)(2,1)} %collective-permute-done.8.t2, bf16[512,1536]{1,0:T(8,128)(2,1)S(1)} %collective-permute-done.9.t3), custom_call_target="tpu_custom_call" | custom-call | bytes 12582912 | tf_op jit(solution)/shard_map/sort_tokens/pallas_call | solution.py:129
  57.6 7.4 %up_part.1.so_far = f32[512,768]{1,0:T(8,128)S(1)} custom-call(bf16[4,512,1536]{2,1,0:T(8,128)(2,1)S(1)} %sort_tokens.1.t, bf16[1536,768]{1,0:T(8,128)(2,1)S(1)} %copy-done.1, bf16[1536,384]{1,0:T(8,128)(2,1)} %collective-permute-done.6.w1, bf16[1536,384]{1,0:T(8,128)(2,1)} %collective-permute-done.7.w3, bf16[3,384,384]{2,1,0:T(8,128)(2,1)S(1)} %pad_maximum_fusion.p0, ...), custom_call_target="tpu_custom_call" | custom-call | flops 3623878656 | bytes 11796480 | tf_op jit(solution)/shard_map/up_part/pallas_call | solution.py:183
  65.1 2.2 %collective-permute-done.10.p2 = bf16[3,384,384]{2,1,0:T(8,128)(2,1)S(1)} collective-permute-done((bf16[3,384,384]{2,1,0:T(8,128)(2,1)}, bf16[3,384,384]{2,1,0:T(8,128)(2,1)S(1)}, u32[]{:S(2)}, u32[]{:S(2)}) %collective-permute-start.10) | collective-permute-done | bytes 884768 | tf_op jit(solution)/shard_map/ppermute | solution.py:41
  67.2 1.1 collective-permute-done.11.w2
  68.4 2.7 %up_rest.1 = (bf16[512,768]{1,0:T(8,128)(2,1)}, bf16[512,768]{1,0:T(8,128)(2,1)S(1)}) custom-call(bf16[4,512,1536]{2,1,0:T(8,128)(2,1)S(1)} %sort_tokens.1.t, f32[512,768]{1,0:T(8,128)S(1)} %up_part.1.so_far, bf16[1536,384]{1,0:T(8,128)(2,1)S(1)} %collective-permute-done.11.w2, bf16[3,384,384]{2,1,0:T(8,128)(2,1)S(1)} %collective-permute-done.10.p2, ...), custom_call_target="tpu_custom_call" | custom-call | flops 1207959552 | bytes 3932160 | tf_op jit(solution)/shard_map/up_rest/pallas_call | solution.py:197
  71.1 1.2 collective-permute-start.13
  72.3 0.7 collective-permute-start.14
  73.0 3.9 %collective-permute-start.15 = (bf16[768,384]{1,0:T(8,128)(2,1)S(1)}, bf16[768,384]{1,0:T(8,128)(2,1)S(1)}, u32[]{:S(2)}, u32[]{:S(2)}) collective-permute-start(bf16[768,384]{1,0:T(8,128)(2,1)S(1)} %collective-permute-done.12.x0), channel_id=1, source_target_pairs={{0,112},{1,17},{2,114},{3,19},{16,0},{17,33},{18,2},{19,35},{32,16... | collective-permute-start | bytes 1769480 | tf_op jit(solution)/shard_map/ppermute | solution.py:41
  77.0 0.5 collective-permute-start.17
  77.5 13.0 %collective-permute-done.14.x1 = bf16[768,384]{1,0:T(8,128)(2,1)S(1)} collective-permute-done((bf16[768,384]{1,0:T(8,128)(2,1)S(1)}, bf16[768,384]{1,0:T(8,128)(2,1)S(1)}, u32[]{:S(2)}, u32[]{:S(2)}) %collective-permute-start.14) | collective-permute-done | bytes 589856 | tf_op jit(solution)/shard_map/ppermute | solution.py:41
  90.4 3.7 %collective-permute-done.13.rest_0_ = bf16[512,768]{1,0:T(8,128)(2,1)S(1)} collective-permute-done((bf16[512,768]{1,0:T(8,128)(2,1)S(1)}, bf16[512,768]{1,0:T(8,128)(2,1)S(1)}, u32[]{:S(2)}, u32[]{:S(2)}) %collective-permute-start.13) | collective-permute-done | bytes 786464 | tf_op jit(solution)/shard_map/ppermute | solution.py:66
  94.2 3.2 %collective-permute-start.19 = (bf16[512,768]{1,0:T(8,128)(2,1)S(1)}, bf16[512,768]{1,0:T(8,128)(2,1)S(1)}, u32[]{:S(2)}, u32[]{:S(2)}) collective-permute-start(bf16[512,768]{1,0:T(8,128)(2,1)S(1)} %collective-permute-done.13.rest_0_), channel_id=1, source_target_pairs={{0,12},{1,5},{2,14},{3,7},{4,0},{5,9},{6,2},{7,11},{8,4},{9,13},{1... | collective-permute-start | bytes 2359304 | tf_op jit(solution)/shard_map/ppermute | solution.py:30
  97.4 0.5 collective-permute-start.22
  97.9 10.6 %collective-permute-done.20.x2 = bf16[768,384]{1,0:T(8,128)(2,1)S(1)} collective-permute-done((bf16[768,384]{1,0:T(8,128)(2,1)S(1)}, bf16[768,384]{1,0:T(8,128)(2,1)S(1)}, u32[]{:S(2)}, u32[]{:S(2)}) %collective-permute-start.20) | collective-permute-done | bytes 589856 | tf_op jit(solution)/shard_map/ppermute | solution.py:41
  108.5 5.8 %collective-permute-done.18.rest_1_ = bf16[512,768]{1,0:T(8,128)(2,1)S(1)} collective-permute-done((bf16[512,768]{1,0:T(8,128)(2,1)S(1)}, bf16[512,768]{1,0:T(8,128)(2,1)S(1)}, u32[]{:S(2)}, u32[]{:S(2)}) %collective-permute-start.18) | collective-permute-done | bytes 786464 | tf_op jit(solution)/shard_map/ppermute | solution.py:30
  114.5 0.5 collective-permute-start.24
  115.0 0.1 collective-permute-start.25
  115.1 0.4 collective-permute-start.26
  115.5 1.0 collective-permute-done.23.c1
  116.5 0.8 collective-permute-done.24.c2
  117.3 0.8 collective-permute-done.25.c3
  118.1 0.8 collective-permute-done.26.y2
  119.0 1.2 sort_w.1.w
  120.2 4.2 %down.1.so_far = f32[512,1536]{1,0:T(8,128)S(1)} custom-call(bf16[4,768,1536]{2,1,0:T(8,128)(2,1)S(1)} %sort_w.1.w, bf16[512,768]{1,0:T(8,128)(2,1)S(1)} %collective-permute-done.13.rest_0_, bf16[512,768]{1,0:T(8,128)(2,1)S(1)} %collective-permute-done.18.rest_1_, bf16[512,768]{1,0:T(8,128)(2,1)S(1)} %collective-permute-done.19.rest_2_), custom_call_target="tpu_custom_call" | custom-call | flops 1572864 | bytes 16384 | tf_op jit(solution)/shard_map/down/pallas_call | solution.py:257
  124.3 3.2 %collective-permute-done.27.g = bf16[512,768]{1,0:T(8,128)(2,1)S(1)} collective-permute-done((bf16[512,768]{1,0:T(8,128)(2,1)S(1)}, bf16[512,768]{1,0:T(8,128)(2,1)S(1)}, u32[]{:S(2)}, u32[]{:S(2)}) %collective-permute-start.27) | collective-permute-done | bytes 786464 | tf_op jit(solution)/shard_map/ppermute | solution.py:30
  127.6 2.2 %down_last.1 = bf16[512,1536]{1,0:T(8,128)(2,1)} custom-call(bf16[4,768,1536]{2,1,0:T(8,128)(2,1)S(1)} %sort_w.1.w, bf16[512,768]{1,0:T(8,128)(2,1)S(1)} %collective-permute-done.27.g, f32[512,1536]{1,0:T(8,128)S(1)} %down.1.so_far), custom_call_target="tpu_custom_call" | custom-call | flops 1207959552 | bytes 4718592 | tf_op jit(solution)/shard_map/down_last/pallas_call | solution.py:283
  (42 shorter events, 0.3 us)
Async XLA Ops:
  0.6 19.3 %collective-permute-start.3 = (bf16[512,1536]{1,0:T(8,128)(2,1)}, bf16[512,1536]{1,0:T(8,128)(2,1)}, u32[]{:S(2)}, u32[]{:S(2)}) collective-permute-start(bf16[512,1536]{1,0:T(8,128)(2,1)} %t0.1), channel_id=1, source_target_pairs={{0,1},{1,0},{2,3},{3,2},{4,5},{5,4},{6,7},{7,6},{8,9},{9,8},{10,11... | collective-permute-start | bytes 4718600 | tf_op jit(solution)/shard_map/ppermute | solution.py:53
  0.7 1.7 %copy-start = (bf16[1536,768]{1,0:T(8,128)(2,1)S(1)}, bf16[1536,768]{1,0:T(8,128)(2,1)}, u32[]{:S(2)}) copy-start(bf16[1536,768]{1,0:T(8,128)(2,1)} %own.1) | copy-start | bytes 7077892
  2.4 6.5 %copy-start.1 = (bf16[1536,768]{1,0:T(8,128)(2,1)S(1)}, bf16[1536,768]{1,0:T(8,128)(2,1)}, u32[]{:S(2)}) copy-start(bf16[1536,768]{1,0:T(8,128)(2,1)} %own.1) | copy-start | bytes 7077892
  2.5 13.0 %collective-permute-start = (bf16[384,384]{1,0:T(8,128)(2,1)S(1)}, bf16[384,384]{1,0:T(8,128)(2,1)S(1)}, u32[]{:S(2)}, u32[]{:S(2)}) collective-permute-start(bf16[384,384]{1,0:T(8,128)(2,1)S(1)} %cut.1), channel_id=1, source_target_pairs={{0,4},{1,13},{2,6},{3,15},{4,8},{5,1},{6,10},{7,3},{8,12},{9,5},{1... | collective-permute-start | bytes 884744 | tf_op jit(solution)/shard_map/ppermute | solution.py:30
  4.1 15.8 %collective-permute-start.1 = (bf16[384,384]{1,0:T(8,128)(2,1)S(1)}, bf16[384,384]{1,0:T(8,128)(2,1)S(1)}, u32[]{:S(2)}, u32[]{:S(2)}) collective-permute-start(bf16[384,384]{1,0:T(8,128)(2,1)S(1)} %cut.1), channel_id=1, source_target_pairs={{0,8},{4,12},{8,0},{12,4},{1,9},{5,13},{9,1},{13,5},{2,10},{6,14},... | collective-permute-start | bytes 884744 | tf_op jit(solution)/shard_map/ppermute | solution.py:48
  7.0 12.9 %collective-permute-start.2 = (bf16[384,384]{1,0:T(8,128)(2,1)S(1)}, bf16[384,384]{1,0:T(8,128)(2,1)S(1)}, u32[]{:S(2)}, u32[]{:S(2)}) collective-permute-start(bf16[384,384]{1,0:T(8,128)(2,1)S(1)} %cut.1), channel_id=1, source_target_pairs={{0,12},{1,5},{2,14},{3,7},{4,0},{5,9},{6,2},{7,11},{8,4},{9,13},{1... | collective-permute-start | bytes 884744 | tf_op jit(solution)/shard_map/ppermute | solution.py:30
  8.4 36.6 %collective-permute-start.8 = (bf16[512,1536]{1,0:T(8,128)(2,1)}, bf16[512,1536]{1,0:T(8,128)(2,1)}, u32[]{:S(2)}, u32[]{:S(2)}) collective-permute-start(bf16[512,1536]{1,0:T(8,128)(2,1)} %t0.1), channel_id=1, source_target_pairs={{0,2},{1,3},{2,0},{3,1},{4,6},{5,7},{6,4},{7,5},{8,10},{9,11},{10,... | collective-permute-start | bytes 4718600 | tf_op jit(solution)/shard_map/ppermute | solution.py:53
  19.9 3.3 %copy-start.9 = (bf16[384,384]{1,0:T(8,128)(2,1)}, bf16[384,384]{1,0:T(8,128)(2,1)S(1)}, u32[]{:S(2)}) copy-start(bf16[384,384]{1,0:T(8,128)(2,1)S(1)} %collective-permute-done.1) | copy-start | bytes 884740
  19.9 3.3 %copy-start.10 = (bf16[384,384]{1,0:T(8,128)(2,1)}, bf16[384,384]{1,0:T(8,128)(2,1)S(1)}, u32[]{:S(2)}) copy-start(bf16[384,384]{1,0:T(8,128)(2,1)S(1)} %collective-permute-done.2) | copy-start | bytes 884740
  19.9 30.6 %collective-permute-start.6 = (bf16[1536,384]{1,0:T(8,128)(2,1)}, bf16[1536,384]{1,0:T(8,128)(2,1)}, u32[]{:S(2)}, u32[]{:S(2)}) collective-permute-start(bf16[1536,384]{1,0:T(8,128)(2,1)} %slice.3), channel_id=1, source_target_pairs={{0,4},{1,13},{2,6},{3,15},{4,8},{5,1},{6,10},{7,3},{8,12},{9,5},{1... | collective-permute-start | bytes 3538952 | tf_op jit(solution)/shard_map/ppermute | solution.py:30
  20.0 30.5 %collective-permute-start.7 = (bf16[1536,384]{1,0:T(8,128)(2,1)}, bf16[1536,384]{1,0:T(8,128)(2,1)}, u32[]{:S(2)}, u32[]{:S(2)}) collective-permute-start(bf16[1536,384]{1,0:T(8,128)(2,1)} %slice.3), channel_id=1, source_target_pairs={{0,12},{1,5},{2,14},{3,7},{4,0},{5,9},{6,2},{7,11},{8,4},{9,13},{1... | collective-permute-start | bytes 3538952 | tf_op jit(solution)/shard_map/ppermute | solution.py:30
  24.4 26.1 %collective-permute-start.4 = (bf16[3,384,384]{2,1,0:T(8,128)(2,1)S(1)}, bf16[3,384,384]{2,1,0:T(8,128)(2,1)}, u32[]{:S(2)}, u32[]{:S(2)}) collective-permute-start(bf16[3,384,384]{2,1,0:T(8,128)(2,1)S(1)} %pad_maximum_fusion.p0), channel_id=1, source_target_pairs={{0,16},{1,113},{2,18},{3,115},{16,32},{17,1},{18,34},{19,3},{32,48... | collective-permute-start | bytes 2654216 | tf_op jit(solution)/shard_map/ppermute | solution.py:41
  26.4 24.1 %collective-permute-start.5 = (bf16[3,384,384]{2,1,0:T(8,128)(2,1)S(1)}, bf16[3,384,384]{2,1,0:T(8,128)(2,1)}, u32[]{:S(2)}, u32[]{:S(2)}) collective-permute-start(bf16[3,384,384]{2,1,0:T(8,128)(2,1)S(1)} %pad_maximum_fusion.p0), channel_id=1, source_target_pairs={{0,112},{1,17},{2,114},{3,19},{16,0},{17,33},{18,2},{19,35},{32,16... | collective-permute-start | bytes 2654216 | tf_op jit(solution)/shard_map/ppermute | solution.py:41
  50.5 3.7 %collective-permute-start.9 = (bf16[512,1536]{1,0:T(8,128)(2,1)}, bf16[512,1536]{1,0:T(8,128)(2,1)S(1)}, u32[]{:S(2)}, u32[]{:S(2)}) collective-permute-start(bf16[512,1536]{1,0:T(8,128)(2,1)} %collective-permute-done.8.t2), channel_id=1, source_target_pairs={{0,1},{1,0},{2,3},{3,2},{4,5},{5,4},{6,7},{7,6},{8,9},{9,8},{10,11... | collective-permute-start | bytes 4718600 | tf_op jit(solution)/shard_map/ppermute | solution.py:53
  50.8 17.6 %collective-permute-start.11 = (bf16[1536,384]{1,0:T(8,128)(2,1)}, bf16[1536,384]{1,0:T(8,128)(2,1)S(1)}, u32[]{:S(2)}, u32[]{:S(2)}) collective-permute-start(bf16[1536,384]{1,0:T(8,128)(2,1)} %collective-permute-done.6.w1), channel_id=1, source_target_pairs={{0,4},{1,13},{2,6},{3,15},{4,8},{5,1},{6,10},{7,3},{8,12},{9,5},{1... | collective-permute-start | bytes 3538952 | tf_op jit(solution)/shard_map/ppermute | solution.py:30
  50.8 16.5 %collective-permute-start.10 = (bf16[3,384,384]{2,1,0:T(8,128)(2,1)}, bf16[3,384,384]{2,1,0:T(8,128)(2,1)S(1)}, u32[]{:S(2)}, u32[]{:S(2)}) collective-permute-start(bf16[3,384,384]{2,1,0:T(8,128)(2,1)} %collective-permute-done.4.p1), channel_id=1, source_target_pairs={{0,16},{1,113},{2,18},{3,115},{16,32},{17,1},{18,34},{19,3},{32,48... | collective-permute-start | bytes 2654216 | tf_op jit(solution)/shard_map/ppermute | solution.py:41
  52.1 19.1 %collective-permute-start.12 = (bf16[768,384]{1,0:T(8,128)(2,1)S(1)}, bf16[768,384]{1,0:T(8,128)(2,1)S(1)}, u32[]{:S(2)}, u32[]{:S(2)}) collective-permute-start(bf16[768,384]{1,0:T(8,128)(2,1)S(1)} %constant_dynamic-slice_fusion), channel_id=1, source_target_pairs={{0,2},{1,3},{2,0},{3,1},{4,6},{5,7},{6,4},{7,5},{8,10},{9,11},{10,... | collective-permute-start | bytes 1769480 | tf_op jit(solution)/shard_map/ppermute | solution.py:53
  54.2 1.4 %copy-start.3 = (bf16[512,1536]{1,0:T(8,128)(2,1)S(1)}, bf16[512,1536]{1,0:T(8,128)(2,1)}, u32[]{:S(2)}) copy-start(bf16[512,1536]{1,0:T(8,128)(2,1)} %t0.1) | copy-start | bytes 4718596
  57.6 10.8 %copy-start.4 = (bf16[512,768]{1,0:T(8,128)(2,1)S(1)}, bf16[512,768]{1,0:T(8,128)(2,1)}, u32[]{:S(2)}) copy-start(bf16[512,768]{1,0:T(8,128)(2,1)} %cot.1) | copy-start | bytes 2359300
  65.1 11.9 %copy-start.8 = (bf16[192,1536]{1,0:T(8,128)(2,1)S(1)}, bf16[192,1536]{1,0:T(8,128)(2,1)}, u32[]{:S(2)}) copy-start(bf16[192,1536]{1,0:T(8,128)(2,1)} %get-tuple-element.69) | copy-start | bytes 1769476
  65.1 49.3 %copy-start.7 = (bf16[192,1536]{1,0:T(8,128)(2,1)S(1)}, bf16[192,1536]{1,0:T(8,128)(2,1)}, u32[]{:S(2)}) copy-start(bf16[192,1536]{1,0:T(8,128)(2,1)} %get-tuple-element.77) | copy-start | bytes 1769476
  65.1 49.4 %copy-start.6 = (bf16[192,1536]{1,0:T(8,128)(2,1)S(1)}, bf16[192,1536]{1,0:T(8,128)(2,1)}, u32[]{:S(2)}) copy-start(bf16[192,1536]{1,0:T(8,128)(2,1)} %get-tuple-element.78) | copy-start | bytes 1769476
  65.1 49.9 %copy-start.5 = (bf16[192,1536]{1,0:T(8,128)(2,1)S(1)}, bf16[192,1536]{1,0:T(8,128)(2,1)}, u32[]{:S(2)}) copy-start(bf16[192,1536]{1,0:T(8,128)(2,1)} %get-tuple-element.79) | copy-start | bytes 1769476
  68.4 50.6 %copy-start.2 = (bf16[1536,768]{0,1:T(8,128)(2,1)S(1)}, bf16[1536,768]{0,1:T(8,128)(2,1)}, u32[]{:S(2)}) copy-start(bf16[1536,768]{0,1:T(8,128)(2,1)} %copy.5) | copy-start | bytes 7077892
  71.1 23.0 %collective-permute-start.13 = (bf16[512,768]{1,0:T(8,128)(2,1)S(1)}, bf16[512,768]{1,0:T(8,128)(2,1)S(1)}, u32[]{:S(2)}, u32[]{:S(2)}) collective-permute-start(bf16[512,768]{1,0:T(8,128)(2,1)S(1)} %get-tuple-element.67), channel_id=1, source_target_pairs={{0,12},{1,4},{2,0},{3,8},{4,1},{5,9},{6,5},{7,13},{8,10},{9,2},{10... | collective-permute-start | bytes 2359304 | tf_op jit(solution)/shard_map/ppermute | solution.py:66
  72.3 18.1 %collective-permute-start.14 = (bf16[768,384]{1,0:T(8,128)(2,1)S(1)}, bf16[768,384]{1,0:T(8,128)(2,1)S(1)}, u32[]{:S(2)}, u32[]{:S(2)}) collective-permute-start(bf16[768,384]{1,0:T(8,128)(2,1)S(1)} %collective-permute-done.12.x0), channel_id=1, source_target_pairs={{0,16},{1,113},{2,18},{3,115},{16,32},{17,1},{18,34},{19,3},{32,48... | collective-permute-start | bytes 1769480 | tf_op jit(solution)/shard_map/ppermute | solution.py:41
  73.0 17.4 %collective-permute-start.15 = (bf16[768,384]{1,0:T(8,128)(2,1)S(1)}, bf16[768,384]{1,0:T(8,128)(2,1)S(1)}, u32[]{:S(2)}, u32[]{:S(2)}) collective-permute-start(bf16[768,384]{1,0:T(8,128)(2,1)S(1)} %collective-permute-done.12.x0), channel_id=1, source_target_pairs={{0,112},{1,17},{2,114},{3,19},{16,0},{17,33},{18,2},{19,35},{32,16... | collective-permute-start | bytes 1769480 | tf_op jit(solution)/shard_map/ppermute | solution.py:41
  77.0 13.5 %collective-permute-start.16 = (bf16[768,384]{1,0:T(8,128)(2,1)S(1)}, bf16[768,384]{1,0:T(8,128)(2,1)S(1)}, u32[]{:S(2)}, u32[]{:S(2)}) collective-permute-start(bf16[768,384]{1,0:T(8,128)(2,1)S(1)} %collective-permute-done.12.x0), channel_id=1, source_target_pairs={{0,1},{1,0},{2,3},{3,2},{4,5},{5,4},{6,7},{7,6},{8,9},{9,8},{10,11... | collective-permute-start | bytes 1769480 | tf_op jit(solution)/shard_map/ppermute | solution.py:53
  77.0 13.5 %collective-permute-start.17 = (bf16[192,1536]{1,0:T(8,128)(2,1)S(1)}, bf16[192,1536]{1,0:T(8,128)(2,1)S(1)}, u32[]{:S(2)}, u32[]{:S(2)}) collective-permute-start(bf16[192,1536]{1,0:T(8,128)(2,1)S(1)} %copy-done.8), channel_id=1, source_target_pairs={{0,1},{1,0},{2,3},{3,2},{4,5},{5,4},{6,7},{7,6},{8,9},{9,8},{10,11... | collective-permute-start | bytes 1769480 | tf_op jit(solution)/shard_map/ppermute | solution.py:53
  94.2 20.2 %collective-permute-start.18 = (bf16[512,768]{1,0:T(8,128)(2,1)S(1)}, bf16[512,768]{1,0:T(8,128)(2,1)S(1)}, u32[]{:S(2)}, u32[]{:S(2)}) collective-permute-start(bf16[512,768]{1,0:T(8,128)(2,1)S(1)} %collective-permute-done.13.rest_0_), channel_id=1, source_target_pairs={{0,4},{1,13},{2,6},{3,15},{4,8},{5,1},{6,10},{7,3},{8,12},{9,5},{1... | collective-permute-start | bytes 2359304 | tf_op jit(solution)/shard_map/ppermute | solution.py:30
  94.2 20.2 %collective-permute-start.19 = (bf16[512,768]{1,0:T(8,128)(2,1)S(1)}, bf16[512,768]{1,0:T(8,128)(2,1)S(1)}, u32[]{:S(2)}, u32[]{:S(2)}) collective-permute-start(bf16[512,768]{1,0:T(8,128)(2,1)S(1)} %collective-permute-done.13.rest_0_), channel_id=1, source_target_pairs={{0,12},{1,5},{2,14},{3,7},{4,0},{5,9},{6,2},{7,11},{8,4},{9,13},{1... | collective-permute-start | bytes 2359304 | tf_op jit(solution)/shard_map/ppermute | solution.py:30
  97.4 11.1 %collective-permute-start.20 = (bf16[768,384]{1,0:T(8,128)(2,1)S(1)}, bf16[768,384]{1,0:T(8,128)(2,1)S(1)}, u32[]{:S(2)}, u32[]{:S(2)}) collective-permute-start(bf16[768,384]{1,0:T(8,128)(2,1)S(1)} %collective-permute-done.14.x1), channel_id=1, source_target_pairs={{0,16},{1,113},{2,18},{3,115},{16,32},{17,1},{18,34},{19,3},{32,48... | collective-permute-start | bytes 1769480 | tf_op jit(solution)/shard_map/ppermute | solution.py:41
  97.4 11.1 %collective-permute-start.21 = (bf16[768,384]{1,0:T(8,128)(2,1)S(1)}, bf16[768,384]{1,0:T(8,128)(2,1)S(1)}, u32[]{:S(2)}, u32[]{:S(2)}) collective-permute-start(bf16[768,384]{1,0:T(8,128)(2,1)S(1)} %collective-permute-done.14.x1), channel_id=1, source_target_pairs={{0,1},{1,0},{2,3},{3,2},{4,5},{5,4},{6,7},{7,6},{8,9},{9,8},{10,11... | collective-permute-start | bytes 1769480 | tf_op jit(solution)/shard_map/ppermute | solution.py:53
  97.4 11.1 %collective-permute-start.22 = (bf16[768,384]{1,0:T(8,128)(2,1)S(1)}, bf16[768,384]{1,0:T(8,128)(2,1)S(1)}, u32[]{:S(2)}, u32[]{:S(2)}) collective-permute-start(bf16[768,384]{1,0:T(8,128)(2,1)S(1)} %collective-permute-done.15.x3), channel_id=1, source_target_pairs={{0,1},{1,0},{2,3},{3,2},{4,5},{5,4},{6,7},{7,6},{8,9},{9,8},{10,11... | collective-permute-start | bytes 1769480 | tf_op jit(solution)/shard_map/ppermute | solution.py:53
  114.4 13.2 %collective-permute-start.27 = (bf16[512,768]{1,0:T(8,128)(2,1)S(1)}, bf16[512,768]{1,0:T(8,128)(2,1)S(1)}, u32[]{:S(2)}, u32[]{:S(2)}) collective-permute-start(bf16[512,768]{1,0:T(8,128)(2,1)S(1)} %collective-permute-done.18.rest_1_), channel_id=1, source_target_pairs={{0,4},{1,13},{2,6},{3,15},{4,8},{5,1},{6,10},{7,3},{8,12},{9,5},{1... | collective-permute-start | bytes 2359304 | tf_op jit(solution)/shard_map/ppermute | solution.py:30
  114.4 2.1 %collective-permute-start.23 = (bf16[192,1536]{1,0:T(8,128)(2,1)S(1)}, bf16[192,1536]{1,0:T(8,128)(2,1)S(1)}, u32[]{:S(2)}, u32[]{:S(2)}) collective-permute-start(bf16[192,1536]{1,0:T(8,128)(2,1)S(1)} %copy-done.7), channel_id=1, source_target_pairs={{0,1},{1,0},{2,3},{3,2},{4,5},{5,4},{6,7},{7,6},{8,9},{9,8},{10,11... | collective-permute-start | bytes 1769480 | tf_op jit(solution)/shard_map/ppermute | solution.py:53
  114.5 2.8 %collective-permute-start.24 = (bf16[192,1536]{1,0:T(8,128)(2,1)S(1)}, bf16[192,1536]{1,0:T(8,128)(2,1)S(1)}, u32[]{:S(2)}, u32[]{:S(2)}) collective-permute-start(bf16[192,1536]{1,0:T(8,128)(2,1)S(1)} %copy-done.6), channel_id=1, source_target_pairs={{0,1},{1,0},{2,3},{3,2},{4,5},{5,4},{6,7},{7,6},{8,9},{9,8},{10,11... | collective-permute-start | bytes 1769480 | tf_op jit(solution)/shard_map/ppermute | solution.py:53
  115.0 3.2 %collective-permute-start.25 = (bf16[192,1536]{1,0:T(8,128)(2,1)S(1)}, bf16[192,1536]{1,0:T(8,128)(2,1)S(1)}, u32[]{:S(2)}, u32[]{:S(2)}) collective-permute-start(bf16[192,1536]{1,0:T(8,128)(2,1)S(1)} %copy-done.5), channel_id=1, source_target_pairs={{0,1},{1,0},{2,3},{3,2},{4,5},{5,4},{6,7},{7,6},{8,9},{9,8},{10,11... | collective-permute-start | bytes 1769480 | tf_op jit(solution)/shard_map/ppermute | solution.py:53
  115.1 3.9 %collective-permute-start.26 = (bf16[768,384]{1,0:T(8,128)(2,1)S(1)}, bf16[768,384]{1,0:T(8,128)(2,1)S(1)}, u32[]{:S(2)}, u32[]{:S(2)}) collective-permute-start(bf16[768,384]{1,0:T(8,128)(2,1)S(1)} %collective-permute-done.20.x2), channel_id=1, source_target_pairs={{0,1},{1,0},{2,3},{3,2},{4,5},{5,4},{6,7},{7,6},{8,9},{9,8},{10,11... | collective-permute-start | bytes 1769480 | tf_op jit(solution)/shard_map/ppermute | solution.py:53

commit v7 on v6

--- a/solution.py
+++ b/solution.py
@@ -133,7 +133,7 @@
         out_specs=VMEM,
         scratch_shapes=[pltpu.SemaphoreType.DMA],
         compiler_params=params(),
-        cost_estimate=cost(0, 16 * rows * depth),
+        cost_estimate=cost(0, 16 * rows),
         name="sort_tokens",
     )(*ts)
 
@@ -186,7 +186,7 @@
         in_specs=[VMEM] * (2 + len(pieces)),
         out_specs=VMEM,
         compiler_params=params(),
-        cost_estimate=cost(6 * rows * depth * width, 6 * depth * (rows + width)),
+        cost_estimate=cost(6 * rows * depth, 6 * (rows + width)),
         name="up_part",
     )(t, own, *pieces)
 

time: 130 us -> 130 us (level)
  no operation moved by 1% of the time
where the time goes in v7:
time: 130 us
  waiting for transfers between devices  68.1 us (52%)
  starting transfers between devices  29.1 us (22%)
  Pallas kernels  19.8 us (15%)
  local copies, waits for them, and re-layouts  10.8 us (8%)
    ppermute x6, waiting for transfers between devices, z_step(): lax.ppermute(x, ('dp', 'col'), flat(sizes, lambda i, c: (i // n * n + (i...  31.2 us
    ppermute x12, waiting for transfers between devices, col_swap(): return lax.ppermute(x, 'col', [(i, i ^ m) for i in range(n)])  18.5 us
    ppermute x6, starting transfers between devices, z_step(): lax.ppermute(x, ('dp', 'col'), flat(sizes, lambda i, c: (i // n * n + (i...  12 us
    ppermute x8, waiting for transfers between devices, y_step(): lax.ppermute(x, ('row', 'col'), flat(sizes, lambda r, c: ((r + 1 - 2 * ((...  10.2 us
    ppermute x8, starting transfers between devices, y_step(): lax.ppermute(x, ('row', 'col'), flat(sizes, lambda r, c: ((r + 1 - 2 * ((...  9.55 us
    pallas_call x1, Pallas kernels, up_part(): pl.pallas_call(up_part_kernel, out_shape=jax.ShapeDtypeStruct((rows, widt...  7.43 us
    unnamed x23, local copies, waits for them, and re-layouts  5.54 us
    ppermute x1, waiting for transfers between devices, opposite(): return lax.ppermute(x, 'row', [(i, (i + 2) % n) for i in range(n)])  4.42 us
  transfers between devices with their start and end apart: 28, of which 15 were waited for; matrix products, arithmetic and copies ran while one was open for 7% of the time, Pallas kernels for 14%

profile of v7, /device:TPU:4, one launch (start us, length us, event | category | flops | bytes accessed | tf_op | source)
XLA Modules:
  0.0 129.9 jit_solution(14120934215472690713)
XLA Ops:
  0.6 0.1 collective-permute-start.3
  0.7 1.7 %copy-done = bf16[1536,768]{1,0:T(8,128)(2,1)S(1)} copy-done((bf16[1536,768]{1,0:T(8,128)(2,1)S(1)}, bf16[1536,768]{1,0:T(8,128)(2,1)}, u32[]{:S(2)}) %copy-start) | copy-done | bytes 2359320
  2.5 1.7 %collective-permute-start = (bf16[384,384]{1,0:T(8,128)(2,1)S(1)}, bf16[384,384]{1,0:T(8,128)(2,1)S(1)}, u32[]{:S(2)}, u32[]{:S(2)}) collective-permute-start(bf16[384,384]{1,0:T(8,128)(2,1)S(1)} %cut.1), channel_id=1, source_target_pairs={{0,4},{1,13},{2,6},{3,15},{4,8},{5,1},{6,10},{7,3},{8,12},{9,5},{1... | collective-permute-start | bytes 884744 | tf_op jit(solution)/shard_map/ppermute | solution.py:30
  4.1 2.9 %collective-permute-start.1 = (bf16[384,384]{1,0:T(8,128)(2,1)S(1)}, bf16[384,384]{1,0:T(8,128)(2,1)S(1)}, u32[]{:S(2)}, u32[]{:S(2)}) collective-permute-start(bf16[384,384]{1,0:T(8,128)(2,1)S(1)} %cut.1), channel_id=1, source_target_pairs={{0,8},{4,12},{8,0},{12,4},{1,9},{5,13},{9,1},{13,5},{2,10},{6,14},... | collective-permute-start | bytes 884744 | tf_op jit(solution)/shard_map/ppermute | solution.py:48
  7.0 1.3 %collective-permute-start.2 = (bf16[384,384]{1,0:T(8,128)(2,1)S(1)}, bf16[384,384]{1,0:T(8,128)(2,1)S(1)}, u32[]{:S(2)}, u32[]{:S(2)}) collective-permute-start(bf16[384,384]{1,0:T(8,128)(2,1)S(1)} %cut.1), channel_id=1, source_target_pairs={{0,12},{1,5},{2,14},{3,7},{4,0},{5,9},{6,2},{7,11},{8,4},{9,13},{1... | collective-permute-start | bytes 884744 | tf_op jit(solution)/shard_map/ppermute | solution.py:30
  8.4 0.5 collective-permute-start.8
  8.9 1.1 slice.3
  10.0 2.4 %copy.5 = bf16[1536,768]{0,1:T(8,128)(2,1)} copy(bf16[1536,768]{1,0:T(8,128)(2,1)S(1)} %copy-done.1) | data formatting | bytes 4718592 | tf_op args[1]
  12.4 3.0 %fusion = (bf16[192,1536]{1,0:T(8,128)(2,1)}, bf16[192,1536]{1,0:T(8,128)(2,1)}, bf16[192,1536]{1,0:T(8,128)(2,1)}, bf16[192,1536]{1,0:T(8,128)(2,1)}) fusion(bf16[768,1536]{1,0:T(8,128)(2,1)} %bitcast.4), kind=kLoop, calls=%fused_computation.2 | loop fusion | bytes 4718592 | tf_op jit(solution)/shard_map/split | solution.py:310
  15.5 4.4 %collective-permute-done.1 = bf16[384,384]{1,0:T(8,128)(2,1)S(1)} collective-permute-done((bf16[384,384]{1,0:T(8,128)(2,1)S(1)}, bf16[384,384]{1,0:T(8,128)(2,1)S(1)}, u32[]{:S(2)}, u32[]{:S(2)}) %collective-permute-start.1) | collective-permute-done | bytes 294944 | tf_op jit(solution)/shard_map/ppermute | solution.py:48
  20.0 3.2 %collective-permute-start.7 = (bf16[1536,384]{1,0:T(8,128)(2,1)}, bf16[1536,384]{1,0:T(8,128)(2,1)}, u32[]{:S(2)}, u32[]{:S(2)}) collective-permute-start(bf16[1536,384]{1,0:T(8,128)(2,1)} %slice.3), channel_id=1, source_target_pairs={{0,12},{1,5},{2,14},{3,7},{4,0},{5,9},{6,2},{7,11},{8,4},{9,13},{1... | collective-permute-start | bytes 3538952 | tf_op jit(solution)/shard_map/ppermute | solution.py:30
  23.2 1.2 pad_maximum_fusion.p0
  24.4 2.0 %collective-permute-start.4 = (bf16[3,384,384]{2,1,0:T(8,128)(2,1)S(1)}, bf16[3,384,384]{2,1,0:T(8,128)(2,1)}, u32[]{:S(2)}, u32[]{:S(2)}) collective-permute-start(bf16[3,384,384]{2,1,0:T(8,128)(2,1)S(1)} %pad_maximum_fusion.p0), channel_id=1, source_target_pairs={{0,16},{1,113},{2,18},{3,115},{16,32},{17,1},{18,34},{19,3},{32,48... | collective-permute-start | bytes 2654216 | tf_op jit(solution)/shard_map/ppermute | solution.py:41
  26.4 4.0 %collective-permute-start.5 = (bf16[3,384,384]{2,1,0:T(8,128)(2,1)S(1)}, bf16[3,384,384]{2,1,0:T(8,128)(2,1)}, u32[]{:S(2)}, u32[]{:S(2)}) collective-permute-start(bf16[3,384,384]{2,1,0:T(8,128)(2,1)S(1)} %pad_maximum_fusion.p0), channel_id=1, source_target_pairs={{0,112},{1,17},{2,114},{3,19},{16,0},{17,33},{18,2},{19,35},{32,16... | collective-permute-start | bytes 2654216 | tf_op jit(solution)/shard_map/ppermute | solution.py:41
  30.4 1.1 constant_dynamic-slice_fusion
  31.5 13.4 %collective-permute-done.8.t2 = bf16[512,1536]{1,0:T(8,128)(2,1)} collective-permute-done((bf16[512,1536]{1,0:T(8,128)(2,1)}, bf16[512,1536]{1,0:T(8,128)(2,1)}, u32[]{:S(2)}, u32[]{:S(2)}) %collective-permute-start.8) | collective-permute-done | bytes 1572896 | tf_op jit(solution)/shard_map/ppermute | solution.py:53
  44.9 5.6 %collective-permute-done.4.p1 = bf16[3,384,384]{2,1,0:T(8,128)(2,1)} collective-permute-done((bf16[3,384,384]{2,1,0:T(8,128)(2,1)S(1)}, bf16[3,384,384]{2,1,0:T(8,128)(2,1)}, u32[]{:S(2)}, u32[]{:S(2)}) %collective-permute-start.4) | collective-permute-done | bytes 884768 | tf_op jit(solution)/shard_map/ppermute | solution.py:41
  50.5 0.3 collective-permute-start.9
  50.8 1.3 %collective-permute-start.10 = (bf16[3,384,384]{2,1,0:T(8,128)(2,1)}, bf16[3,384,384]{2,1,0:T(8,128)(2,1)S(1)}, u32[]{:S(2)}, u32[]{:S(2)}) collective-permute-start(bf16[3,384,384]{2,1,0:T(8,128)(2,1)} %collective-permute-done.4.p1), channel_id=1, source_target_pairs={{0,16},{1,113},{2,18},{3,115},{16,32},{17,1},{18,34},{19,3},{32,48... | collective-permute-start | bytes 2654216 | tf_op jit(solution)/shard_map/ppermute | solution.py:41
  52.1 0.5 collective-permute-start.12
  52.6 1.6 %collective-permute-done.9.t3 = bf16[512,1536]{1,0:T(8,128)(2,1)S(1)} collective-permute-done((bf16[512,1536]{1,0:T(8,128)(2,1)}, bf16[512,1536]{1,0:T(8,128)(2,1)S(1)}, u32[]{:S(2)}, u32[]{:S(2)}) %collective-permute-start.9) | collective-permute-done | bytes 1572896 | tf_op jit(solution)/shard_map/ppermute | solution.py:53
  54.2 1.4 %copy-done.3 = bf16[512,1536]{1,0:T(8,128)(2,1)S(1)} copy-done((bf16[512,1536]{1,0:T(8,128)(2,1)S(1)}, bf16[512,1536]{1,0:T(8,128)(2,1)}, u32[]{:S(2)}) %copy-start.3) | copy-done | bytes 1572888
  55.6 2.0 %sort_tokens.1.t = bf16[4,512,1536]{2,1,0:T(8,128)(2,1)S(1)} custom-call(bf16[512,1536]{1,0:T(8,128)(2,1)S(1)} %copy-done.3, bf16[512,1536]{1,0:T(8,128)(2,1)} %collective-permute-done.3.t1, bf16[512,1536]{1,0:T(8,128)(2,1)} %collective-permute-done.8.t2, bf16[512,1536]{1,0:T(8,128)(2,1)S(1)} %collective-permute-done.9.t3), custom_call_target="tpu_custom_call" | custom-call | bytes 8192 | tf_op jit(solution)/shard_map/sort_tokens/pallas_call | solution.py:129
  57.6 7.4 %up_part.1.so_far = f32[512,768]{1,0:T(8,128)S(1)} custom-call(bf16[4,512,1536]{2,1,0:T(8,128)(2,1)S(1)} %sort_tokens.1.t, bf16[1536,768]{1,0:T(8,128)(2,1)S(1)} %copy-done.1, bf16[1536,384]{1,0:T(8,128)(2,1)} %collective-permute-done.6.w1, bf16[1536,384]{1,0:T(8,128)(2,1)} %collective-permute-done.7.w3, bf16[3,384,384]{2,1,0:T(8,128)(2,1)S(1)} %pad_maximum_fusion.p0, ...), custom_call_target="tpu_custom_call" | custom-call | flops 4718592 | bytes 7680 | tf_op jit(solution)/shard_map/up_part/pallas_call | solution.py:183
  65.1 2.2 %collective-permute-done.10.p2 = bf16[3,384,384]{2,1,0:T(8,128)(2,1)S(1)} collective-permute-done((bf16[3,384,384]{2,1,0:T(8,128)(2,1)}, bf16[3,384,384]{2,1,0:T(8,128)(2,1)S(1)}, u32[]{:S(2)}, u32[]{:S(2)}) %collective-permute-start.10) | collective-permute-done | bytes 884768 | tf_op jit(solution)/shard_map/ppermute | solution.py:41
  67.2 1.1 collective-permute-done.11.w2
  68.4 2.7 %up_rest.1 = (bf16[512,768]{1,0:T(8,128)(2,1)}, bf16[512,768]{1,0:T(8,128)(2,1)S(1)}) custom-call(bf16[4,512,1536]{2,1,0:T(8,128)(2,1)S(1)} %sort_tokens.1.t, f32[512,768]{1,0:T(8,128)S(1)} %up_part.1.so_far, bf16[1536,384]{1,0:T(8,128)(2,1)S(1)} %collective-permute-done.11.w2, bf16[3,384,384]{2,1,0:T(8,128)(2,1)S(1)} %collective-permute-done.10.p2, ...), custom_call_target="tpu_custom_call" | custom-call | flops 1207959552 | bytes 3932160 | tf_op jit(solution)/shard_map/up_rest/pallas_call | solution.py:197
  71.1 1.2 collective-permute-start.13
  72.3 0.7 collective-permute-start.14
  73.0 3.9 %collective-permute-start.15 = (bf16[768,384]{1,0:T(8,128)(2,1)S(1)}, bf16[768,384]{1,0:T(8,128)(2,1)S(1)}, u32[]{:S(2)}, u32[]{:S(2)}) collective-permute-start(bf16[768,384]{1,0:T(8,128)(2,1)S(1)} %collective-permute-done.12.x0), channel_id=1, source_target_pairs={{0,112},{1,17},{2,114},{3,19},{16,0},{17,33},{18,2},{19,35},{32,16... | collective-permute-start | bytes 1769480 | tf_op jit(solution)/shard_map/ppermute | solution.py:41
  77.0 0.5 collective-permute-start.17
  77.5 13.0 %collective-permute-done.14.x1 = bf16[768,384]{1,0:T(8,128)(2,1)S(1)} collective-permute-done((bf16[768,384]{1,0:T(8,128)(2,1)S(1)}, bf16[768,384]{1,0:T(8,128)(2,1)S(1)}, u32[]{:S(2)}, u32[]{:S(2)}) %collective-permute-start.14) | collective-permute-done | bytes 589856 | tf_op jit(solution)/shard_map/ppermute | solution.py:41
  90.4 3.7 %collective-permute-done.13.rest_0_ = bf16[512,768]{1,0:T(8,128)(2,1)S(1)} collective-permute-done((bf16[512,768]{1,0:T(8,128)(2,1)S(1)}, bf16[512,768]{1,0:T(8,128)(2,1)S(1)}, u32[]{:S(2)}, u32[]{:S(2)}) %collective-permute-start.13) | collective-permute-done | bytes 786464 | tf_op jit(solution)/shard_map/ppermute | solution.py:66
  94.2 3.2 %collective-permute-start.19 = (bf16[512,768]{1,0:T(8,128)(2,1)S(1)}, bf16[512,768]{1,0:T(8,128)(2,1)S(1)}, u32[]{:S(2)}, u32[]{:S(2)}) collective-permute-start(bf16[512,768]{1,0:T(8,128)(2,1)S(1)} %collective-permute-done.13.rest_0_), channel_id=1, source_target_pairs={{0,12},{1,5},{2,14},{3,7},{4,0},{5,9},{6,2},{7,11},{8,4},{9,13},{1... | collective-permute-start | bytes 2359304 | tf_op jit(solution)/shard_map/ppermute | solution.py:30
  97.4 0.5 collective-permute-start.22
  97.9 10.6 %collective-permute-done.20.x2 = bf16[768,384]{1,0:T(8,128)(2,1)S(1)} collective-permute-done((bf16[768,384]{1,0:T(8,128)(2,1)S(1)}, bf16[768,384]{1,0:T(8,128)(2,1)S(1)}, u32[]{:S(2)}, u32[]{:S(2)}) %collective-permute-start.20) | collective-permute-done | bytes 589856 | tf_op jit(solution)/shard_map/ppermute | solution.py:41
  108.5 5.8 %collective-permute-done.18.rest_1_ = bf16[512,768]{1,0:T(8,128)(2,1)S(1)} collective-permute-done((bf16[512,768]{1,0:T(8,128)(2,1)S(1)}, bf16[512,768]{1,0:T(8,128)(2,1)S(1)}, u32[]{:S(2)}, u32[]{:S(2)}) %collective-permute-start.18) | collective-permute-done | bytes 786464 | tf_op jit(solution)/shard_map/ppermute | solution.py:30
  114.5 0.5 collective-permute-start.24
  115.0 0.1 collective-permute-start.25
  115.1 0.4 collective-permute-start.26
  115.5 1.0 collective-permute-done.23.c1
  116.5 0.8 collective-permute-done.24.c2
  117.3 0.8 collective-permute-done.25.c3
  118.1 0.8 collective-permute-done.26.y2
  119.0 1.2 sort_w.1.w
  120.2 4.2 %down.1.so_far = f32[512,1536]{1,0:T(8,128)S(1)} custom-call(bf16[4,768,1536]{2,1,0:T(8,128)(2,1)S(1)} %sort_w.1.w, bf16[512,768]{1,0:T(8,128)(2,1)S(1)} %collective-permute-done.13.rest_0_, bf16[512,768]{1,0:T(8,128)(2,1)S(1)} %collective-permute-done.18.rest_1_, bf16[512,768]{1,0:T(8,128)(2,1)S(1)} %collective-permute-done.19.rest_2_), custom_call_target="tpu_custom_call" | custom-call | flops 1572864 | bytes 16384 | tf_op jit(solution)/shard_map/down/pallas_call | solution.py:257
  124.3 3.2 %collective-permute-done.27.g = bf16[512,768]{1,0:T(8,128)(2,1)S(1)} collective-permute-done((bf16[512,768]{1,0:T(8,128)(2,1)S(1)}, bf16[512,768]{1,0:T(8,128)(2,1)S(1)}, u32[]{:S(2)}, u32[]{:S(2)}) %collective-permute-start.27) | collective-permute-done | bytes 786464 | tf_op jit(solution)/shard_map/ppermute | solution.py:30
  127.6 2.2 %down_last.1 = bf16[512,1536]{1,0:T(8,128)(2,1)} custom-call(bf16[4,768,1536]{2,1,0:T(8,128)(2,1)S(1)} %sort_w.1.w, bf16[512,768]{1,0:T(8,128)(2,1)S(1)} %collective-permute-done.27.g, f32[512,1536]{1,0:T(8,128)S(1)} %down.1.so_far), custom_call_target="tpu_custom_call" | custom-call | flops 1207959552 | bytes 4718592 | tf_op jit(solution)/shard_map/down_last/pallas_call | solution.py:283
  (42 shorter events, 0.3 us)
Async XLA Ops:
  0.6 19.3 %collective-permute-start.3 = (bf16[512,1536]{1,0:T(8,128)(2,1)}, bf16[512,1536]{1,0:T(8,128)(2,1)}, u32[]{:S(2)}, u32[]{:S(2)}) collective-permute-start(bf16[512,1536]{1,0:T(8,128)(2,1)} %t0.1), channel_id=1, source_target_pairs={{0,1},{1,0},{2,3},{3,2},{4,5},{5,4},{6,7},{7,6},{8,9},{9,8},{10,11... | collective-permute-start | bytes 4718600 | tf_op jit(solution)/shard_map/ppermute | solution.py:53
  0.7 1.7 %copy-start = (bf16[1536,768]{1,0:T(8,128)(2,1)S(1)}, bf16[1536,768]{1,0:T(8,128)(2,1)}, u32[]{:S(2)}) copy-start(bf16[1536,768]{1,0:T(8,128)(2,1)} %own.1) | copy-start | bytes 7077892
  2.4 6.5 %copy-start.1 = (bf16[1536,768]{1,0:T(8,128)(2,1)S(1)}, bf16[1536,768]{1,0:T(8,128)(2,1)}, u32[]{:S(2)}) copy-start(bf16[1536,768]{1,0:T(8,128)(2,1)} %own.1) | copy-start | bytes 7077892
  2.5 13.0 %collective-permute-start = (bf16[384,384]{1,0:T(8,128)(2,1)S(1)}, bf16[384,384]{1,0:T(8,128)(2,1)S(1)}, u32[]{:S(2)}, u32[]{:S(2)}) collective-permute-start(bf16[384,384]{1,0:T(8,128)(2,1)S(1)} %cut.1), channel_id=1, source_target_pairs={{0,4},{1,13},{2,6},{3,15},{4,8},{5,1},{6,10},{7,3},{8,12},{9,5},{1... | collective-permute-start | bytes 884744 | tf_op jit(solution)/shard_map/ppermute | solution.py:30
  4.1 15.8 %collective-permute-start.1 = (bf16[384,384]{1,0:T(8,128)(2,1)S(1)}, bf16[384,384]{1,0:T(8,128)(2,1)S(1)}, u32[]{:S(2)}, u32[]{:S(2)}) collective-permute-start(bf16[384,384]{1,0:T(8,128)(2,1)S(1)} %cut.1), channel_id=1, source_target_pairs={{0,8},{4,12},{8,0},{12,4},{1,9},{5,13},{9,1},{13,5},{2,10},{6,14},... | collective-permute-start | bytes 884744 | tf_op jit(solution)/shard_map/ppermute | solution.py:48
  7.0 12.9 %collective-permute-start.2 = (bf16[384,384]{1,0:T(8,128)(2,1)S(1)}, bf16[384,384]{1,0:T(8,128)(2,1)S(1)}, u32[]{:S(2)}, u32[]{:S(2)}) collective-permute-start(bf16[384,384]{1,0:T(8,128)(2,1)S(1)} %cut.1), channel_id=1, source_target_pairs={{0,12},{1,5},{2,14},{3,7},{4,0},{5,9},{6,2},{7,11},{8,4},{9,13},{1... | collective-permute-start | bytes 884744 | tf_op jit(solution)/shard_map/ppermute | solution.py:30
  8.4 36.6 %collective-permute-start.8 = (bf16[512,1536]{1,0:T(8,128)(2,1)}, bf16[512,1536]{1,0:T(8,128)(2,1)}, u32[]{:S(2)}, u32[]{:S(2)}) collective-permute-start(bf16[512,1536]{1,0:T(8,128)(2,1)} %t0.1), channel_id=1, source_target_pairs={{0,2},{1,3},{2,0},{3,1},{4,6},{5,7},{6,4},{7,5},{8,10},{9,11},{10,... | collective-permute-start | bytes 4718600 | tf_op jit(solution)/shard_map/ppermute | solution.py:53
  19.9 3.3 %copy-start.9 = (bf16[384,384]{1,0:T(8,128)(2,1)}, bf16[384,384]{1,0:T(8,128)(2,1)S(1)}, u32[]{:S(2)}) copy-start(bf16[384,384]{1,0:T(8,128)(2,1)S(1)} %collective-permute-done.1) | copy-start | bytes 884740
  19.9 3.3 %copy-start.10 = (bf16[384,384]{1,0:T(8,128)(2,1)}, bf16[384,384]{1,0:T(8,128)(2,1)S(1)}, u32[]{:S(2)}) copy-start(bf16[384,384]{1,0:T(8,128)(2,1)S(1)} %collective-permute-done.2) | copy-start | bytes 884740
  19.9 30.6 %collective-permute-start.6 = (bf16[1536,384]{1,0:T(8,128)(2,1)}, bf16[1536,384]{1,0:T(8,128)(2,1)}, u32[]{:S(2)}, u32[]{:S(2)}) collective-permute-start(bf16[1536,384]{1,0:T(8,128)(2,1)} %slice.3), channel_id=1, source_target_pairs={{0,4},{1,13},{2,6},{3,15},{4,8},{5,1},{6,10},{7,3},{8,12},{9,5},{1... | collective-permute-start | bytes 3538952 | tf_op jit(solution)/shard_map/ppermute | solution.py:30
  20.0 30.5 %collective-permute-start.7 = (bf16[1536,384]{1,0:T(8,128)(2,1)}, bf16[1536,384]{1,0:T(8,128)(2,1)}, u32[]{:S(2)}, u32[]{:S(2)}) collective-permute-start(bf16[1536,384]{1,0:T(8,128)(2,1)} %slice.3), channel_id=1, source_target_pairs={{0,12},{1,5},{2,14},{3,7},{4,0},{5,9},{6,2},{7,11},{8,4},{9,13},{1... | collective-permute-start | bytes 3538952 | tf_op jit(solution)/shard_map/ppermute | solution.py:30
  24.4 26.1 %collective-permute-start.4 = (bf16[3,384,384]{2,1,0:T(8,128)(2,1)S(1)}, bf16[3,384,384]{2,1,0:T(8,128)(2,1)}, u32[]{:S(2)}, u32[]{:S(2)}) collective-permute-start(bf16[3,384,384]{2,1,0:T(8,128)(2,1)S(1)} %pad_maximum_fusion.p0), channel_id=1, source_target_pairs={{0,16},{1,113},{2,18},{3,115},{16,32},{17,1},{18,34},{19,3},{32,48... | collective-permute-start | bytes 2654216 | tf_op jit(solution)/shard_map/ppermute | solution.py:41
  26.4 24.1 %collective-permute-start.5 = (bf16[3,384,384]{2,1,0:T(8,128)(2,1)S(1)}, bf16[3,384,384]{2,1,0:T(8,128)(2,1)}, u32[]{:S(2)}, u32[]{:S(2)}) collective-permute-start(bf16[3,384,384]{2,1,0:T(8,128)(2,1)S(1)} %pad_maximum_fusion.p0), channel_id=1, source_target_pairs={{0,112},{1,17},{2,114},{3,19},{16,0},{17,33},{18,2},{19,35},{32,16... | collective-permute-start | bytes 2654216 | tf_op jit(solution)/shard_map/ppermute | solution.py:41
  50.5 3.7 %collective-permute-start.9 = (bf16[512,1536]{1,0:T(8,128)(2,1)}, bf16[512,1536]{1,0:T(8,128)(2,1)S(1)}, u32[]{:S(2)}, u32[]{:S(2)}) collective-permute-start(bf16[512,1536]{1,0:T(8,128)(2,1)} %collective-permute-done.8.t2), channel_id=1, source_target_pairs={{0,1},{1,0},{2,3},{3,2},{4,5},{5,4},{6,7},{7,6},{8,9},{9,8},{10,11... | collective-permute-start | bytes 4718600 | tf_op jit(solution)/shard_map/ppermute | solution.py:53
  50.8 17.6 %collective-permute-start.11 = (bf16[1536,384]{1,0:T(8,128)(2,1)}, bf16[1536,384]{1,0:T(8,128)(2,1)S(1)}, u32[]{:S(2)}, u32[]{:S(2)}) collective-permute-start(bf16[1536,384]{1,0:T(8,128)(2,1)} %collective-permute-done.6.w1), channel_id=1, source_target_pairs={{0,4},{1,13},{2,6},{3,15},{4,8},{5,1},{6,10},{7,3},{8,12},{9,5},{1... | collective-permute-start | bytes 3538952 | tf_op jit(solution)/shard_map/ppermute | solution.py:30
  50.8 16.5 %collective-permute-start.10 = (bf16[3,384,384]{2,1,0:T(8,128)(2,1)}, bf16[3,384,384]{2,1,0:T(8,128)(2,1)S(1)}, u32[]{:S(2)}, u32[]{:S(2)}) collective-permute-start(bf16[3,384,384]{2,1,0:T(8,128)(2,1)} %collective-permute-done.4.p1), channel_id=1, source_target_pairs={{0,16},{1,113},{2,18},{3,115},{16,32},{17,1},{18,34},{19,3},{32,48... | collective-permute-start | bytes 2654216 | tf_op jit(solution)/shard_map/ppermute | solution.py:41
  52.1 19.1 %collective-permute-start.12 = (bf16[768,384]{1,0:T(8,128)(2,1)S(1)}, bf16[768,384]{1,0:T(8,128)(2,1)S(1)}, u32[]{:S(2)}, u32[]{:S(2)}) collective-permute-start(bf16[768,384]{1,0:T(8,128)(2,1)S(1)} %constant_dynamic-slice_fusion), channel_id=1, source_target_pairs={{0,2},{1,3},{2,0},{3,1},{4,6},{5,7},{6,4},{7,5},{8,10},{9,11},{10,... | collective-permute-start | bytes 1769480 | tf_op jit(solution)/shard_map/ppermute | solution.py:53
  54.2 1.4 %copy-start.3 = (bf16[512,1536]{1,0:T(8,128)(2,1)S(1)}, bf16[512,1536]{1,0:T(8,128)(2,1)}, u32[]{:S(2)}) copy-start(bf16[512,1536]{1,0:T(8,128)(2,1)} %t0.1) | copy-start | bytes 4718596
  57.6 10.8 %copy-start.4 = (bf16[512,768]{1,0:T(8,128)(2,1)S(1)}, bf16[512,768]{1,0:T(8,128)(2,1)}, u32[]{:S(2)}) copy-start(bf16[512,768]{1,0:T(8,128)(2,1)} %cot.1) | copy-start | bytes 2359300
  65.1 11.9 %copy-start.8 = (bf16[192,1536]{1,0:T(8,128)(2,1)S(1)}, bf16[192,1536]{1,0:T(8,128)(2,1)}, u32[]{:S(2)}) copy-start(bf16[192,1536]{1,0:T(8,128)(2,1)} %get-tuple-element.69) | copy-start | bytes 1769476
  65.1 49.3 %copy-start.7 = (bf16[192,1536]{1,0:T(8,128)(2,1)S(1)}, bf16[192,1536]{1,0:T(8,128)(2,1)}, u32[]{:S(2)}) copy-start(bf16[192,1536]{1,0:T(8,128)(2,1)} %get-tuple-element.77) | copy-start | bytes 1769476
  65.1 49.4 %copy-start.6 = (bf16[192,1536]{1,0:T(8,128)(2,1)S(1)}, bf16[192,1536]{1,0:T(8,128)(2,1)}, u32[]{:S(2)}) copy-start(bf16[192,1536]{1,0:T(8,128)(2,1)} %get-tuple-element.78) | copy-start | bytes 1769476
  65.1 49.9 %copy-start.5 = (bf16[192,1536]{1,0:T(8,128)(2,1)S(1)}, bf16[192,1536]{1,0:T(8,128)(2,1)}, u32[]{:S(2)}) copy-start(bf16[192,1536]{1,0:T(8,128)(2,1)} %get-tuple-element.79) | copy-start | bytes 1769476
  68.4 50.6 %copy-start.2 = (bf16[1536,768]{0,1:T(8,128)(2,1)S(1)}, bf16[1536,768]{0,1:T(8,128)(2,1)}, u32[]{:S(2)}) copy-start(bf16[1536,768]{0,1:T(8,128)(2,1)} %copy.5) | copy-start | bytes 7077892
  71.1 23.0 %collective-permute-start.13 = (bf16[512,768]{1,0:T(8,128)(2,1)S(1)}, bf16[512,768]{1,0:T(8,128)(2,1)S(1)}, u32[]{:S(2)}, u32[]{:S(2)}) collective-permute-start(bf16[512,768]{1,0:T(8,128)(2,1)S(1)} %get-tuple-element.67), channel_id=1, source_target_pairs={{0,12},{1,4},{2,0},{3,8},{4,1},{5,9},{6,5},{7,13},{8,10},{9,2},{10... | collective-permute-start | bytes 2359304 | tf_op jit(solution)/shard_map/ppermute | solution.py:66
  72.3 18.1 %collective-permute-start.14 = (bf16[768,384]{1,0:T(8,128)(2,1)S(1)}, bf16[768,384]{1,0:T(8,128)(2,1)S(1)}, u32[]{:S(2)}, u32[]{:S(2)}) collective-permute-start(bf16[768,384]{1,0:T(8,128)(2,1)S(1)} %collective-permute-done.12.x0), channel_id=1, source_target_pairs={{0,16},{1,113},{2,18},{3,115},{16,32},{17,1},{18,34},{19,3},{32,48... | collective-permute-start | bytes 1769480 | tf_op jit(solution)/shard_map/ppermute | solution.py:41
  73.0 17.4 %collective-permute-start.15 = (bf16[768,384]{1,0:T(8,128)(2,1)S(1)}, bf16[768,384]{1,0:T(8,128)(2,1)S(1)}, u32[]{:S(2)}, u32[]{:S(2)}) collective-permute-start(bf16[768,384]{1,0:T(8,128)(2,1)S(1)} %collective-permute-done.12.x0), channel_id=1, source_target_pairs={{0,112},{1,17},{2,114},{3,19},{16,0},{17,33},{18,2},{19,35},{32,16... | collective-permute-start | bytes 1769480 | tf_op jit(solution)/shard_map/ppermute | solution.py:41
  77.0 13.5 %collective-permute-start.16 = (bf16[768,384]{1,0:T(8,128)(2,1)S(1)}, bf16[768,384]{1,0:T(8,128)(2,1)S(1)}, u32[]{:S(2)}, u32[]{:S(2)}) collective-permute-start(bf16[768,384]{1,0:T(8,128)(2,1)S(1)} %collective-permute-done.12.x0), channel_id=1, source_target_pairs={{0,1},{1,0},{2,3},{3,2},{4,5},{5,4},{6,7},{7,6},{8,9},{9,8},{10,11... | collective-permute-start | bytes 1769480 | tf_op jit(solution)/shard_map/ppermute | solution.py:53
  77.0 13.5 %collective-permute-start.17 = (bf16[192,1536]{1,0:T(8,128)(2,1)S(1)}, bf16[192,1536]{1,0:T(8,128)(2,1)S(1)}, u32[]{:S(2)}, u32[]{:S(2)}) collective-permute-start(bf16[192,1536]{1,0:T(8,128)(2,1)S(1)} %copy-done.8), channel_id=1, source_target_pairs={{0,1},{1,0},{2,3},{3,2},{4,5},{5,4},{6,7},{7,6},{8,9},{9,8},{10,11... | collective-permute-start | bytes 1769480 | tf_op jit(solution)/shard_map/ppermute | solution.py:53
  94.2 20.2 %collective-permute-start.18 = (bf16[512,768]{1,0:T(8,128)(2,1)S(1)}, bf16[512,768]{1,0:T(8,128)(2,1)S(1)}, u32[]{:S(2)}, u32[]{:S(2)}) collective-permute-start(bf16[512,768]{1,0:T(8,128)(2,1)S(1)} %collective-permute-done.13.rest_0_), channel_id=1, source_target_pairs={{0,4},{1,13},{2,6},{3,15},{4,8},{5,1},{6,10},{7,3},{8,12},{9,5},{1... | collective-permute-start | bytes 2359304 | tf_op jit(solution)/shard_map/ppermute | solution.py:30
  94.2 20.2 %collective-permute-start.19 = (bf16[512,768]{1,0:T(8,128)(2,1)S(1)}, bf16[512,768]{1,0:T(8,128)(2,1)S(1)}, u32[]{:S(2)}, u32[]{:S(2)}) collective-permute-start(bf16[512,768]{1,0:T(8,128)(2,1)S(1)} %collective-permute-done.13.rest_0_), channel_id=1, source_target_pairs={{0,12},{1,5},{2,14},{3,7},{4,0},{5,9},{6,2},{7,11},{8,4},{9,13},{1... | collective-permute-start | bytes 2359304 | tf_op jit(solution)/shard_map/ppermute | solution.py:30
  97.4 11.1 %collective-permute-start.20 = (bf16[768,384]{1,0:T(8,128)(2,1)S(1)}, bf16[768,384]{1,0:T(8,128)(2,1)S(1)}, u32[]{:S(2)}, u32[]{:S(2)}) collective-permute-start(bf16[768,384]{1,0:T(8,128)(2,1)S(1)} %collective-permute-done.14.x1), channel_id=1, source_target_pairs={{0,16},{1,113},{2,18},{3,115},{16,32},{17,1},{18,34},{19,3},{32,48... | collective-permute-start | bytes 1769480 | tf_op jit(solution)/shard_map/ppermute | solution.py:41
  97.4 11.1 %collective-permute-start.21 = (bf16[768,384]{1,0:T(8,128)(2,1)S(1)}, bf16[768,384]{1,0:T(8,128)(2,1)S(1)}, u32[]{:S(2)}, u32[]{:S(2)}) collective-permute-start(bf16[768,384]{1,0:T(8,128)(2,1)S(1)} %collective-permute-done.14.x1), channel_id=1, source_target_pairs={{0,1},{1,0},{2,3},{3,2},{4,5},{5,4},{6,7},{7,6},{8,9},{9,8},{10,11... | collective-permute-start | bytes 1769480 | tf_op jit(solution)/shard_map/ppermute | solution.py:53
  97.4 11.1 %collective-permute-start.22 = (bf16[768,384]{1,0:T(8,128)(2,1)S(1)}, bf16[768,384]{1,0:T(8,128)(2,1)S(1)}, u32[]{:S(2)}, u32[]{:S(2)}) collective-permute-start(bf16[768,384]{1,0:T(8,128)(2,1)S(1)} %collective-permute-done.15.x3), channel_id=1, source_target_pairs={{0,1},{1,0},{2,3},{3,2},{4,5},{5,4},{6,7},{7,6},{8,9},{9,8},{10,11... | collective-permute-start | bytes 1769480 | tf_op jit(solution)/shard_map/ppermute | solution.py:53
  114.4 13.2 %collective-permute-start.27 = (bf16[512,768]{1,0:T(8,128)(2,1)S(1)}, bf16[512,768]{1,0:T(8,128)(2,1)S(1)}, u32[]{:S(2)}, u32[]{:S(2)}) collective-permute-start(bf16[512,768]{1,0:T(8,128)(2,1)S(1)} %collective-permute-done.18.rest_1_), channel_id=1, source_target_pairs={{0,4},{1,13},{2,6},{3,15},{4,8},{5,1},{6,10},{7,3},{8,12},{9,5},{1... | collective-permute-start | bytes 2359304 | tf_op jit(solution)/shard_map/ppermute | solution.py:30
  114.4 2.1 %collective-permute-start.23 = (bf16[192,1536]{1,0:T(8,128)(2,1)S(1)}, bf16[192,1536]{1,0:T(8,128)(2,1)S(1)}, u32[]{:S(2)}, u32[]{:S(2)}) collective-permute-start(bf16[192,1536]{1,0:T(8,128)(2,1)S(1)} %copy-done.7), channel_id=1, source_target_pairs={{0,1},{1,0},{2,3},{3,2},{4,5},{5,4},{6,7},{7,6},{8,9},{9,8},{10,11... | collective-permute-start | bytes 1769480 | tf_op jit(solution)/shard_map/ppermute | solution.py:53
  114.5 2.8 %collective-permute-start.24 = (bf16[192,1536]{1,0:T(8,128)(2,1)S(1)}, bf16[192,1536]{1,0:T(8,128)(2,1)S(1)}, u32[]{:S(2)}, u32[]{:S(2)}) collective-permute-start(bf16[192,1536]{1,0:T(8,128)(2,1)S(1)} %copy-done.6), channel_id=1, source_target_pairs={{0,1},{1,0},{2,3},{3,2},{4,5},{5,4},{6,7},{7,6},{8,9},{9,8},{10,11... | collective-permute-start | bytes 1769480 | tf_op jit(solution)/shard_map/ppermute | solution.py:53
  115.0 3.2 %collective-permute-start.25 = (bf16[192,1536]{1,0:T(8,128)(2,1)S(1)}, bf16[192,1536]{1,0:T(8,128)(2,1)S(1)}, u32[]{:S(2)}, u32[]{:S(2)}) collective-permute-start(bf16[192,1536]{1,0:T(8,128)(2,1)S(1)} %copy-done.5), channel_id=1, source_target_pairs={{0,1},{1,0},{2,3},{3,2},{4,5},{5,4},{6,7},{7,6},{8,9},{9,8},{10,11... | collective-permute-start | bytes 1769480 | tf_op jit(solution)/shard_map/ppermute | solution.py:53
  115.1 3.9 %collective-permute-start.26 = (bf16[768,384]{1,0:T(8,128)(2,1)S(1)}, bf16[768,384]{1,0:T(8,128)(2,1)S(1)}, u32[]{:S(2)}, u32[]{:S(2)}) collective-permute-start(bf16[768,384]{1,0:T(8,128)(2,1)S(1)} %collective-permute-done.20.x2), channel_id=1, source_target_pairs={{0,1},{1,0},{2,3},{3,2},{4,5},{5,4},{6,7},{7,6},{8,9},{9,8},{10,11... | collective-permute-start | bytes 1769480 | tf_op jit(solution)/shard_map/ppermute | solution.py:53
